TPU v7x, 128 devices: a whole 4x4x4 slice. The times are simulated.
128 devices in a mesh: gx: 8 (over y, x_lo), gy: 16 (over x_hi, z, core).
Axes of the slice: x: 4 (x_hi: 2, x_lo: 2; x = x_hi * 2 + x_lo), y: 4, z: 4, core: 2. Of those that a mesh axis runs over, the one named last changes fastest.
Arguments:
- inputs: bfloat16 [24, 197, 1024], P('gx', None, 'gy'), may hold values from -28 to 28
- cotangent: bfloat16 [24, 197, 1024], P('gx', None, 'gy'), may hold values from -6 to 6
- group_images: int32 [8], replicated, may hold values from 1 to 3, 16 in all
- ln1_gain: float32 [2, 1024], P(None, 'gy'), may hold values from 0.25 to 1.75
- ln1_bias: float32 [2, 1024], P(None, 'gy'), may hold values from -4 to 4
- w_qkv: bfloat16 [2, 1024, 16, 192], P(None, 'gx', 'gy'), may hold values from -0.1875 to 0.1875
- b_qv: float32 [2, 16, 128], P(None, 'gy'), may hold values from -4 to 4
- w_out: bfloat16 [2, 1024, 1024], P(None, 'gy', 'gx'), may hold values from -1.5 to 1.5
- b_out: float32 [2, 1024], P(None, 'gy'), may hold values from -4 to 4
- ln2_gain: float32 [2, 1024], P(None, 'gy'), may hold values from 0.25 to 1.75
- ln2_bias: float32 [2, 1024], P(None, 'gy'), may hold values from -4 to 4
- w_up: bfloat16 [2, 1024, 4096], P(None, 'gx', 'gy'), may hold values from -0.1875 to 0.1875
- b_up: float32 [2, 4096], P(None, 'gy'), may hold values from -4 to 4
- w_down: bfloat16 [2, 4096, 1024], P(None, 'gy', 'gx'), may hold values from -0.09375 to 0.09375
- b_down: float32 [2, 1024], P(None, 'gy'), may hold values from -4 to 4
Outputs:
- out: float32 [24, 197, 1024], P('gx', None, 'gy')
- grad_inputs: float32 [24, 197, 1024], P('gx', None, 'gy')
- grad_ln1_gain: float32 [2, 1024], P(None, 'gy')
- grad_ln1_bias: float32 [2, 1024], P(None, 'gy')
- grad_w_qkv: float32 [2, 1024, 16, 192], P(None, 'gx', 'gy')
- grad_b_qv: float32 [2, 16, 128], P(None, 'gy')
- grad_w_out: float32 [2, 1024, 1024], P(None, 'gy', 'gx')
- grad_b_out: float32 [2, 1024], P(None, 'gy')
- grad_ln2_gain: float32 [2, 1024], P(None, 'gy')
- grad_ln2_bias: float32 [2, 1024], P(None, 'gy')
- grad_w_up: float32 [2, 1024, 4096], P(None, 'gx', 'gy')
- grad_b_up: float32 [2, 4096], P(None, 'gy')
- grad_w_down: float32 [2, 4096, 1024], P(None, 'gy', 'gx')
- grad_b_down: float32 [2, 1024], P(None, 'gy')
Inputs may be any that keep to these rules, and one draw needn't show every extreme that they name: x-group g holds live images in its first group_images[g] of its 3 slots; the rest are padding; some group is full.
All inputs are finite; a program needn't handle non-finite values.
Results may differ from a plain program's by a relative error of at most 0.023.
Values may be sent and summed in bfloat16 or wider, within the bound.
No kernel may reach another device: no remote copies, remote signals or barrier semaphores. Data moves between devices by JAX's collectives and lax.ppermute only.
A program may use at most 64 MiB of HBM per device.

v0:
```python
import functools

import jax
import jax.numpy as jnp
from jax import lax
from jax.experimental import pallas as pl
from jax.experimental.pallas import tpu as pltpu
from jax.sharding import Mesh, PartitionSpec as P

EPS = 1e-06
BF = jnp.bfloat16
F32 = jnp.float32
DP = ("y", "xl", "xh")
SWAP = [(0, 1), (1, 0)]
PAIR_A = [(0, 1), (1, 0), (2, 3), (3, 2)]
PAIR_B = [(0, 3), (3, 0), (1, 2), (2, 1)]


def dot(a, b, ca, cb):
    return lax.dot_general(a, b, (((ca,), (cb,)), ((), ())), preferred_element_type=F32)


def core_swap(block):
    return lax.ppermute(block, "c", SWAP)


def ring_blocks(block):
    return [block] + [
        lax.ppermute(block, "z", [(i, (i + step) % 4) for i in range(4)]) for step in (1, 3, 2)
    ]


def total(mine, theirs, work=None, late=None):
    mine = (mine + core_swap(theirs).astype(F32)).astype(BF)
    if work is not None:
        mine, given = lax.optimization_barrier((mine, work[1]))
    cut = mine.shape[1] // 2
    left, right = mine[:, :cut], mine[:, cut:]
    got_left = lax.ppermute(left, "z", PAIR_A)
    got_right = lax.ppermute(right, "z", PAIR_B)
    done = work[0](given) if work is not None else None
    left = (left.astype(F32) + got_left.astype(F32)).astype(BF)
    right = (right.astype(F32) + got_right.astype(F32)).astype(BF)
    left, right, late, done = lax.optimization_barrier((left, right, late, done))
    got_left = lax.ppermute(left, "z", PAIR_B)
    got_right = lax.ppermute(right, "z", PAIR_A)
    return (left, got_left, right, got_right), done, late


HALF = 112
ROWS = 2 * HALF
WIDTH = 1024


def run(kernel, outs, args, flops, scratch=(), smem=0, far=(), grant=16):
    far = [f if isinstance(f, tuple) else (f, None, None) for f in far]
    size = sum(a.size * a.dtype.itemsize for a in args)
    size += sum(o.size * o.dtype.itemsize for o in outs)
    fetched = [f[0] for f in far]
    specs = [
        pl.BlockSpec(
            memory_space=pltpu.SMEM if i < smem else pltpu.HBM if i in fetched else pltpu.VMEM
        )
        for i in range(len(args))
    ]
    held = []
    for i, _, count in far:
        sizes = args[i].shape
        sizes = sizes if count is None else (sizes[0], count) + sizes[2:]
        held.append(pltpu.VMEM(sizes, args[i].dtype))

    def body(*refs):
        refs = list(refs)
        rest = refs[len(args) :]
        if far:
            spaces, sems = rest[-1 - len(far) : -1], rest[-1]
            rest = rest[: -1 - len(far)]
            copies = []
            for k, (i, start, count) in enumerate(far):
                source = refs[i] if count is None else refs[i].at[:, start : start + count]
                copies.append(pltpu.make_async_copy(source, spaces[k], sems.at[k]))
                copies[-1].start()
            for k, copy in enumerate(copies):
                copy.wait()
                refs[fetched[k]] = spaces[k]
        kernel(*refs[: len(args)], *rest)

    return pl.pallas_call(
        body,
        out_shape=list(outs),
        in_specs=specs,
        out_specs=[pl.BlockSpec(memory_space=pltpu.VMEM)] * len(outs),
        scratch_shapes=list(scratch) + held + ([pltpu.SemaphoreType.DMA((len(far),))] if far else []),
        compiler_params=pltpu.CompilerParams(vmem_limit_bytes=grant * 2**20),
        cost_estimate=pl.CostEstimate(
            flops=int(flops), bytes_accessed=int(size), transcendentals=0
        ),
    )(*args)


def shape(dtype, *sizes):
    return jax.ShapeDtypeStruct(sizes, dtype)


def norm_parts(stream):
    center = stream - jnp.mean(stream, axis=-1, keepdims=True)
    factor = lax.rsqrt(jnp.mean(center * center, axis=-1, keepdims=True) + EPS)
    return center * factor, factor


def place_attention(w, w_qkv, w_out):
    for g in range(8):
        rows = slice(128 * g, 128 * g + 128)
        for i in range(2):
            w_qkv[rows, 128 * i : 128 * i + 128] = w[2 * g + i, :128]
            w_out[64 * i : 64 * i + 64, rows] = w[2 * g + i, 192:256]
        first, second = w[2 * g, 128:192], w[2 * g + 1, 128:192]
        w_qkv[128 * g : 128 * g + 64, 256:] = jnp.concatenate(
            [first[:, :64], second[:, :64]], axis=1
        )
        w_qkv[128 * g + 64 : 128 * g + 128, 256:] = jnp.concatenate(
            [first[:, 64:], second[:, 64:]], axis=1
        )


def place_mlp(w, w_up, w_down):
    for g in range(8):
        rows = slice(128 * g, 128 * g + 128)
        for i in range(2):
            for j in range(2):
                at = 256 * i + 128 * j
                w_up[rows, at : at + 128] = w[2 * g + i, 128 * j : 128 * j + 128]
            w_down[256 * i : 256 * i + 256, rows] = w[2 * g + i, 256:512]


def both_rows(mine, other):
    return jnp.concatenate([mine[...], other[...]], axis=0)


def softmax(valid, query, key):
    scores = dot(query, key, 1, 1) * 64**-0.5
    at = lax.broadcasted_iota(jnp.int32, (1, ROWS), 1)
    limit = jnp.where(at < HALF, valid[0], valid[1] + HALF)
    scores = jnp.where(at < limit, scores, -1e30)
    exponent = jnp.exp(scores - jnp.max(scores, axis=-1, keepdims=True))
    return exponent / jnp.sum(exponent, axis=-1, keepdims=True)


def part_of(packed, name, i):
    start = {"q": 128 * i, "k": 128 * i + 64, "v": 256 + 64 * i}[name]
    return packed[:, start : start + 64]


def attention_forward(valid, mine, other, w, bias, packed_out, heads_out, out, away, w_qkv, w_out):
    place_attention(w, w_qkv, w_out)
    packed = dot(both_rows(mine, other), w_qkv[...], 1, 0) + bias[...]
    packed_out[...] = packed.astype(BF)
    heads = []
    for i in range(2):
        query, key, value = [part_of(packed, n, i).astype(BF) for n in "qkv"]
        probs = softmax(valid, query, key).astype(BF)
        heads.append(dot(probs, value, 1, 0))
    heads = jnp.concatenate(heads, axis=1).astype(BF)
    heads_out[...] = heads
    result = dot(heads, w_out[...], 1, 0)
    out[...] = result[:HALF]
    away[...] = result[HALF:].astype(BF)


def attention_backward(valid, mine, other, packed_in, w, grad_out, sums, out, away, w_qkv, w_out):
    place_attention(w, w_qkv, w_out)
    heads_grad = dot(both_rows(mine, other), w_out[...], 1, 1)
    packed = packed_in[...].astype(F32)
    parts = []
    values = []
    for i in range(2):
        query, key, value = [part_of(packed, n, i).astype(BF) for n in "qkv"]
        p = softmax(valid, query, key)
        upstream = heads_grad[:, 64 * i : 64 * i + 64].astype(BF)
        prob_grad = dot(upstream, value, 1, 1)
        values.append(dot(p.astype(BF), upstream, 0, 0))
        score_grad = (
            p * (prob_grad - jnp.sum(prob_grad * p, axis=-1, keepdims=True))
        ).astype(BF)
        parts.append(dot(score_grad, key, 1, 0) * 64**-0.5)
        parts.append(dot(score_grad, query, 0, 0) * 64**-0.5)
    grad = jnp.concatenate(parts + values, axis=1).astype(BF)
    grad_out[...] = grad
    sums[...] = jnp.sum(grad.astype(F32), axis=0, keepdims=True)
    result = dot(grad, w_qkv[...], 1, 1)
    out[...] = result[:HALF]
    away[...] = result[HALF:].astype(BF)


def attention_weights(h_mine, h_other, grad, heads, mine, other, rows_out):
    qkv = dot(both_rows(h_mine, h_other), grad[...], 0, 0)
    back = dot(heads[...], both_rows(mine, other), 0, 0).astype(BF)
    for g in range(8):
        for i in range(2):
            at = 2 * g + i
            rows_out[at, :128] = qkv[128 * g : 128 * g + 128, 128 * i : 128 * i + 128].astype(BF)
            side = qkv[128 * g : 128 * g + 128, 256 + 64 * i : 320 + 64 * i]
            rows_out[at, 128:192] = jnp.concatenate([side[:64], side[64:]], axis=1).astype(BF)
            rows_out[at, 192:256] = back[64 * i : 64 * i + 64, 128 * g : 128 * g + 128]


def mlp_forward(mine, other, w, bias, act_out, slope_out, out, away, w_up, w_down):
    place_mlp(w, w_up, w_down)
    upper = dot(both_rows(mine, other), w_up[...], 1, 0) + bias[...]
    phi = 0.5 * (1.0 + lax.erf(upper * 0.5**0.5))
    act = (upper * phi).astype(BF)
    act_out[...] = act
    slope_out[...] = phi + upper * (jnp.exp(-0.5 * upper * upper) * 0.3989422804014327)
    result = dot(act, w_down[...], 1, 0)
    out[...] = result[:HALF]
    away[...] = result[HALF:].astype(BF)


def mlp_backward(mine, other, w, slope, grad_out, sums, out, away, w_up, w_down):
    place_mlp(w, w_up, w_down)
    grad = (dot(both_rows(mine, other), w_down[...], 1, 1) * slope[...]).astype(BF)
    grad_out[...] = grad
    sums[...] = jnp.sum(grad.astype(F32), axis=0, keepdims=True)
    result = dot(grad, w_up[...], 1, 1)
    out[...] = result[:HALF]
    away[...] = result[HALF:].astype(BF)


def mixed_rows(place, h_mine, h_other, grad, act, mine, other, attention, keep, got, rows_out):
    mlp_weights(h_mine, h_other, grad, act, mine, other, rows_out)
    tokens = owner_rows(place[1] == 0, keep, got)
    for g in range(8):
        for i in range(2):
            rows_out[2 * g + i, 512:768] = attention[2 * g + i]
            rows_out[2 * g + i, 768:] = tokens[i]


def mlp_weights(h_mine, h_other, grad, act, mine, other, rows_out):
    up = dot(both_rows(h_mine, h_other), grad[...], 0, 0).astype(BF)
    down = dot(act[...], both_rows(mine, other), 0, 0).astype(BF)
    for g in range(8):
        cols = slice(128 * g, 128 * g + 128)
        for i in range(2):
            for j in range(2):
                at = 256 * i + 128 * j
                rows_out[2 * g + i, 128 * j : 128 * j + 128] = up[cols, at : at + 128]
            rows_out[2 * g + i, 256:512] = down[256 * i : 256 * i + 256, cols]


def pair_sum(left, got_left, right, got_right):
    return jnp.concatenate(
        [
            left[...].astype(F32) + got_left[...].astype(F32),
            right[...].astype(F32) + got_right[...].astype(F32),
        ],
        axis=1,
    )


def ring_place(ring, blocks, store):
    for step, block in zip((0, 1, 3, 2), blocks):
        place = lax.rem(ring + 4 - step, 4) * 128
        for i in range(2):
            store(pl.ds(pl.multiple_of(512 * i + place, 128), 128), block, i)


def norm_first(ring, a, b, c, d, stream_out, out, wide_out, cotangent, sums):
    def store(columns, block, i):
        stream_out[:, columns] = block[i, :HALF].astype(F32)
        for depth in range(2):
            rows = block[i, HALF + 16 * depth : HALF + 16 * depth + 16].astype(F32)
            wide_out[depth, :, columns] = rows[:8] + rows[8:]
        upstream = block[i, HALF + 32 :]
        cotangent[:, columns] = upstream
        sums[:, columns] = jnp.sum(upstream.astype(F32), axis=0, keepdims=True)

    ring_place(ring[0], (a, b, c, d), store)
    normed, _ = norm_parts(stream_out[...])
    out[...] = (normed * wide_out[0, 0:1] + wide_out[0, 1:2]).astype(BF)


def owner_lanes(source, ring, first_core, keep, give):
    parts = []
    for i in range(2):
        at = pl.multiple_of(512 * i + 128 * ring, 128)
        parts.append(source[:, pl.ds(at, 128)].astype(F32))
    lanes = [
        jnp.concatenate([parts[0][:, s], parts[1][:, s]], axis=1)
        for s in (slice(0, 64), slice(64, 128))
    ]
    keep[...] = jnp.where(first_core, lanes[0], lanes[1]).astype(keep.dtype)
    give[...] = jnp.where(first_core, lanes[1], lanes[0]).astype(give.dtype)


def owner_rows(first_core, keep, got):
    keep, got = keep[...].astype(F32), got[...].astype(F32)
    early, late = jnp.where(first_core, keep, got), jnp.where(first_core, got, keep)
    return [
        jnp.concatenate([early[:, s], late[:, s]], axis=1).astype(BF)
        for s in (slice(0, 64), slice(64, 128))
    ]


def owner_tokens(block, live):
    block = block.astype(F32)
    tokens = jnp.concatenate([block[:, :64], block[:, 64:]], axis=0)
    return jnp.where(live, tokens.T[:, :197], 0.0)


def norm_last(place, left, got_left, right, got_right, stream, wide, keep, give, new):
    new[...] = stream[...] + (pair_sum(left, got_left, right, got_right) + wide[1, 5:6])
    owner_lanes(new, place[0], place[1] == 0, keep, give)


def prepare(offset, images, g1, b1, bo, g2, b2, bd, qv, up, w_qkv, w_out, out):
    wide = [jnp.concatenate([v[0:1], v[1:2]], axis=1) for v in (g1, b1, bo, g2, b2, bd)]
    wide = jnp.concatenate(wide + [jnp.zeros((2, 128), F32)], axis=0)
    narrow = [qv[0], qv[1], up[0:1, :128], up[0:1, 128:], up[1:2, :128], up[1:2, 128:]]
    narrow = jnp.concatenate(narrow + [jnp.zeros((2, 128), F32)], axis=0)
    rows = []
    for v in (wide, narrow):
        high = v.astype(BF).astype(F32)
        rows += [high, v - high]
    rows = jnp.concatenate(rows, axis=0).astype(BF)
    side = w_qkv[0, :, 128:].astype(F32)
    side = jnp.concatenate([side[:64], side[64:]], axis=1).astype(BF)
    for w in range(16):
        out[w, :ROWS] = images[jnp.clip(w - offset[0], 0, 2)]
        out[w, ROWS:256] = rows
        out[w, 256:384] = w_qkv[0, :, :128]
        out[w, 384:448] = side
        out[w, 448:512] = w_out[0]


def prepare_next(w_qkv, w_out, w_up, w_down, out):
    side = w_qkv[1, :, 128:].astype(F32)
    side = jnp.concatenate([side[:64], side[64:]], axis=1).astype(BF)
    for w in range(16):
        out[w, :128] = w_up[0, :, :128]
        out[w, 128:256] = w_up[0, :, 128:]
        out[w, 256:512] = w_down[0]
        out[w, 512:640] = w_qkv[1, :, :128]
        out[w, 640:704] = side
        out[w, 704:768] = w_out[1]


def prepare_mlp(w_up, w_down, out):
    for w in range(out.shape[0]):
        out[w, :128] = w_up[1, :, :128]
        out[w, 128:256] = w_up[1, :, 128:]
        out[w, 256:] = w_down[1]


def norm_forward(at, left, got_left, right, got_right, stream, wide, stream_out, out):
    shift, gain, bias = [wide[d, i : i + 1] for d, i in at]
    new = stream[...] + (pair_sum(left, got_left, right, got_right) + shift)
    stream_out[...] = new
    normed, _ = norm_parts(new)
    out[...] = (normed * gain + bias).astype(BF)


def norm_backward(at, left, got_left, right, got_right, stream, upstream, wide, grad_out, low_out, sums):
    grad = pair_sum(left, got_left, right, got_right)
    normed, factor = norm_parts(stream[...])
    scaled = grad * wide[at[0], at[1] : at[1] + 1]
    first = jnp.mean(scaled, axis=-1, keepdims=True)
    second = jnp.mean(scaled * normed, axis=-1, keepdims=True)
    new = upstream[...].astype(F32) + factor * (scaled - first - normed * second)
    grad_out[...] = new
    low = new.astype(BF)
    low_out[...] = low.astype(low_out.dtype)
    sums[0:1] = jnp.sum(grad * normed, axis=0, keepdims=True)
    sums[1:2] = jnp.sum(grad, axis=0, keepdims=True)
    sums[2:3] = jnp.sum(low.astype(F32), axis=0, keepdims=True)
    sums[3:8] = jnp.zeros((5, WIDTH), F32)


def norm_backward_last(
    place, left, got_left, right, got_right, stream, upstream, wide, s20, s11, s21, low_sum,
    keep, give, keep_v, give_v, new, sums, table,
):
    norm_backward((0, 0), left, got_left, right, got_right, stream, upstream, wide, new, new, sums)
    owner_lanes(new, place[0], place[1] == 0, keep, give)
    pieces = [sums[0:2], s20[2:3], s20[0:2], s11[2:3], s11[0:2], s21[2:3], s21[0:2], low_sum[...]]
    table[...] = jnp.concatenate(pieces + [jnp.zeros((4, WIDTH), F32)], axis=0)
    owner_lanes(table, place[0], place[1] == 0, keep_v, give_v)


def final_rows(place, rows_in, keep, got, keep_v, got_v, p0, p1, u0, u1, out, held, sem):
    wide = keep_v[...] + got_v[...]
    high = wide.astype(BF).astype(F32)
    low = wide - high
    tokens = owner_rows(place[1] == 0, keep, got)
    for i in range(2):
        part = slice(64 * i, 64 * i + 64)
        narrow = [
            jnp.concatenate(
                [p[:, 128 * i : 128 * i + 64], p[:, 256 + 64 * i : 320 + 64 * i]], axis=1
            )
            for p in (p0, p1)
        ]
        for u in (u0, u1):
            narrow += [u[:, 256 * i : 256 * i + 128], u[:, 256 * i + 128 : 256 * i + 256]]
        narrow = jnp.concatenate(narrow + [jnp.zeros((2, 128), F32)], axis=0)
        narrow_high = narrow.astype(BF).astype(F32)
        rows = jnp.concatenate(
            [jnp.concatenate([high[:, part], low[:, part]], axis=1), narrow_high, narrow - narrow_high],
            axis=0,
        ).astype(BF)
        for g in range(8):
            held[2 * g + i, :HALF] = tokens[i]
            held[2 * g + i, HALF:] = rows
    copy = pltpu.make_async_copy(held, out.at[:, 256:400], sem)
    copy.start()
    copy.wait()


def collect(meta, received, out, held, sems):
    copies = []
    for s in range(3):
        at = jnp.minimum(meta[0] + s, 15)
        copies.append(
            pltpu.make_async_copy(received.at[at, 768:880], held.at[s], sems.at[s])
        )
        copies[-1].start()
    for s in range(3):
        copies[s].wait()
        out[s] = owner_tokens(held[s], s < meta[1])


def finish(meta, received, sum_1, out, qkv, w_out, g1, b1, bo, g2, b2, bd, qv, up, weights, vectors, held, sems):
    copies = [
        pltpu.make_async_copy(received.at[:, 0:256], weights, sems.at[3]),
        pltpu.make_async_copy(received.at[:, 368:400], vectors, sems.at[4]),
    ]
    for s in range(3):
        at = jnp.minimum(meta[0] + s, 15)
        copies.append(
            pltpu.make_async_copy(received.at[at, 256:368], held.at[s], sems.at[s])
        )
    for copy in copies:
        copy.start()
    for copy in copies:
        copy.wait()
    for s in range(3):
        out[s] = owner_tokens(held[s], s < meta[1])
    total_v = jnp.sum(vectors[...].astype(F32), axis=0)
    wide = total_v[:16, :64] + total_v[:16, 64:]
    for v, ref in enumerate((g1, b1, bo, g2, b2, bd)):
        ref[...] = jnp.concatenate([wide[v : v + 1], wide[v + 6 : v + 7]], axis=0)
    narrow = total_v[16:24] + total_v[24:32]
    qv[...] = narrow[0:2]
    for d in range(2):
        up[d : d + 1] = jnp.concatenate([narrow[2 + 2 * d : 3 + 2 * d], narrow[3 + 2 * d : 4 + 2 * d]], axis=1)
    for d in range(2):
        block = jnp.sum(weights[...].astype(F32), axis=0) if d == 0 else sum_1[...]
        side = block[128:192]
        qkv[d, :, :128] = block[:128]
        qkv[d, :64, 128:] = side[:, :64]
        qkv[d, 64:, 128:] = side[:, 64:]
        w_out[d] = block[192:256]


ATTENTION_SCRATCH = (pltpu.VMEM((WIDTH, 384), BF), pltpu.VMEM((128, WIDTH), BF))
MLP_SCRATCH = (pltpu.VMEM((WIDTH, 512), BF), pltpu.VMEM((512, WIDTH), BF))
SUM_SHAPES = (shape(F32, HALF, WIDTH), shape(BF, HALF, WIDTH))
NORM_SHAPES = (shape(F32, HALF, WIDTH), shape(BF, HALF, WIDTH))
ATTENTION_FLOPS = 2 * ROWS * WIDTH * 512
MLP_FLOPS = 2 * ROWS * WIDTH * 1024


def exchange(chunks):
    return lax.all_to_all(chunks, DP, 0, 0)


def shards(
    inputs,
    cotangent,
    group_images,
    ln1_gain,
    ln1_bias,
    w_qkv,
    b_qv,
    w_out,
    b_out,
    ln2_gain,
    ln2_bias,
    w_up,
    b_up,
    w_down,
    b_down,
):
    seq = inputs.shape[1]
    half, rows = HALF, ROWS
    core = lax.axis_index("c")
    ring = lax.axis_index("z")
    group = lax.axis_index(("y", "xl"))
    worker = lax.axis_index(DP)
    first_core = core == 0

    earlier = jnp.arange(8)[:, None] > jnp.arange(8)[None, :]
    offsets = jnp.sum(jnp.where(earlier, group_images[None, :], 0), axis=1)
    my_offset = jnp.sum(jnp.where(jnp.arange(8) < group, group_images, 0))
    my_live = jnp.sum(jnp.where(jnp.arange(8) == group, group_images, 0))
    source = jnp.sum((offsets <= worker).astype(jnp.int32)) - 1
    valid = jnp.where(first_core, jnp.array([half, seq - half]), jnp.array([seq - half, half]))
    valid = valid.astype(jnp.int32)

    images = jnp.concatenate([inputs, cotangent], axis=-1)
    images = jnp.pad(images, ((0, 0), (0, rows - seq), (0, 0)))
    w_qkv = w_qkv.reshape(2, 128, 192)
    (chunks,) = run(
        prepare,
        (shape(BF, 16, 512, 128),),
        (my_offset.reshape(1), images, ln1_gain, ln1_bias, b_out, ln2_gain, ln2_bias)
        + (b_down, b_qv, b_up, w_qkv, w_out),
        0,
        (),
        1,
        range(2, 12),
        56,
    )
    arrived = exchange(chunks)
    (next_rows,) = run(
        prepare_next, (shape(BF, 16, 768, 128),), (w_qkv, w_out, w_up, w_down), 0
    )
    (mlp_rows_1,) = run(prepare_mlp, (shape(BF, 16, 512, 128),), (w_up, w_down), 0)
    next_rows, mlp_rows_1, arrived = lax.optimization_barrier((next_rows, mlp_rows_1, arrived))
    following = exchange(next_rows)
    mlp_w = [following, None]
    attention_w = [arrived, following]
    attention_at = [256, 512]

    picked = lax.dynamic_slice(arrived, (2 * source, 0, 0), (2, rows, 128))
    vectors_here = arrived[:2, rows:256]
    low_part, high_part = picked[:, :half], picked[:, half:rows]
    tail = vectors_here[:, :16]
    keep = jnp.concatenate([jnp.where(first_core, low_part, high_part), tail], axis=1)
    give = jnp.concatenate([jnp.where(first_core, high_part, low_part), tail], axis=1)
    got = core_swap(give)
    part_0 = jnp.where(first_core, keep, got)
    part_1 = jnp.where(first_core, got, keep)
    left = jnp.concatenate([part_0[..., :64], part_1[..., :64]], axis=-1)
    right = jnp.concatenate([part_0[..., 64:], part_1[..., 64:]], axis=-1)
    place = jnp.stack([ring, core]).astype(jnp.int32)
    stream, h1, wide, cotangent_low, low_sum = run(
        norm_first,
        NORM_SHAPES
        + (shape(F32, 2, 8, WIDTH), shape(BF, half, WIDTH), shape(F32, 1, WIDTH)),
        [place] + ring_blocks(jnp.concatenate([left, right[:, half:], right[:, :half]], axis=1)),
        0,
        (),
        1,
    )
    narrow_all = vectors_here[:, 16:].astype(F32)
    narrow_all = narrow_all[:, :8] + narrow_all[:, 8:]
    bias_qv = [narrow_all[:, d] for d in range(2)]
    bias_up = [narrow_all[:, 2 + 2 * d : 4 + 2 * d].reshape(512) for d in range(2)]

    row = lambda v: v.reshape(1, -1)
    bias_packed = [
        jnp.concatenate(
            [bias_qv[d][0, :64], jnp.zeros(64), bias_qv[d][1, :64], jnp.zeros(64)]
            + [bias_qv[d][0, 64:], bias_qv[d][1, 64:]]
        )[None]
        for d in range(2)
    ]

    kept = []
    for d in range(2):
        h1_other = core_swap(h1)
        packed, heads, mine, theirs = run(
            attention_forward,
            (shape(BF, ROWS, 384), shape(BF, ROWS, 128)) + SUM_SHAPES,
            (valid, h1, h1_other, attention_w[d], bias_packed[d]),
            ATTENTION_FLOPS,
            ATTENTION_SCRATCH,
            1,
            ((3, attention_at[d], 256),),
        )
        pairs, _, _ = total(mine, theirs)
        if d == 1:
            pairs, mlp_w[1] = lax.optimization_barrier((pairs, mlp_w[1]))
        middle, h2 = run(
            functools.partial(norm_forward, ((d, 2), (d, 3), (d, 4))),
            NORM_SHAPES,
            pairs + (stream, wide),
            0,
        )
        h2_other = core_swap(h2)
        act, slope, mine, theirs = run(
            mlp_forward,
            (shape(BF, ROWS, 512), shape(F32, ROWS, 512)) + SUM_SHAPES,
            (h2, h2_other, mlp_w[d], row(bias_up[d])),
            MLP_FLOPS,
            MLP_SCRATCH,
            0,
            ((2, 0, 512),),
        )
        kept.append((stream, h1, h1_other, packed, heads, middle, h2, h2_other, act, slope))
        if d == 0:
            pairs, _, _ = total(mine, theirs)
            mlp_rows_1, _ = lax.optimization_barrier((mlp_rows_1, following))
            mlp_w[1] = exchange(mlp_rows_1)
            stream, h1 = run(
                functools.partial(norm_forward, ((0, 5), (1, 0), (1, 1))),
                NORM_SHAPES,
                pairs + (middle, wide),
                0,
            )
    grad_low = cotangent_low
    low_other = core_swap(grad_low)
    pairs, _, _ = total(mine, theirs)
    keep, give = run(
        norm_last,
        (shape(BF, half, 128), shape(BF, half, 128)),
        (place,) + pairs + (middle, wide),
        0,
        (pltpu.VMEM((half, WIDTH), F32),),
        1,
    )
    out_keep, out_got = keep, core_swap(give)

    grad_stream = cotangent_low
    previous = mlp_got = None
    sums, narrow_sums = {}, {}
    for d in (1, 0):
        start, h1, h1_other, packed, heads, middle, h2, h2_other, act, slope = kept[d]
        if d == 0:
            low_other = core_swap(grad_low)
            low_other, mlp_got = lax.optimization_barrier((low_other, previous))
        upper_grad, up_sum, mine, theirs = run(
            mlp_backward,
            (shape(BF, ROWS, 512), shape(F32, 1, 512)) + SUM_SHAPES,
            (grad_low, low_other, mlp_w[d], slope),
            MLP_FLOPS,
            MLP_SCRATCH,
            0,
            ((2, 0, 512), 3),
        )

        def mlp_work(upper_grad):
            args = (h2, h2_other, upper_grad, act, grad_low, low_other)
            if d == 0:
                return run(
                    mixed_rows,
                    (shape(BF, 16, 880, 128),),
                    (place,) + args + (attention_grad, out_keep, out_got),
                    MLP_FLOPS,
                    (),
                    1,
                    (1, 2, 4),
                )[0]
            return run(mlp_weights, (shape(BF, 16, 512, 128),), args, MLP_FLOPS, (), 0, (0, 1, 3))[0]

        pairs, mlp_grad, _ = total(mine, theirs, (mlp_work, upper_grad))
        if d == 0:
            mlp_grad, mlp_got = lax.optimization_barrier((mlp_grad, mlp_got))
        previous = exchange(mlp_grad)
        grad_stream, grad_low, sums[2, d] = run(
            functools.partial(norm_backward, (d, 3)),
            NORM_SHAPES + (shape(F32, 8, WIDTH),),
            pairs + (middle, grad_stream, wide),
            0,
        )
        low_other = core_swap(grad_low)
        packed_grad, packed_sum, mine, theirs = run(
            attention_backward,
            (shape(BF, ROWS, 384), shape(F32, 1, 384)) + SUM_SHAPES,
            (valid, grad_low, low_other, packed, attention_w[d]),
            ATTENTION_FLOPS,
            ATTENTION_SCRATCH,
            1,
            (3, (4, attention_at[d], 256)),
        )
        narrow_sums[d] = (packed_sum, up_sum)

        def attention_work(packed_grad):
            return run(
                attention_weights,
                (shape(BF, 16, 256 if d == 1 else 400, 128),),
                (h1, h1_other, packed_grad, heads, grad_low, low_other),
                ATTENTION_FLOPS,
                (),
                0,
                (0, 1, 3),
            )[0]

        pairs, attention_grad, _ = total(mine, theirs, (attention_work, packed_grad))
        if d == 1:
            grad_stream, grad_low, sums[1, d] = run(
                functools.partial(norm_backward, (d, 0)),
                NORM_SHAPES + (shape(F32, 8, WIDTH),),
                pairs + (start, grad_stream, wide),
                0,
            )
    keep, give, keep_v, give_v = run(
        norm_backward_last,
        (shape(BF, half, 128), shape(BF, half, 128), shape(F32, 16, 128), shape(F32, 16, 128)),
        (place,) + pairs + (start, grad_stream, wide, sums[2, 0], sums[1, 1], sums[2, 1], low_sum),
        0,
        (pltpu.VMEM((half, WIDTH), F32), pltpu.VMEM((8, WIDTH), F32), pltpu.VMEM((16, WIDTH), F32)),
        1,
    )
    (last_rows,) = pl.pallas_call(
        final_rows,
        out_shape=[shape(BF, 16, 400, 128)],
        in_specs=[pl.BlockSpec(memory_space=pltpu.SMEM), pl.BlockSpec(memory_space=pltpu.HBM)]
        + [pl.BlockSpec(memory_space=pltpu.VMEM)] * 8,
        out_specs=[pl.BlockSpec(memory_space=pltpu.HBM)],
        scratch_shapes=[pltpu.VMEM((16, 144, 128), BF), pltpu.SemaphoreType.DMA(())],
        input_output_aliases={1: 0},
        compiler_params=pltpu.CompilerParams(vmem_limit_bytes=16 * 2**20),
    )(
        place,
        attention_grad,
        keep,
        core_swap(give),
        keep_v,
        core_swap(give_v),
        narrow_sums[0][0],
        narrow_sums[1][0],
        narrow_sums[0][1],
        narrow_sums[1][1],
    )
    last_rows, previous = lax.optimization_barrier((last_rows, previous))
    last = exchange(last_rows)
    mixed, _ = lax.optimization_barrier((previous, last_rows))

    def summed(block):
        return jnp.sum(block.astype(F32), axis=0)

    mlp = [summed(mixed[:, :512]), summed(mlp_got)]
    grad_up = jnp.stack([jnp.concatenate([m[:128], m[128:256]], axis=-1) for m in mlp])
    grad_down = jnp.stack([m[256:] for m in mlp])
    meta = jnp.stack([my_offset, my_live]).astype(jnp.int32)
    hbm, vmem = pl.BlockSpec(memory_space=pltpu.HBM), pl.BlockSpec(memory_space=pltpu.VMEM)
    smem = pl.BlockSpec(memory_space=pltpu.SMEM)
    (result,) = pl.pallas_call(
        collect,
        out_shape=[shape(F32, 3, 64, seq)],
        in_specs=[smem, hbm],
        out_specs=[vmem],
        scratch_shapes=[pltpu.VMEM((3, half, 128), BF), pltpu.SemaphoreType.DMA((3,))],
    )(meta, mixed)
    grad_inputs, grad_qkv, grad_out, g1, b1, bo, g2, b2, bd, grad_qv, grad_b_up = pl.pallas_call(
        finish,
        out_shape=[shape(F32, 3, 64, seq), shape(F32, 2, 128, 192), shape(F32, 2, 64, 128)]
        + [shape(F32, 2, 64)] * 6
        + [shape(F32, 2, 128), shape(F32, 2, 256)],
        in_specs=[smem, hbm, vmem],
        out_specs=[vmem] * 11,
        scratch_shapes=[
            pltpu.VMEM((16, 256, 128), BF),
            pltpu.VMEM((16, 32, 128), BF),
            pltpu.VMEM((3, half, 128), BF),
            pltpu.SemaphoreType.DMA((5,)),
        ],
        compiler_params=pltpu.CompilerParams(vmem_limit_bytes=16 * 2**20),
    )(meta, last, summed(mixed[:, 512:768]))
    return (
        result.transpose(0, 2, 1),
        grad_inputs.transpose(0, 2, 1),
        g1,
        b1,
        grad_qkv[:, :, None, :],
        grad_qv[:, None, :],
        grad_out,
        bo,
        g2,
        b2,
        grad_up,
        grad_b_up,
        grad_down,
        bd,
    )


def solution(mesh):
    split = Mesh(mesh.devices.reshape(4, 2, 2, 4, 2), ("y", "xl", "xh", "z", "c"))
    gx = ("y", "xl")
    gy = ("xh", "z", "c")
    token = P(gx, None, gy)
    vector = P(None, gy)
    return jax.shard_map(
        shards,
        mesh=split,
        in_specs=(
            token,
            token,
            P(),
            vector,
            vector,
            P(None, gx, gy, None),
            P(None, gy, None),
            P(None, gy, gx),
            vector,
            vector,
            vector,
            P(None, gx, gy),
            vector,
            P(None, gy, gx),
            vector,
        ),
        out_specs=(
            token,
            token,
            vector,
            vector,
            P(None, gx, gy, None),
            P(None, gy, None),
            P(None, gy, gx),
            vector,
            vector,
            vector,
            P(None, gx, gy),
            vector,
            P(None, gy, gx),
            vector,
        ),
        check_vma=False,
    )
```

profile of v0, /device:TPU:4, one launch (start us, length us, event | category | flops | bytes accessed | tf_op | source)
XLA Modules:
  0.0 320.7 jit_solution(12302112352281786904)
XLA Ops:
  6.5 4.3 %shard_map.274 = bf16[16,512,128]{2,1,0:T(8,128)(2,1)} custom-call(s32[1]{0:T(128)} %bitcast.refs_0_, bf16[3,224,128]{2,1,0:T(8,128)(2,1)} %fusion.5.refs_1_, f32[2,64]{1,0:T(2,128)} %refs_2_.3, f32[2,64]{1,0:T(2,128)} %refs_3_.3, f32[2,64]{1,0:T(2,128)} %refs_4_.1, f32[2,64]{1,0:T(2,128)} %refs_5_.1, f32[2,64]{1,0:T(2,128)} %refs_6_.1, f32[2,64]{1,0:T(2,128)} %refs_7_.1, ...), custom_call_target="tpu_custom_call" | custom-call | bytes 2406404 | tf_op jit(solution)/shard_map/pallas_call | solution.py:88
  10.8 7.6 %all-to-all-start = ((bf16[16,512,128]{2,1,0:T(8,128)(2,1)}), bf16[16,512,128]{2,1,0:T(8,128)(2,1)}, u32[]{:S(2)}, u32[]{:S(2)}) async-start(bf16[16,512,128]{2,1,0:T(8,128)(2,1)} %shard_map.274), calls=%async_computation | async-start | bytes 4194304 | tf_op jit(solution)/shard_map/all_to_all | solution.py:473
  24.4 22.3 %all-to-all-done.refs_3_.refs_4_ = bf16[16,512,128]{2,1,0:T(8,128)(2,1)} async-done(((bf16[16,512,128]{2,1,0:T(8,128)(2,1)}), bf16[16,512,128]{2,1,0:T(8,128)(2,1)}, u32[]{:S(2)}, u32[]{:S(2)}) %all-to-all-start) | async-done | bytes 2097184 | tf_op jit(solution)/shard_map/all_to_all | solution.py:473
  47.4 5.4 %all-to-all-start.1 = ((bf16[16,768,128]{2,1,0:T(8,128)(2,1)}), bf16[16,768,128]{2,1,0:T(8,128)(2,1)S(1)}, u32[]{:S(2)}, u32[]{:S(2)}) async-start(bf16[16,768,128]{2,1,0:T(8,128)(2,1)} %copy-done.2), calls=%async_computation.1 | async-start | bytes 6291456 | tf_op jit(solution)/shard_map/all_to_all | solution.py:473
  55.3 2.0 collective-permute-start.1
  57.2 2.2 collective-permute-start.2
  61.2 1.9 collective-permute-done.1.refs_2_
  63.2 2.2 collective-permute-done.2.refs_3_
  72.0 3.7 %shard_map.276 = (bf16[224,384]{1,0:T(8,128)(2,1)S(1)}, bf16[224,128]{1,0:T(8,128)(2,1)S(1)}, f32[112,1024]{1,0:T(8,128)S(1)}, bf16[112,1024]{1,0:T(8,128)(2,1)S(1)}) custom-call(s32[2]{0:T(128)S(1)} %broadcast_select_fusion.4.refs_0_, bf16[112,1024]{1,0:T(8,128)(2,1)} %get-tuple-element.129.refs_1_.refs_0_, ...), custom_call_target="tpu_custom_call" | custom-call | flops 234881024 | bytes 3474952 | tf_op jit(solution)/shard_map/pallas_call | solution.py:88
  79.4 3.2 %collective-permute-done.7 = bf16[112,512]{1,0:T(8,128)(2,1)S(1)} collective-permute-done((bf16[112,512]{1,0:T(8,128)(2,1)S(1)}, bf16[112,512]{1,0:T(8,128)(2,1)S(1)}, u32[]{:S(2)}, u32[]{:S(2)}) %collective-permute-start.7) | collective-permute-done | bytes 114720 | tf_op jit(solution)/shard_map/ppermute | solution.py:39
  82.6 2.1 collective-permute-done.8
  86.3 3.3 %collective-permute-done.10.refs_3_ = bf16[112,512]{1,0:T(8,128)(2,1)S(1)} collective-permute-done((bf16[112,512]{1,0:T(8,128)(2,1)S(1)}, bf16[112,512]{1,0:T(8,128)(2,1)S(1)}, u32[]{:S(2)}, u32[]{:S(2)}) %collective-permute-start.10) | collective-permute-done | bytes 114720 | tf_op jit(solution)/shard_map/ppermute | solution.py:46
  96.0 1.9 shard_map.278
  100.5 7.2 %all-to-all-start.2 = ((bf16[16,512,128]{2,1,0:T(8,128)(2,1)}), bf16[16,512,128]{2,1,0:T(8,128)(2,1)}, u32[]{:S(2)}, u32[]{:S(2)}) async-start(bf16[16,512,128]{2,1,0:T(8,128)(2,1)} %copy-done.3), calls=%async_computation.2 | async-start | bytes 4194304 | tf_op jit(solution)/shard_map/all_to_all | solution.py:473
  110.9 3.0 collective-permute-done.13
  113.8 1.9 collective-permute-done.14
  117.0 4.9 %collective-permute-done.15.refs_1_ = bf16[112,512]{1,0:T(8,128)(2,1)S(1)} collective-permute-done((bf16[112,512]{1,0:T(8,128)(2,1)S(1)}, bf16[112,512]{1,0:T(8,128)(2,1)S(1)}, u32[]{:S(2)}, u32[]{:S(2)}) %collective-permute-start.15) | collective-permute-done | bytes 114720 | tf_op jit(solution)/shard_map/ppermute | solution.py:45
  125.8 2.5 shard_map.280
  130.0 2.1 collective-permute-start.20
  132.2 3.1 collective-permute-done.19
  136.6 2.1 collective-permute-start.21
  139.3 3.3 %collective-permute-done.21.refs_1_ = bf16[112,512]{1,0:T(8,128)(2,1)S(1)} collective-permute-done((bf16[112,512]{1,0:T(8,128)(2,1)S(1)}, bf16[112,512]{1,0:T(8,128)(2,1)S(1)}, u32[]{:S(2)}, u32[]{:S(2)}) %collective-permute-start.21) | collective-permute-done | bytes 114720 | tf_op jit(solution)/shard_map/ppermute | solution.py:45
  151.8 2.6 shard_map.282
  155.9 2.5 shard_map.283
  168.6 7.2 %all-to-all-start.3 = ((bf16[16,512,128]{2,1,0:T(8,128)(2,1)}), bf16[16,512,128]{2,1,0:T(8,128)(2,1)}, u32[]{:S(2)}, u32[]{:S(2)}) async-start(bf16[16,512,128]{2,1,0:T(8,128)(2,1)} %copy-done.4), calls=%async_computation.3 | async-start | bytes 4194304 | tf_op jit(solution)/shard_map/all_to_all | solution.py:473
  182.1 2.7 shard_map.286
  186.4 2.1 collective-permute-start.31
  188.5 2.0 collective-permute-start.32
  194.7 2.1 collective-permute-start.33
  196.8 9.4 %collective-permute-start.34 = (bf16[112,512]{1,0:T(8,128)(2,1)S(1)}, bf16[112,512]{1,0:T(8,128)(2,1)S(1)}, u32[]{:S(2)}, u32[]{:S(2)}) collective-permute-start(bf16[112,512]{1,0:T(8,128)(2,1)S(1)} %get-tuple-element.176.refs_2_), channel_id=1, source_target_pairs={{0,2},{2,0},{4,6},{6,4},{1,3},{3,1},{5,7},{7,5},{8,10},{10,8},{12,... | collective-permute-start | bytes 344072 | tf_op jit(solution)/shard_map/ppermute | solution.py:46
  206.3 4.7 %collective-permute-done.34.refs_3_ = bf16[112,512]{1,0:T(8,128)(2,1)S(1)} collective-permute-done((bf16[112,512]{1,0:T(8,128)(2,1)S(1)}, bf16[112,512]{1,0:T(8,128)(2,1)S(1)}, u32[]{:S(2)}, u32[]{:S(2)}) %collective-permute-start.34) | collective-permute-done | bytes 114720 | tf_op jit(solution)/shard_map/ppermute | solution.py:46
  221.9 2.1 collective-permute-start.37
  224.0 1.9 collective-permute-start.38
  229.6 2.3 shard_map.291
  231.9 1.8 copy-done.1
  233.8 7.4 %all-to-all-start.4 = ((bf16[16,880,128]{2,1,0:T(8,128)(2,1)}), bf16[16,880,128]{2,1,0:T(8,128)(2,1)}, u32[]{:S(2)}, u32[]{:S(2)}) async-start(bf16[16,880,128]{2,1,0:T(8,128)(2,1)} %copy-done.1), calls=%async_computation.4 | async-start | bytes 7208960 | tf_op jit(solution)/shard_map/all_to_all | solution.py:473
  241.2 1.9 collective-permute-start.45
  243.1 4.1 %collective-permute-done.45.refs_1_ = bf16[112,512]{1,0:T(8,128)(2,1)S(1)} collective-permute-done((bf16[112,512]{1,0:T(8,128)(2,1)S(1)}, bf16[112,512]{1,0:T(8,128)(2,1)S(1)}, u32[]{:S(2)}, u32[]{:S(2)}) %collective-permute-start.45) | collective-permute-done | bytes 114720 | tf_op jit(solution)/shard_map/ppermute | solution.py:45
  250.0 3.9 %shard_map.293 = (bf16[224,384]{1,0:T(8,128)(2,1)S(1)}, f32[1,384]{1,0:T(1,128)S(1)}, f32[112,1024]{1,0:T(8,128)S(1)}, bf16[112,1024]{1,0:T(8,128)(2,1)S(1)}) custom-call(s32[2]{0:T(128)S(1)} %copy-done.61, bf16[112,1024]{1,0:T(8,128)(2,1)S(1)} %get-tuple-element.198.refs_1_.refs_4_, bf16[112,1024]{1,0:T(8,128)(2,1)S(1)} %collective-permute-done.47.refs_2_.refs_5_, ...), custom_call_target="tpu_custom_call" | custom-call | flops 234881024 | bytes 3589640 | tf_op jit(solution)/shard_map/pallas_call | solution.py:88
  257.0 1.9 pad_add_fusion.meta
  263.6 1.9 convert_reduce_fusion
  265.5 2.8 collective-permute-done.51.refs_2_
  272.8 15.0 %all-to-all-done.4.received = bf16[16,880,128]{2,1,0:T(8,128)(2,1)} async-done(((bf16[16,880,128]{2,1,0:T(8,128)(2,1)}), bf16[16,880,128]{2,1,0:T(8,128)(2,1)}, u32[]{:S(2)}, u32[]{:S(2)}) %all-to-all-start.4) | async-done | bytes 3604512 | tf_op jit(solution)/shard_map/all_to_all | solution.py:473
  287.8 8.3 %all-to-all-start.5 = ((bf16[16,400,128]{2,1,0:T(8,128)(2,1)}), bf16[16,400,128]{2,1,0:T(8,128)(2,1)S(1)}, u32[]{:S(2)}, u32[]{:S(2)}) async-start(bf16[16,400,128]{2,1,0:T(8,128)(2,1)} %copy-done), calls=%async_computation.5 | async-start | bytes 3276800 | tf_op jit(solution)/shard_map/all_to_all | solution.py:473
  296.1 2.6 shard_map.297
  298.7 1.9 convert_reduce_fusion.1
  303.5 14.3 %all-to-all-done.5.received = bf16[16,400,128]{2,1,0:T(8,128)(2,1)S(1)} async-done(((bf16[16,400,128]{2,1,0:T(8,128)(2,1)}), bf16[16,400,128]{2,1,0:T(8,128)(2,1)S(1)}, u32[]{:S(2)}, u32[]{:S(2)}) %all-to-all-start.5) | async-done | bytes 1638432 | tf_op jit(solution)/shard_map/all_to_all | solution.py:473
  317.8 1.8 shard_map.298
  (313 shorter events, 114.8 us)
Async XLA Ops:
  10.8 35.8 %all-to-all-start = ((bf16[16,512,128]{2,1,0:T(8,128)(2,1)}), bf16[16,512,128]{2,1,0:T(8,128)(2,1)}, u32[]{:S(2)}, u32[]{:S(2)}) async-start(bf16[16,512,128]{2,1,0:T(8,128)(2,1)} %shard_map.274), calls=%async_computation | async-start | bytes 4194304 | tf_op jit(solution)/shard_map/all_to_all | solution.py:473
  47.4 46.8 %all-to-all-start.1 = ((bf16[16,768,128]{2,1,0:T(8,128)(2,1)}), bf16[16,768,128]{2,1,0:T(8,128)(2,1)S(1)}, u32[]{:S(2)}, u32[]{:S(2)}) async-start(bf16[16,768,128]{2,1,0:T(8,128)(2,1)} %copy-done.2), calls=%async_computation.1 | async-start | bytes 6291456 | tf_op jit(solution)/shard_map/all_to_all | solution.py:473
  55.3 7.9 %collective-permute-start.1 = (bf16[2,256,128]{2,1,0:T(8,128)(2,1)S(1)}, bf16[2,256,128]{2,1,0:T(8,128)(2,1)S(1)}, u32[]{:S(2)}, u32[]{:S(2)}) collective-permute-start(bf16[2,256,128]{2,1,0:T(8,128)(2,1)S(1)} %fusion.8.refs_1_), channel_id=1, source_target_pairs={{0,2},{2,4},{4,6},{6,0},{1,3},{3,5},{5,7},{7,1},{8,10},{10,12},{12... | collective-permute-start | bytes 393224 | tf_op jit(solution)/shard_map/ppermute | solution.py:29
  57.2 8.1 %collective-permute-start.2 = (bf16[2,256,128]{2,1,0:T(8,128)(2,1)S(1)}, bf16[2,256,128]{2,1,0:T(8,128)(2,1)S(1)}, u32[]{:S(2)}, u32[]{:S(2)}) collective-permute-start(bf16[2,256,128]{2,1,0:T(8,128)(2,1)S(1)} %fusion.8.refs_1_), channel_id=1, source_target_pairs={{0,6},{2,0},{4,2},{6,4},{1,7},{3,1},{5,3},{7,5},{8,14},{10,8},{12,... | collective-permute-start | bytes 393224 | tf_op jit(solution)/shard_map/ppermute | solution.py:29
  59.4 7.7 %collective-permute-start.3 = (bf16[2,256,128]{2,1,0:T(8,128)(2,1)S(1)}, bf16[2,256,128]{2,1,0:T(8,128)(2,1)S(1)}, u32[]{:S(2)}, u32[]{:S(2)}) collective-permute-start(bf16[2,256,128]{2,1,0:T(8,128)(2,1)S(1)} %fusion.8.refs_1_), channel_id=1, source_target_pairs={{0,4},{2,6},{4,0},{6,2},{1,5},{3,7},{5,1},{7,3},{8,12},{10,14},{12... | collective-permute-start | bytes 393224 | tf_op jit(solution)/shard_map/ppermute | solution.py:29
  70.2 1.8 collective-permute-start.5
  77.3 5.3 %collective-permute-start.7 = (bf16[112,512]{1,0:T(8,128)(2,1)S(1)}, bf16[112,512]{1,0:T(8,128)(2,1)S(1)}, u32[]{:S(2)}, u32[]{:S(2)}) collective-permute-start(bf16[112,512]{1,0:T(8,128)(2,1)S(1)} %get-tuple-element.309), channel_id=1, source_target_pairs={{0,2},{2,0},{4,6},{6,4},{1,3},{3,1},{5,7},{7,5},{8,10},{10,8},{12,... | collective-permute-start | bytes 344072 | tf_op jit(solution)/shard_map/ppermute | solution.py:39
  78.5 6.1 %collective-permute-start.8 = (bf16[112,512]{1,0:T(8,128)(2,1)S(1)}, bf16[112,512]{1,0:T(8,128)(2,1)S(1)}, u32[]{:S(2)}, u32[]{:S(2)}) collective-permute-start(bf16[112,512]{1,0:T(8,128)(2,1)S(1)} %get-tuple-element.308), channel_id=1, source_target_pairs={{0,6},{6,0},{2,4},{4,2},{1,7},{7,1},{3,5},{5,3},{8,14},{14,8},{10,... | collective-permute-start | bytes 344072 | tf_op jit(solution)/shard_map/ppermute | solution.py:40
  84.7 4.9 %collective-permute-start.10 = (bf16[112,512]{1,0:T(8,128)(2,1)S(1)}, bf16[112,512]{1,0:T(8,128)(2,1)S(1)}, u32[]{:S(2)}, u32[]{:S(2)}) collective-permute-start(bf16[112,512]{1,0:T(8,128)(2,1)S(1)} %get-tuple-element.133.refs_2_), channel_id=1, source_target_pairs={{0,2},{2,0},{4,6},{6,4},{1,3},{3,1},{5,7},{7,5},{8,10},{10,8},{12,... | collective-permute-start | bytes 344072 | tf_op jit(solution)/shard_map/ppermute | solution.py:46
  84.8 6.1 %collective-permute-start.9 = (bf16[112,512]{1,0:T(8,128)(2,1)S(1)}, bf16[112,512]{1,0:T(8,128)(2,1)S(1)}, u32[]{:S(2)}, u32[]{:S(2)}) collective-permute-start(bf16[112,512]{1,0:T(8,128)(2,1)S(1)} %get-tuple-element.132.refs_0_), channel_id=1, source_target_pairs={{0,6},{6,0},{2,4},{4,2},{1,7},{7,1},{3,5},{5,3},{8,14},{14,8},{10,... | collective-permute-start | bytes 344072 | tf_op jit(solution)/shard_map/ppermute | solution.py:45
  100.2 7.5 %collective-permute-start.12 = (bf16[112,1024]{1,0:T(8,128)(2,1)}, bf16[112,1024]{1,0:T(8,128)(2,1)}, u32[]{:S(2)}, u32[]{:S(2)}) collective-permute-start(bf16[112,1024]{1,0:T(8,128)(2,1)} %get-tuple-element.139), channel_id=1, source_target_pairs={{0,1},{1,0},{2,3},{3,2},{4,5},{5,4},{6,7},{7,6},{8,9},{9,8},{10,11... | collective-permute-start | bytes 688136 | tf_op jit(solution)/shard_map/ppermute | solution.py:24
  100.5 44.3 %all-to-all-start.2 = ((bf16[16,512,128]{2,1,0:T(8,128)(2,1)}), bf16[16,512,128]{2,1,0:T(8,128)(2,1)}, u32[]{:S(2)}, u32[]{:S(2)}) async-start(bf16[16,512,128]{2,1,0:T(8,128)(2,1)} %copy-done.3), calls=%async_computation.2 | async-start | bytes 4194304 | tf_op jit(solution)/shard_map/all_to_all | solution.py:473
  109.0 4.9 %collective-permute-start.13 = (bf16[112,512]{1,0:T(8,128)(2,1)S(1)}, bf16[112,512]{1,0:T(8,128)(2,1)S(1)}, u32[]{:S(2)}, u32[]{:S(2)}) collective-permute-start(bf16[112,512]{1,0:T(8,128)(2,1)S(1)} %get-tuple-element.305), channel_id=1, source_target_pairs={{0,2},{2,0},{4,6},{6,4},{1,3},{3,1},{5,7},{7,5},{8,10},{10,8},{12,... | collective-permute-start | bytes 344072 | tf_op jit(solution)/shard_map/ppermute | solution.py:39
  109.8 6.0 %collective-permute-start.14 = (bf16[112,512]{1,0:T(8,128)(2,1)S(1)}, bf16[112,512]{1,0:T(8,128)(2,1)S(1)}, u32[]{:S(2)}, u32[]{:S(2)}) collective-permute-start(bf16[112,512]{1,0:T(8,128)(2,1)S(1)} %get-tuple-element.304), channel_id=1, source_target_pairs={{0,6},{6,0},{2,4},{4,2},{1,7},{7,1},{3,5},{5,3},{8,14},{14,8},{10,... | collective-permute-start | bytes 344072 | tf_op jit(solution)/shard_map/ppermute | solution.py:40
  115.8 6.1 %collective-permute-start.15 = (bf16[112,512]{1,0:T(8,128)(2,1)S(1)}, bf16[112,512]{1,0:T(8,128)(2,1)S(1)}, u32[]{:S(2)}, u32[]{:S(2)}) collective-permute-start(bf16[112,512]{1,0:T(8,128)(2,1)S(1)} %get-tuple-element.140.refs_0_), channel_id=1, source_target_pairs={{0,6},{6,0},{2,4},{4,2},{1,7},{7,1},{3,5},{5,3},{8,14},{14,8},{10,... | collective-permute-start | bytes 344072 | tf_op jit(solution)/shard_map/ppermute | solution.py:45
  117.0 4.9 %collective-permute-start.16 = (bf16[112,512]{1,0:T(8,128)(2,1)S(1)}, bf16[112,512]{1,0:T(8,128)(2,1)S(1)}, u32[]{:S(2)}, u32[]{:S(2)}) collective-permute-start(bf16[112,512]{1,0:T(8,128)(2,1)S(1)} %get-tuple-element.141.refs_2_), channel_id=1, source_target_pairs={{0,2},{2,0},{4,6},{6,4},{1,3},{3,1},{5,7},{7,5},{8,10},{10,8},{12,... | collective-permute-start | bytes 344072 | tf_op jit(solution)/shard_map/ppermute | solution.py:46
  123.7 2.1 collective-permute-start.17
  129.9 5.3 %collective-permute-start.19 = (bf16[112,512]{1,0:T(8,128)(2,1)S(1)}, bf16[112,512]{1,0:T(8,128)(2,1)S(1)}, u32[]{:S(2)}, u32[]{:S(2)}) collective-permute-start(bf16[112,512]{1,0:T(8,128)(2,1)S(1)} %get-tuple-element.301), channel_id=1, source_target_pairs={{0,2},{2,0},{4,6},{6,4},{1,3},{3,1},{5,7},{7,5},{8,10},{10,8},{12,... | collective-permute-start | bytes 344072 | tf_op jit(solution)/shard_map/ppermute | solution.py:39
  130.0 6.5 %collective-permute-start.20 = (bf16[112,512]{1,0:T(8,128)(2,1)S(1)}, bf16[112,512]{1,0:T(8,128)(2,1)S(1)}, u32[]{:S(2)}, u32[]{:S(2)}) collective-permute-start(bf16[112,512]{1,0:T(8,128)(2,1)S(1)} %get-tuple-element.300), channel_id=1, source_target_pairs={{0,6},{6,0},{2,4},{4,2},{1,7},{7,1},{3,5},{5,3},{8,14},{14,8},{10,... | collective-permute-start | bytes 344072 | tf_op jit(solution)/shard_map/ppermute | solution.py:40
  136.6 6.1 %collective-permute-start.21 = (bf16[112,512]{1,0:T(8,128)(2,1)S(1)}, bf16[112,512]{1,0:T(8,128)(2,1)S(1)}, u32[]{:S(2)}, u32[]{:S(2)}) collective-permute-start(bf16[112,512]{1,0:T(8,128)(2,1)S(1)} %get-tuple-element.151.refs_0_), channel_id=1, source_target_pairs={{0,6},{6,0},{2,4},{4,2},{1,7},{7,1},{3,5},{5,3},{8,14},{14,8},{10,... | collective-permute-start | bytes 344072 | tf_op jit(solution)/shard_map/ppermute | solution.py:45
  139.3 4.8 %collective-permute-start.22 = (bf16[112,512]{1,0:T(8,128)(2,1)S(1)}, bf16[112,512]{1,0:T(8,128)(2,1)S(1)}, u32[]{:S(2)}, u32[]{:S(2)}) collective-permute-start(bf16[112,512]{1,0:T(8,128)(2,1)S(1)} %get-tuple-element.153.refs_2_), channel_id=1, source_target_pairs={{0,2},{2,0},{4,6},{6,4},{1,3},{3,1},{5,7},{7,5},{8,10},{10,8},{12,... | collective-permute-start | bytes 344072 | tf_op jit(solution)/shard_map/ppermute | solution.py:46
  149.6 6.3 %collective-permute-start.4 = (bf16[112,1024]{1,0:T(8,128)(2,1)S(1)}, bf16[112,1024]{1,0:T(8,128)(2,1)S(1)}, u32[]{:S(2)}, u32[]{:S(2)}) collective-permute-start(bf16[112,1024]{1,0:T(8,128)(2,1)S(1)} %get-tuple-element.128.refs_0_.refs_4_.refs_5_), channel_id=1, source_target_pairs={{0,1},{1,0},{2,3},{3,2},{4,5},{5,4},{6,7},{7,6},{8,9},{9,8},{10,11... | collective-permute-start | bytes 688136 | tf_op jit(solution)/shard_map/ppermute | solution.py:24
  160.1 5.3 %collective-permute-start.25 = (bf16[112,512]{1,0:T(8,128)(2,1)S(1)}, bf16[112,512]{1,0:T(8,128)(2,1)S(1)}, u32[]{:S(2)}, u32[]{:S(2)}) collective-permute-start(bf16[112,512]{1,0:T(8,128)(2,1)S(1)} %get-tuple-element.297), channel_id=1, source_target_pairs={{0,2},{2,0},{4,6},{6,4},{1,3},{3,1},{5,7},{7,5},{8,10},{10,8},{12,... | collective-permute-start | bytes 344072 | tf_op jit(solution)/shard_map/ppermute | solution.py:39
  160.2 6.5 %collective-permute-start.26 = (bf16[112,512]{1,0:T(8,128)(2,1)S(1)}, bf16[112,512]{1,0:T(8,128)(2,1)S(1)}, u32[]{:S(2)}, u32[]{:S(2)}) collective-permute-start(bf16[112,512]{1,0:T(8,128)(2,1)S(1)} %get-tuple-element.296), channel_id=1, source_target_pairs={{0,6},{6,0},{2,4},{4,2},{1,7},{7,1},{3,5},{5,3},{8,14},{14,8},{10,... | collective-permute-start | bytes 344072 | tf_op jit(solution)/shard_map/ppermute | solution.py:40
  167.4 8.4 %collective-permute-start.27 = (bf16[112,512]{1,0:T(8,128)(2,1)}, bf16[112,512]{1,0:T(8,128)(2,1)}, u32[]{:S(2)}, u32[]{:S(2)}) collective-permute-start(bf16[112,512]{1,0:T(8,128)(2,1)} %get-tuple-element.164.refs_0_), channel_id=1, source_target_pairs={{0,6},{6,0},{2,4},{4,2},{1,7},{7,1},{3,5},{5,3},{8,14},{14,8},{10,... | collective-permute-start | bytes 344072 | tf_op jit(solution)/shard_map/ppermute | solution.py:45
  168.6 7.2 %collective-permute-start.28 = (bf16[112,512]{1,0:T(8,128)(2,1)S(1)}, bf16[112,512]{1,0:T(8,128)(2,1)}, u32[]{:S(2)}, u32[]{:S(2)}) collective-permute-start(bf16[112,512]{1,0:T(8,128)(2,1)S(1)} %get-tuple-element.165.refs_2_), channel_id=1, source_target_pairs={{0,2},{2,0},{4,6},{6,4},{1,3},{3,1},{5,7},{7,5},{8,10},{10,8},{12,... | collective-permute-start | bytes 344072 | tf_op jit(solution)/shard_map/ppermute | solution.py:46
  168.6 45.8 %all-to-all-start.3 = ((bf16[16,512,128]{2,1,0:T(8,128)(2,1)}), bf16[16,512,128]{2,1,0:T(8,128)(2,1)}, u32[]{:S(2)}, u32[]{:S(2)}) async-start(bf16[16,512,128]{2,1,0:T(8,128)(2,1)} %copy-done.4), calls=%async_computation.3 | async-start | bytes 4194304 | tf_op jit(solution)/shard_map/all_to_all | solution.py:473
  186.4 6.8 %collective-permute-start.31 = (bf16[112,512]{1,0:T(8,128)(2,1)S(1)}, bf16[112,512]{1,0:T(8,128)(2,1)S(1)}, u32[]{:S(2)}, u32[]{:S(2)}) collective-permute-start(bf16[112,512]{1,0:T(8,128)(2,1)S(1)} %get-tuple-element.293), channel_id=1, source_target_pairs={{0,2},{2,0},{4,6},{6,4},{1,3},{3,1},{5,7},{7,5},{8,10},{10,8},{12,... | collective-permute-start | bytes 344072 | tf_op jit(solution)/shard_map/ppermute | solution.py:39
  188.5 6.1 %collective-permute-start.32 = (bf16[112,512]{1,0:T(8,128)(2,1)S(1)}, bf16[112,512]{1,0:T(8,128)(2,1)S(1)}, u32[]{:S(2)}, u32[]{:S(2)}) collective-permute-start(bf16[112,512]{1,0:T(8,128)(2,1)S(1)} %get-tuple-element.292), channel_id=1, source_target_pairs={{0,6},{6,0},{2,4},{4,2},{1,7},{7,1},{3,5},{5,3},{8,14},{14,8},{10,... | collective-permute-start | bytes 344072 | tf_op jit(solution)/shard_map/ppermute | solution.py:40
  190.6 15.7 %collective-permute-start.39 = (bf16[112,1024]{1,0:T(8,128)(2,1)S(1)}, bf16[112,1024]{1,0:T(8,128)(2,1)S(1)}, u32[]{:S(2)}, u32[]{:S(2)}) collective-permute-start(bf16[112,1024]{1,0:T(8,128)(2,1)S(1)} %copy-done.69), channel_id=1, source_target_pairs={{0,1},{1,0},{2,3},{3,2},{4,5},{5,4},{6,7},{7,6},{8,9},{9,8},{10,11... | collective-permute-start | bytes 688136 | tf_op jit(solution)/shard_map/ppermute | solution.py:24
  194.7 11.6 %collective-permute-start.33 = (bf16[112,512]{1,0:T(8,128)(2,1)S(1)}, bf16[112,512]{1,0:T(8,128)(2,1)S(1)}, u32[]{:S(2)}, u32[]{:S(2)}) collective-permute-start(bf16[112,512]{1,0:T(8,128)(2,1)S(1)} %get-tuple-element.175.refs_0_), channel_id=1, source_target_pairs={{0,6},{6,0},{2,4},{4,2},{1,7},{7,1},{3,5},{5,3},{8,14},{14,8},{10,... | collective-permute-start | bytes 344072 | tf_op jit(solution)/shard_map/ppermute | solution.py:45
  196.8 14.2 %collective-permute-start.34 = (bf16[112,512]{1,0:T(8,128)(2,1)S(1)}, bf16[112,512]{1,0:T(8,128)(2,1)S(1)}, u32[]{:S(2)}, u32[]{:S(2)}) collective-permute-start(bf16[112,512]{1,0:T(8,128)(2,1)S(1)} %get-tuple-element.176.refs_2_), channel_id=1, source_target_pairs={{0,2},{2,0},{4,6},{6,4},{1,3},{3,1},{5,7},{7,5},{8,10},{10,8},{12,... | collective-permute-start | bytes 344072 | tf_op jit(solution)/shard_map/ppermute | solution.py:46
  211.5 2.1 collective-permute-start.35
  212.3 5.8 %collective-permute-start.40 = (bf16[112,512]{1,0:T(8,128)(2,1)}, bf16[112,512]{1,0:T(8,128)(2,1)}, u32[]{:S(2)}, u32[]{:S(2)}) collective-permute-start(bf16[112,512]{1,0:T(8,128)(2,1)} %get-tuple-element.285), channel_id=1, source_target_pairs={{0,2},{2,0},{4,6},{6,4},{1,3},{3,1},{5,7},{7,5},{8,10},{10,8},{12,... | collective-permute-start | bytes 344072 | tf_op jit(solution)/shard_map/ppermute | solution.py:39
  212.3 7.0 %collective-permute-start.41 = (bf16[112,512]{1,0:T(8,128)(2,1)}, bf16[112,512]{1,0:T(8,128)(2,1)}, u32[]{:S(2)}, u32[]{:S(2)}) collective-permute-start(bf16[112,512]{1,0:T(8,128)(2,1)} %get-tuple-element.284), channel_id=1, source_target_pairs={{0,6},{6,0},{2,4},{4,2},{1,7},{7,1},{3,5},{5,3},{8,14},{14,8},{10,... | collective-permute-start | bytes 344072 | tf_op jit(solution)/shard_map/ppermute | solution.py:40
  217.7 4.1 %collective-permute-start.36 = (bf16[112,1024]{1,0:T(8,128)(2,1)S(1)}, bf16[112,1024]{1,0:T(8,128)(2,1)S(1)}, u32[]{:S(2)}, u32[]{:S(2)}) collective-permute-start(bf16[112,1024]{1,0:T(8,128)(2,1)S(1)} %get-tuple-element.183), channel_id=1, source_target_pairs={{0,1},{1,0},{2,3},{3,2},{4,5},{5,4},{6,7},{7,6},{8,9},{9,8},{10,11... | collective-permute-start | bytes 688136 | tf_op jit(solution)/shard_map/ppermute | solution.py:24
  220.4 6.1 %collective-permute-start.42 = (bf16[112,512]{1,0:T(8,128)(2,1)S(1)}, bf16[112,512]{1,0:T(8,128)(2,1)S(1)}, u32[]{:S(2)}, u32[]{:S(2)}) collective-permute-start(bf16[112,512]{1,0:T(8,128)(2,1)S(1)} %get-tuple-element.191.refs_1_), channel_id=1, source_target_pairs={{0,6},{6,0},{2,4},{4,2},{1,7},{7,1},{3,5},{5,3},{8,14},{14,8},{10,... | collective-permute-start | bytes 344072 | tf_op jit(solution)/shard_map/ppermute | solution.py:45
  221.8 5.7 %collective-permute-start.43 = (bf16[112,512]{1,0:T(8,128)(2,1)S(1)}, bf16[112,512]{1,0:T(8,128)(2,1)S(1)}, u32[]{:S(2)}, u32[]{:S(2)}) collective-permute-start(bf16[112,512]{1,0:T(8,128)(2,1)S(1)} %get-tuple-element.192.refs_3_), channel_id=1, source_target_pairs={{0,2},{2,0},{4,6},{6,4},{1,3},{3,1},{5,7},{7,5},{8,10},{10,8},{12,... | collective-permute-start | bytes 344072 | tf_op jit(solution)/shard_map/ppermute | solution.py:46
  221.9 11.8 %collective-permute-start.37 = (bf16[112,512]{1,0:T(8,128)(2,1)S(1)}, bf16[112,512]{1,0:T(8,128)(2,1)S(1)}, u32[]{:S(2)}, u32[]{:S(2)}) collective-permute-start(bf16[112,512]{1,0:T(8,128)(2,1)S(1)} %get-tuple-element.289), channel_id=1, source_target_pairs={{0,2},{2,0},{4,6},{6,4},{1,3},{3,1},{5,7},{7,5},{8,10},{10,8},{12,... | collective-permute-start | bytes 344072 | tf_op jit(solution)/shard_map/ppermute | solution.py:39
  224.0 9.8 %collective-permute-start.38 = (bf16[112,512]{1,0:T(8,128)(2,1)S(1)}, bf16[112,512]{1,0:T(8,128)(2,1)S(1)}, u32[]{:S(2)}, u32[]{:S(2)}) collective-permute-start(bf16[112,512]{1,0:T(8,128)(2,1)S(1)} %get-tuple-element.288), channel_id=1, source_target_pairs={{0,6},{6,0},{2,4},{4,2},{1,7},{7,1},{3,5},{5,3},{8,14},{14,8},{10,... | collective-permute-start | bytes 344072 | tf_op jit(solution)/shard_map/ppermute | solution.py:40
  233.8 54.0 %all-to-all-start.4 = ((bf16[16,880,128]{2,1,0:T(8,128)(2,1)}), bf16[16,880,128]{2,1,0:T(8,128)(2,1)}, u32[]{:S(2)}, u32[]{:S(2)}) async-start(bf16[16,880,128]{2,1,0:T(8,128)(2,1)} %copy-done.1), calls=%async_computation.4 | async-start | bytes 7208960 | tf_op jit(solution)/shard_map/all_to_all | solution.py:473
  241.2 6.0 %collective-permute-start.45 = (bf16[112,512]{1,0:T(8,128)(2,1)S(1)}, bf16[112,512]{1,0:T(8,128)(2,1)S(1)}, u32[]{:S(2)}, u32[]{:S(2)}) collective-permute-start(bf16[112,512]{1,0:T(8,128)(2,1)S(1)} %get-tuple-element.195.refs_0_), channel_id=1, source_target_pairs={{0,6},{6,0},{2,4},{4,2},{1,7},{7,1},{3,5},{5,3},{8,14},{14,8},{10,... | collective-permute-start | bytes 344072 | tf_op jit(solution)/shard_map/ppermute | solution.py:45
  243.1 4.8 %collective-permute-start.46 = (bf16[112,512]{1,0:T(8,128)(2,1)S(1)}, bf16[112,512]{1,0:T(8,128)(2,1)S(1)}, u32[]{:S(2)}, u32[]{:S(2)}) collective-permute-start(bf16[112,512]{1,0:T(8,128)(2,1)S(1)} %get-tuple-element.196.refs_2_), channel_id=1, source_target_pairs={{0,2},{2,0},{4,6},{6,4},{1,3},{3,1},{5,7},{7,5},{8,10},{10,8},{12,... | collective-permute-start | bytes 344072 | tf_op jit(solution)/shard_map/ppermute | solution.py:46
  255.5 5.3 %collective-permute-start.49 = (bf16[112,512]{1,0:T(8,128)(2,1)S(1)}, bf16[112,512]{1,0:T(8,128)(2,1)S(1)}, u32[]{:S(2)}, u32[]{:S(2)}) collective-permute-start(bf16[112,512]{1,0:T(8,128)(2,1)S(1)} %get-tuple-element.281), channel_id=1, source_target_pairs={{0,2},{2,0},{4,6},{6,4},{1,3},{3,1},{5,7},{7,5},{8,10},{10,8},{12,... | collective-permute-start | bytes 344072 | tf_op jit(solution)/shard_map/ppermute | solution.py:39
  255.6 6.5 %collective-permute-start.50 = (bf16[112,512]{1,0:T(8,128)(2,1)S(1)}, bf16[112,512]{1,0:T(8,128)(2,1)S(1)}, u32[]{:S(2)}, u32[]{:S(2)}) collective-permute-start(bf16[112,512]{1,0:T(8,128)(2,1)S(1)} %get-tuple-element.280), channel_id=1, source_target_pairs={{0,6},{6,0},{2,4},{4,2},{1,7},{7,1},{3,5},{5,3},{8,14},{14,8},{10,... | collective-permute-start | bytes 344072 | tf_op jit(solution)/shard_map/ppermute | solution.py:40
  262.1 6.1 %collective-permute-start.51 = (bf16[112,512]{1,0:T(8,128)(2,1)S(1)}, bf16[112,512]{1,0:T(8,128)(2,1)S(1)}, u32[]{:S(2)}, u32[]{:S(2)}) collective-permute-start(bf16[112,512]{1,0:T(8,128)(2,1)S(1)} %get-tuple-element.207.refs_1_), channel_id=1, source_target_pairs={{0,6},{6,0},{2,4},{4,2},{1,7},{7,1},{3,5},{5,3},{8,14},{14,8},{10,... | collective-permute-start | bytes 344072 | tf_op jit(solution)/shard_map/ppermute | solution.py:45
  263.6 4.8 %collective-permute-start.52 = (bf16[112,512]{1,0:T(8,128)(2,1)S(1)}, bf16[112,512]{1,0:T(8,128)(2,1)S(1)}, u32[]{:S(2)}, u32[]{:S(2)}) collective-permute-start(bf16[112,512]{1,0:T(8,128)(2,1)S(1)} %get-tuple-element.208.refs_3_), channel_id=1, source_target_pairs={{0,2},{2,0},{4,6},{6,4},{1,3},{3,1},{5,7},{7,5},{8,10},{10,8},{12,... | collective-permute-start | bytes 344072 | tf_op jit(solution)/shard_map/ppermute | solution.py:46
  287.8 30.0 %all-to-all-start.5 = ((bf16[16,400,128]{2,1,0:T(8,128)(2,1)}), bf16[16,400,128]{2,1,0:T(8,128)(2,1)S(1)}, u32[]{:S(2)}, u32[]{:S(2)}) async-start(bf16[16,400,128]{2,1,0:T(8,128)(2,1)} %copy-done), calls=%async_computation.5 | async-start | bytes 3276800 | tf_op jit(solution)/shard_map/all_to_all | solution.py:473
  (88 other events, 582.9 us)
where the time goes:
time: 325 us; the launch traced here: 321 us
  waiting for transfers between devices  124 us (38%)
  starting transfers between devices  93.2 us (29%)
  Pallas kernels  45.8 us (14%)
  local copies, waits for them, and re-layouts  38.8 us (12%)
  other arithmetic  16.7 us (5%)
    all_to_all x6, waiting for transfers between devices, exchange(): return lax.all_to_all(chunks, DP, 0, 0)  51.6 us
    all_to_all x6, starting transfers between devices, exchange(): return lax.all_to_all(chunks, DP, 0, 0)  43.1 us
    pallas_call x24, Pallas kernels, run(): pl.pallas_call(body, out_shape=list(outs), in_specs=specs, out_specs=[pl....  40.7 us
    unnamed x154, local copies, waits for them, and re-layouts  36.9 us
    ppermute x20, waiting for transfers between devices, core_swap(): return lax.ppermute(block, 'c', SWAP)  17.4 us
    ppermute x8, waiting for transfers between devices, total(): got_left = lax.ppermute(left, 'z', PAIR_B)  17 us
    ppermute x8, starting transfers between devices, total(): got_left = lax.ppermute(left, 'z', PAIR_B)  12.8 us
    ppermute x8, starting transfers between devices, total(): got_right = lax.ppermute(right, 'z', PAIR_B)  12 us
  transfers between devices with their start and end apart: 61, of which 45 were waited for; matrix products, arithmetic and copies ran while one was open for 5% of the time, Pallas kernels for 11%

commit v1 on v0

--- a/solution.py
+++ b/solution.py
@@ -31,28 +31,39 @@
 
 
 def total(mine, theirs, work=None, late=None):
-    mine = (mine + core_swap(theirs).astype(F32)).astype(BF)
+    parts = (shape(BF, HALF, WIDTH // 2),) * 2
+    left, right = run(add_cores, parts, (mine, core_swap(theirs)), 0)
     if work is not None:
-        mine, given = lax.optimization_barrier((mine, work[1]))
-    cut = mine.shape[1] // 2
-    left, right = mine[:, :cut], mine[:, cut:]
+        left, right, given = lax.optimization_barrier((left, right, work[1]))
     got_left = lax.ppermute(left, "z", PAIR_A)
     got_right = lax.ppermute(right, "z", PAIR_B)
     done = work[0](given) if work is not None else None
-    left = (left.astype(F32) + got_left.astype(F32)).astype(BF)
-    right = (right.astype(F32) + got_right.astype(F32)).astype(BF)
+    left, right = run(add_pairs, parts, (left, got_left, right, got_right), 0)
     left, right, late, done = lax.optimization_barrier((left, right, late, done))
     got_left = lax.ppermute(left, "z", PAIR_B)
     got_right = lax.ppermute(right, "z", PAIR_A)
     return (left, got_left, right, got_right), done, late
 
 
+def add_cores(mine, got, left, right):
+    both = (mine[...] + got[...].astype(F32)).astype(BF)
+    left[...] = both[:, : WIDTH // 2]
+    right[...] = both[:, WIDTH // 2 :]
+
+
+def add_pairs(left, got_left, right, got_right, left_out, right_out):
+    left_out[...] = (left[...].astype(F32) + got_left[...].astype(F32)).astype(BF)
+    right_out[...] = (right[...].astype(F32) + got_right[...].astype(F32)).astype(BF)
+
+
 HALF = 112
 ROWS = 2 * HALF
 WIDTH = 1024
 
 
-def run(kernel, outs, args, flops, scratch=(), smem=0, far=(), grant=16):
+def run(
+    kernel, outs, args, flops, scratch=(), smem=0, far=(), grant=16, mirrors=(), direct=False
+):
     far = [f if isinstance(f, tuple) else (f, None, None) for f in far]
     size = sum(a.size * a.dtype.itemsize for a in args)
     size += sum(o.size * o.dtype.itemsize for o in outs)
@@ -68,29 +79,66 @@
         sizes = args[i].shape
         sizes = sizes if count is None else (sizes[0], count) + sizes[2:]
         held.append(pltpu.VMEM(sizes, args[i].dtype))
+    more = [
+        shape(args[m[0]].dtype, ROWS, WIDTH) if isinstance(m, tuple) else outs[m] for m in mirrors
+    ]
+    semaphores = [pltpu.SemaphoreType.DMA((max(len(far), 1),))]
+    semaphores += [pltpu.SemaphoreType.DMA((max(2 * len(mirrors), 1),))]
 
     def body(*refs):
         refs = list(refs)
-        rest = refs[len(args) :]
-        if far:
-            spaces, sems = rest[-1 - len(far) : -1], rest[-1]
-            rest = rest[: -1 - len(far)]
-            copies = []
-            for k, (i, start, count) in enumerate(far):
-                source = refs[i] if count is None else refs[i].at[:, start : start + count]
-                copies.append(pltpu.make_async_copy(source, spaces[k], sems.at[k]))
-                copies[-1].start()
-            for k, copy in enumerate(copies):
+        n, m = len(args), len(outs)
+        results, copied = refs[n : n + m], refs[n + m : n + m + len(mirrors)]
+        rest = refs[n + m + len(mirrors) : -2]
+        sems, out_sems = refs[-2:]
+        spaces, rest = rest[len(rest) - len(far) :], rest[: len(rest) - len(far)]
+        copies = []
+        for k, (i, start, count) in enumerate(far):
+            source = refs[i] if count is None else refs[i].at[:, start : start + count]
+            copies.append(pltpu.make_async_copy(source, spaces[k], sems.at[k]))
+            copies[-1].start()
+        sent = {}
+
+        def send(k):
+            if isinstance(mirrors[k], tuple):
+                sent[k] = [
+                    pltpu.make_async_copy(
+                        refs[i], copied[k].at[HALF * j : HALF * j + HALF], out_sems.at[2 * k + j]
+                    )
+                    for j, i in enumerate(mirrors[k])
+                ]
+            else:
+                sent[k] = [
+                    pltpu.make_async_copy(results[mirrors[k]], copied[k], out_sems.at[2 * k])
+                ]
+            for copy in sent[k]:
+                copy.start()
+
+        for k, mirror in enumerate(mirrors):
+            if isinstance(mirror, tuple):
+                send(k)
+        for k, copy in enumerate(copies):
+            copy.wait()
+            refs[fetched[k]] = spaces[k]
+        if mirrors:
+            kernel(*refs[:n], *results, *rest, send=send)
+        else:
+            kernel(*refs[:n], *results, *rest)
+        for k in range(len(mirrors)):
+            if k not in sent:
+                send(k)
+        for group in sent.values():
+            for copy in group:
                 copy.wait()
-                refs[fetched[k]] = spaces[k]
-        kernel(*refs[: len(args)], *rest)
-
+
+    space = pltpu.HBM if direct else pltpu.VMEM
     return pl.pallas_call(
         body,
-        out_shape=list(outs),
+        out_shape=list(outs) + more,
         in_specs=specs,
-        out_specs=[pl.BlockSpec(memory_space=pltpu.VMEM)] * len(outs),
-        scratch_shapes=list(scratch) + held + ([pltpu.SemaphoreType.DMA((len(far),))] if far else []),
+        out_specs=[pl.BlockSpec(memory_space=space)] * len(outs)
+        + [pl.BlockSpec(memory_space=pltpu.HBM)] * len(more),
+        scratch_shapes=list(scratch) + held + semaphores,
         compiler_params=pltpu.CompilerParams(vmem_limit_bytes=grant * 2**20),
         cost_estimate=pl.CostEstimate(
             flops=int(flops), bytes_accessed=int(size), transcendentals=0
@@ -110,17 +158,11 @@
 
 def place_attention(w, w_qkv, w_out):
     for g in range(8):
-        rows = slice(128 * g, 128 * g + 128)
+        cols = slice(128 * g, 128 * g + 128)
         for i in range(2):
-            w_qkv[rows, 128 * i : 128 * i + 128] = w[2 * g + i, :128]
-            w_out[64 * i : 64 * i + 64, rows] = w[2 * g + i, 192:256]
-        first, second = w[2 * g, 128:192], w[2 * g + 1, 128:192]
-        w_qkv[128 * g : 128 * g + 64, 256:] = jnp.concatenate(
-            [first[:, :64], second[:, :64]], axis=1
-        )
-        w_qkv[128 * g + 64 : 128 * g + 128, 256:] = jnp.concatenate(
-            [first[:, 64:], second[:, 64:]], axis=1
-        )
+            w_qkv[128 * i : 128 * i + 128, cols] = w[2 * g + i, :128]
+            w_qkv[256 + 64 * i : 320 + 64 * i, cols] = w[2 * g + i, 128:192]
+            w_out[64 * i : 64 * i + 64, cols] = w[2 * g + i, 192:256]
 
 
 def place_mlp(w, w_up, w_down):
@@ -140,7 +182,7 @@
 def softmax(valid, query, key):
     scores = dot(query, key, 1, 1) * 64**-0.5
     at = lax.broadcasted_iota(jnp.int32, (1, ROWS), 1)
-    limit = jnp.where(at < HALF, valid[0], valid[1] + HALF)
+    limit = jnp.where(at < HALF, valid[4], valid[5] + HALF)
     scores = jnp.where(at < limit, scores, -1e30)
     exponent = jnp.exp(scores - jnp.max(scores, axis=-1, keepdims=True))
     return exponent / jnp.sum(exponent, axis=-1, keepdims=True)
@@ -151,9 +193,9 @@
     return packed[:, start : start + 64]
 
 
-def attention_forward(valid, mine, other, w, bias, packed_out, heads_out, out, away, w_qkv, w_out):
+def attention_forward(at, valid, mine, other, w, bias, packed_out, heads_out, out, away, w_qkv, w_out):
     place_attention(w, w_qkv, w_out)
-    packed = dot(both_rows(mine, other), w_qkv[...], 1, 0) + bias[...]
+    packed = dot(both_rows(mine, other), w_qkv[...], 1, 1) + bias[at, 0:1, :384]
     packed_out[...] = packed.astype(BF)
     heads = []
     for i in range(2):
@@ -187,26 +229,26 @@
     grad = jnp.concatenate(parts + values, axis=1).astype(BF)
     grad_out[...] = grad
     sums[...] = jnp.sum(grad.astype(F32), axis=0, keepdims=True)
-    result = dot(grad, w_qkv[...], 1, 1)
+    result = dot(grad, w_qkv[...], 1, 0)
     out[...] = result[:HALF]
     away[...] = result[HALF:].astype(BF)
 
 
-def attention_weights(h_mine, h_other, grad, heads, mine, other, rows_out):
-    qkv = dot(both_rows(h_mine, h_other), grad[...], 0, 0)
+def attention_weights(h_mine, h_other, grad, heads, mine, other, rows_out, send):
+    qkv = dot(grad[...], both_rows(h_mine, h_other), 0, 0).astype(BF)
     back = dot(heads[...], both_rows(mine, other), 0, 0).astype(BF)
     for g in range(8):
+        cols = slice(128 * g, 128 * g + 128)
         for i in range(2):
             at = 2 * g + i
-            rows_out[at, :128] = qkv[128 * g : 128 * g + 128, 128 * i : 128 * i + 128].astype(BF)
-            side = qkv[128 * g : 128 * g + 128, 256 + 64 * i : 320 + 64 * i]
-            rows_out[at, 128:192] = jnp.concatenate([side[:64], side[64:]], axis=1).astype(BF)
-            rows_out[at, 192:256] = back[64 * i : 64 * i + 64, 128 * g : 128 * g + 128]
-
-
-def mlp_forward(mine, other, w, bias, act_out, slope_out, out, away, w_up, w_down):
+            rows_out[at, :128] = qkv[128 * i : 128 * i + 128, cols]
+            rows_out[at, 128:192] = qkv[256 + 64 * i : 320 + 64 * i, cols]
+            rows_out[at, 192:256] = back[64 * i : 64 * i + 64, cols]
+
+
+def mlp_forward(at, mine, other, w, bias, act_out, slope_out, out, away, w_up, w_down):
     place_mlp(w, w_up, w_down)
-    upper = dot(both_rows(mine, other), w_up[...], 1, 0) + bias[...]
+    upper = dot(both_rows(mine, other), w_up[...], 1, 0) + bias[at, 1:2]
     phi = 0.5 * (1.0 + lax.erf(upper * 0.5**0.5))
     act = (upper * phi).astype(BF)
     act_out[...] = act
@@ -226,16 +268,15 @@
     away[...] = result[HALF:].astype(BF)
 
 
-def mixed_rows(place, h_mine, h_other, grad, act, mine, other, attention, keep, got, rows_out):
-    mlp_weights(h_mine, h_other, grad, act, mine, other, rows_out)
+def attention_weights_and_out(place, h_mine, h_other, grad, heads, mine, other, keep, got, rows_out, send):
+    attention_weights(h_mine, h_other, grad, heads, mine, other, rows_out, send)
     tokens = owner_rows(place[1] == 0, keep, got)
     for g in range(8):
         for i in range(2):
-            rows_out[2 * g + i, 512:768] = attention[2 * g + i]
-            rows_out[2 * g + i, 768:] = tokens[i]
-
-
-def mlp_weights(h_mine, h_other, grad, act, mine, other, rows_out):
+            rows_out[2 * g + i, 256:] = tokens[i]
+
+
+def mlp_weights(h_mine, h_other, grad, act, mine, other, rows_out, send):
     up = dot(both_rows(h_mine, h_other), grad[...], 0, 0).astype(BF)
     down = dot(act[...], both_rows(mine, other), 0, 0).astype(BF)
     for g in range(8):
@@ -264,7 +305,7 @@
             store(pl.ds(pl.multiple_of(512 * i + place, 128), 128), block, i)
 
 
-def norm_first(ring, a, b, c, d, stream_out, out, wide_out, cotangent, sums):
+def norm_first(ring, a, b, c, d, narrow, stream_out, out, wide_out, cotangent, sums, bias_out):
     def store(columns, block, i):
         stream_out[:, columns] = block[i, :HALF].astype(F32)
         for depth in range(2):
@@ -277,6 +318,22 @@
     ring_place(ring[0], (a, b, c, d), store)
     normed, _ = norm_parts(stream_out[...])
     out[...] = (normed * wide_out[0, 0:1] + wide_out[0, 1:2]).astype(BF)
+    pieces = []
+    for i in range(2):
+        piece = narrow[i].astype(F32)
+        pieces.append(piece[:8] + piece[8:])
+    blank = jnp.zeros((1, 64), F32)
+    for depth in range(2):
+        qv = [piece[depth : depth + 1] for piece in pieces]
+        bias_out[depth, 0:1] = jnp.concatenate(
+            [qv[0][:, :64], blank, qv[1][:, :64], blank, qv[0][:, 64:], qv[1][:, 64:]]
+            + [jnp.zeros((1, 128), F32)],
+            axis=1,
+        )
+        bias_out[depth, 1:2] = jnp.concatenate(
+            [piece[at : at + 1] for piece in pieces for at in (2 + 2 * depth, 3 + 2 * depth)],
+            axis=1,
+        )
 
 
 def owner_lanes(source, ring, first_core, keep, give):
@@ -312,7 +369,13 @@
     owner_lanes(new, place[0], place[1] == 0, keep, give)
 
 
-def prepare(offset, images, g1, b1, bo, g2, b2, bd, qv, up, w_qkv, w_out, out):
+def prepare(
+    counts, inputs, cotangent, g1, b1, bo, g2, b2, bd, qv, up, w_qkv, w_out, out, turned, held, block, sems
+):
+    group = lax.axis_index(("y", "xl"))
+    first = jnp.int32(0)
+    for g in range(8):
+        first = first + jnp.where(g < group, counts[g], 0)
     wide = [jnp.concatenate([v[0:1], v[1:2]], axis=1) for v in (g1, b1, bo, g2, b2, bd)]
     wide = jnp.concatenate(wide + [jnp.zeros((2, 128), F32)], axis=0)
     narrow = [qv[0], qv[1], up[0:1, :128], up[0:1, 128:], up[1:2, :128], up[1:2, 128:]]
@@ -321,26 +384,32 @@
     for v in (wide, narrow):
         high = v.astype(BF).astype(F32)
         rows += [high, v - high]
-    rows = jnp.concatenate(rows, axis=0).astype(BF)
-    side = w_qkv[0, :, 128:].astype(F32)
-    side = jnp.concatenate([side[:64], side[64:]], axis=1).astype(BF)
+    block[:32] = jnp.concatenate(rows, axis=0).astype(BF)
+    block[32:224] = w_qkv[0]
+    block[224:288] = w_out[0]
+    copies = [pltpu.make_async_copy(block, out.at[w, ROWS:512], sems.at[16 + w]) for w in range(16)]
+    for copy in copies:
+        copy.start()
+    seq = inputs.shape[2]
+    turned[...] = jnp.zeros(turned.shape, F32)
+    for s in range(3):
+        turned[:64, :seq] = inputs[s].astype(F32)
+        turned[64:, :seq] = cotangent[s].astype(F32)
+        held[s] = turned[...].T[:ROWS].astype(BF)
     for w in range(16):
-        out[w, :ROWS] = images[jnp.clip(w - offset[0], 0, 2)]
-        out[w, ROWS:256] = rows
-        out[w, 256:384] = w_qkv[0, :, :128]
-        out[w, 384:448] = side
-        out[w, 448:512] = w_out[0]
+        slot = jnp.clip(w - first, 0, 2)
+        copies.append(pltpu.make_async_copy(held.at[slot], out.at[w, 0:ROWS], sems.at[w]))
+        copies[-1].start()
+    for copy in copies:
+        copy.wait()
 
 
 def prepare_next(w_qkv, w_out, w_up, w_down, out):
-    side = w_qkv[1, :, 128:].astype(F32)
-    side = jnp.concatenate([side[:64], side[64:]], axis=1).astype(BF)
     for w in range(16):
         out[w, :128] = w_up[0, :, :128]
         out[w, 128:256] = w_up[0, :, 128:]
         out[w, 256:512] = w_down[0]
-        out[w, 512:640] = w_qkv[1, :, :128]
-        out[w, 640:704] = side
+        out[w, 512:704] = w_qkv[1]
         out[w, 704:768] = w_out[1]
 
 
@@ -418,14 +487,14 @@
 def collect(meta, received, out, held, sems):
     copies = []
     for s in range(3):
-        at = jnp.minimum(meta[0] + s, 15)
+        at = jnp.minimum(meta[2] + s, 15)
         copies.append(
-            pltpu.make_async_copy(received.at[at, 768:880], held.at[s], sems.at[s])
+            pltpu.make_async_copy(received.at[at, 256:368], held.at[s], sems.at[s])
         )
         copies[-1].start()
     for s in range(3):
         copies[s].wait()
-        out[s] = owner_tokens(held[s], s < meta[1])
+        out[s] = owner_tokens(held[s], s < meta[3])
 
 
 def finish(meta, received, sum_1, out, qkv, w_out, g1, b1, bo, g2, b2, bd, qv, up, weights, vectors, held, sems):
@@ -434,7 +503,7 @@
         pltpu.make_async_copy(received.at[:, 368:400], vectors, sems.at[4]),
     ]
     for s in range(3):
-        at = jnp.minimum(meta[0] + s, 15)
+        at = jnp.minimum(meta[2] + s, 15)
         copies.append(
             pltpu.make_async_copy(received.at[at, 256:368], held.at[s], sems.at[s])
         )
@@ -443,7 +512,7 @@
     for copy in copies:
         copy.wait()
     for s in range(3):
-        out[s] = owner_tokens(held[s], s < meta[1])
+        out[s] = owner_tokens(held[s], s < meta[3])
     total_v = jnp.sum(vectors[...].astype(F32), axis=0)
     wide = total_v[:16, :64] + total_v[:16, 64:]
     for v, ref in enumerate((g1, b1, bo, g2, b2, bd)):
@@ -454,14 +523,11 @@
         up[d : d + 1] = jnp.concatenate([narrow[2 + 2 * d : 3 + 2 * d], narrow[3 + 2 * d : 4 + 2 * d]], axis=1)
     for d in range(2):
         block = jnp.sum(weights[...].astype(F32), axis=0) if d == 0 else sum_1[...]
-        side = block[128:192]
-        qkv[d, :, :128] = block[:128]
-        qkv[d, :64, 128:] = side[:, :64]
-        qkv[d, 64:, 128:] = side[:, 64:]
+        qkv[d] = block[:192]
         w_out[d] = block[192:256]
 
 
-ATTENTION_SCRATCH = (pltpu.VMEM((WIDTH, 384), BF), pltpu.VMEM((128, WIDTH), BF))
+ATTENTION_SCRATCH = (pltpu.VMEM((384, WIDTH), BF), pltpu.VMEM((128, WIDTH), BF))
 MLP_SCRATCH = (pltpu.VMEM((WIDTH, 512), BF), pltpu.VMEM((512, WIDTH), BF))
 SUM_SHAPES = (shape(F32, HALF, WIDTH), shape(BF, HALF, WIDTH))
 NORM_SHAPES = (shape(F32, HALF, WIDTH), shape(BF, HALF, WIDTH))
@@ -503,33 +569,37 @@
     my_offset = jnp.sum(jnp.where(jnp.arange(8) < group, group_images, 0))
     my_live = jnp.sum(jnp.where(jnp.arange(8) == group, group_images, 0))
     source = jnp.sum((offsets <= worker).astype(jnp.int32)) - 1
-    valid = jnp.where(first_core, jnp.array([half, seq - half]), jnp.array([seq - half, half]))
-    valid = valid.astype(jnp.int32)
-
-    images = jnp.concatenate([inputs, cotangent], axis=-1)
-    images = jnp.pad(images, ((0, 0), (0, rows - seq), (0, 0)))
-    w_qkv = w_qkv.reshape(2, 128, 192)
+    mine_valid = jnp.where(first_core, half, seq - half)
+    place = jnp.stack([ring, core, my_offset, my_live, mine_valid, seq - mine_valid])
+    place = place.astype(jnp.int32)
+
+    w_qkv = w_qkv.transpose(0, 2, 3, 1).reshape(2, 192, 128)
     (chunks,) = run(
         prepare,
         (shape(BF, 16, 512, 128),),
-        (my_offset.reshape(1), images, ln1_gain, ln1_bias, b_out, ln2_gain, ln2_bias)
-        + (b_down, b_qv, b_up, w_qkv, w_out),
+        (group_images, inputs.transpose(0, 2, 1), cotangent.transpose(0, 2, 1))
+        + (ln1_gain, ln1_bias, b_out, ln2_gain, ln2_bias, b_down, b_qv, b_up, w_qkv, w_out),
         0,
+        (
+            pltpu.VMEM((128, 256), F32),
+            pltpu.VMEM((3, rows, 128), BF),
+            pltpu.VMEM((288, 128), BF),
+            pltpu.SemaphoreType.DMA((32,)),
+        ),
+        1,
+        range(1, 13),
+        56,
         (),
-        1,
-        range(2, 12),
-        56,
+        True,
     )
     arrived = exchange(chunks)
     (next_rows,) = run(
         prepare_next, (shape(BF, 16, 768, 128),), (w_qkv, w_out, w_up, w_down), 0
     )
     (mlp_rows_1,) = run(prepare_mlp, (shape(BF, 16, 512, 128),), (w_up, w_down), 0)
-    next_rows, mlp_rows_1, arrived = lax.optimization_barrier((next_rows, mlp_rows_1, arrived))
-    following = exchange(next_rows)
-    mlp_w = [following, None]
-    attention_w = [arrived, following]
-    attention_at = [256, 512]
+    next_rows, mlp_rows_1, arrived, place = lax.optimization_barrier(
+        (next_rows, mlp_rows_1, arrived, place)
+    )
 
     picked = lax.dynamic_slice(arrived, (2 * source, 0, 0), (2, rows, 128))
     vectors_here = arrived[:2, rows:256]
@@ -542,45 +612,35 @@
     part_1 = jnp.where(first_core, got, keep)
     left = jnp.concatenate([part_0[..., :64], part_1[..., :64]], axis=-1)
     right = jnp.concatenate([part_0[..., 64:], part_1[..., 64:]], axis=-1)
-    place = jnp.stack([ring, core]).astype(jnp.int32)
-    stream, h1, wide, cotangent_low, low_sum = run(
+    blocks = ring_blocks(jnp.concatenate([left, right[:, half:], right[:, :half]], axis=1))
+    following = exchange(next_rows)
+    mlp_w = [following, None]
+    attention_w = [arrived, following]
+    attention_at = [256, 512]
+    stream, h1, wide, cotangent_low, low_sum, bias = run(
         norm_first,
         NORM_SHAPES
-        + (shape(F32, 2, 8, WIDTH), shape(BF, half, WIDTH), shape(F32, 1, WIDTH)),
-        [place] + ring_blocks(jnp.concatenate([left, right[:, half:], right[:, :half]], axis=1)),
+        + (shape(F32, 2, 8, WIDTH), shape(BF, half, WIDTH), shape(F32, 1, WIDTH))
+        + (shape(F32, 2, 2, 512),),
+        [place] + blocks + [vectors_here[:, 16:]],
         0,
         (),
         1,
     )
-    narrow_all = vectors_here[:, 16:].astype(F32)
-    narrow_all = narrow_all[:, :8] + narrow_all[:, 8:]
-    bias_qv = [narrow_all[:, d] for d in range(2)]
-    bias_up = [narrow_all[:, 2 + 2 * d : 4 + 2 * d].reshape(512) for d in range(2)]
-
-    row = lambda v: v.reshape(1, -1)
-    bias_packed = [
-        jnp.concatenate(
-            [bias_qv[d][0, :64], jnp.zeros(64), bias_qv[d][1, :64], jnp.zeros(64)]
-            + [bias_qv[d][0, 64:], bias_qv[d][1, 64:]]
-        )[None]
-        for d in range(2)
-    ]
-
     kept = []
     for d in range(2):
         h1_other = core_swap(h1)
         packed, heads, mine, theirs = run(
-            attention_forward,
+            functools.partial(attention_forward, d),
             (shape(BF, ROWS, 384), shape(BF, ROWS, 128)) + SUM_SHAPES,
-            (valid, h1, h1_other, attention_w[d], bias_packed[d]),
+            (place, h1, h1_other, attention_w[d], bias),
             ATTENTION_FLOPS,
             ATTENTION_SCRATCH,
             1,
             ((3, attention_at[d], 256),),
         )
-        pairs, _, _ = total(mine, theirs)
-        if d == 1:
-            pairs, mlp_w[1] = lax.optimization_barrier((pairs, mlp_w[1]))
+        pairs, _, done = total(mine, theirs, None, mlp_w[1])
+        mlp_w[1] = done
         middle, h2 = run(
             functools.partial(norm_forward, ((d, 2), (d, 3), (d, 4))),
             NORM_SHAPES,
@@ -589,9 +649,9 @@
         )
         h2_other = core_swap(h2)
         act, slope, mine, theirs = run(
-            mlp_forward,
+            functools.partial(mlp_forward, d),
             (shape(BF, ROWS, 512), shape(F32, ROWS, 512)) + SUM_SHAPES,
-            (h2, h2_other, mlp_w[d], row(bias_up[d])),
+            (h2, h2_other, mlp_w[d], bias),
             MLP_FLOPS,
             MLP_SCRATCH,
             0,
@@ -600,7 +660,7 @@
         kept.append((stream, h1, h1_other, packed, heads, middle, h2, h2_other, act, slope))
         if d == 0:
             pairs, _, _ = total(mine, theirs)
-            mlp_rows_1, _ = lax.optimization_barrier((mlp_rows_1, following))
+            mlp_rows_1, _ = lax.optimization_barrier((mlp_rows_1, act))
             mlp_w[1] = exchange(mlp_rows_1)
             stream, h1 = run(
                 functools.partial(norm_forward, ((0, 5), (1, 0), (1, 1))),
@@ -628,7 +688,8 @@
         start, h1, h1_other, packed, heads, middle, h2, h2_other, act, slope = kept[d]
         if d == 0:
             low_other = core_swap(grad_low)
-            low_other, mlp_got = lax.optimization_barrier((low_other, previous))
+            attention_grad, _ = lax.optimization_barrier((attention_grad, mlp_got))
+            mixed = exchange(attention_grad)
         upper_grad, up_sum, mine, theirs = run(
             mlp_backward,
             (shape(BF, ROWS, 512), shape(F32, 1, 512)) + SUM_SHAPES,
@@ -636,26 +697,22 @@
             MLP_FLOPS,
             MLP_SCRATCH,
             0,
-            ((2, 0, 512), 3),
+            ((2, 0, 512),),
         )
 
         def mlp_work(upper_grad):
             args = (h2, h2_other, upper_grad, act, grad_low, low_other)
-            if d == 0:
-                return run(
-                    mixed_rows,
-                    (shape(BF, 16, 880, 128),),
-                    (place,) + args + (attention_grad, out_keep, out_got),
-                    MLP_FLOPS,
-                    (),
-                    1,
-                    (1, 2, 4),
-                )[0]
-            return run(mlp_weights, (shape(BF, 16, 512, 128),), args, MLP_FLOPS, (), 0, (0, 1, 3))[0]
+            return run(
+                mlp_weights,
+                (shape(BF, 16, 512, 128),),
+                args,
+                MLP_FLOPS,
+                mirrors=(0,),
+            )[1]
 
         pairs, mlp_grad, _ = total(mine, theirs, (mlp_work, upper_grad))
         if d == 0:
-            mlp_grad, mlp_got = lax.optimization_barrier((mlp_grad, mlp_got))
+            mlp_grad, mixed = lax.optimization_barrier((mlp_grad, mixed))
         previous = exchange(mlp_grad)
         grad_stream, grad_low, sums[2, d] = run(
             functools.partial(norm_backward, (d, 3)),
@@ -667,26 +724,38 @@
         packed_grad, packed_sum, mine, theirs = run(
             attention_backward,
             (shape(BF, ROWS, 384), shape(F32, 1, 384)) + SUM_SHAPES,
-            (valid, grad_low, low_other, packed, attention_w[d]),
+            (place, grad_low, low_other, packed, attention_w[d]),
             ATTENTION_FLOPS,
             ATTENTION_SCRATCH,
             1,
-            (3, (4, attention_at[d], 256)),
+            ((4, attention_at[d], 256),),
         )
         narrow_sums[d] = (packed_sum, up_sum)
 
         def attention_work(packed_grad):
+            args = (h1, h1_other, packed_grad, heads, grad_low, low_other)
+            if d == 1:
+                return run(
+                    attention_weights_and_out,
+                    (shape(BF, 16, 368, 128),),
+                    (place,) + args + (out_keep, out_got),
+                    ATTENTION_FLOPS,
+                    smem=1,
+                    mirrors=(0,),
+                )[1]
             return run(
                 attention_weights,
-                (shape(BF, 16, 256 if d == 1 else 400, 128),),
-                (h1, h1_other, packed_grad, heads, grad_low, low_other),
+                (shape(BF, 16, 400, 128),),
+                args,
                 ATTENTION_FLOPS,
-                (),
-                0,
-                (0, 1, 3),
-            )[0]
-
-        pairs, attention_grad, _ = total(mine, theirs, (attention_work, packed_grad))
+                mirrors=(0,),
+            )[1]
+
+        pairs, attention_grad, mlp_done = total(
+            mine, theirs, (attention_work, packed_grad), previous if d == 1 else None
+        )
+        if d == 1:
+            mlp_got = mlp_done
         if d == 1:
             grad_stream, grad_low, sums[1, d] = run(
                 functools.partial(norm_backward, (d, 0)),
@@ -710,7 +779,7 @@
         out_specs=[pl.BlockSpec(memory_space=pltpu.HBM)],
         scratch_shapes=[pltpu.VMEM((16, 144, 128), BF), pltpu.SemaphoreType.DMA(())],
         input_output_aliases={1: 0},
-        compiler_params=pltpu.CompilerParams(vmem_limit_bytes=16 * 2**20),
+        compiler_params=pltpu.CompilerParams(vmem_limit_bytes=56 * 2**20),
     )(
         place,
         attention_grad,
@@ -725,15 +794,14 @@
     )
     last_rows, previous = lax.optimization_barrier((last_rows, previous))
     last = exchange(last_rows)
-    mixed, _ = lax.optimization_barrier((previous, last_rows))
+    mixed, previous, mlp_got, _ = lax.optimization_barrier((mixed, previous, mlp_got, last_rows))
 
     def summed(block):
         return jnp.sum(block.astype(F32), axis=0)
 
-    mlp = [summed(mixed[:, :512]), summed(mlp_got)]
+    mlp = [summed(previous), summed(mlp_got)]
     grad_up = jnp.stack([jnp.concatenate([m[:128], m[128:256]], axis=-1) for m in mlp])
     grad_down = jnp.stack([m[256:] for m in mlp])
-    meta = jnp.stack([my_offset, my_live]).astype(jnp.int32)
     hbm, vmem = pl.BlockSpec(memory_space=pltpu.HBM), pl.BlockSpec(memory_space=pltpu.VMEM)
     smem = pl.BlockSpec(memory_space=pltpu.SMEM)
     (result,) = pl.pallas_call(
@@ -742,10 +810,10 @@
         in_specs=[smem, hbm],
         out_specs=[vmem],
         scratch_shapes=[pltpu.VMEM((3, half, 128), BF), pltpu.SemaphoreType.DMA((3,))],
-    )(meta, mixed)
+    )(place, mixed)
     grad_inputs, grad_qkv, grad_out, g1, b1, bo, g2, b2, bd, grad_qv, grad_b_up = pl.pallas_call(
         finish,
-        out_shape=[shape(F32, 3, 64, seq), shape(F32, 2, 128, 192), shape(F32, 2, 64, 128)]
+        out_shape=[shape(F32, 3, 64, seq), shape(F32, 2, 192, 128), shape(F32, 2, 64, 128)]
         + [shape(F32, 2, 64)] * 6
         + [shape(F32, 2, 128), shape(F32, 2, 256)],
         in_specs=[smem, hbm, vmem],
@@ -757,13 +825,13 @@
             pltpu.SemaphoreType.DMA((5,)),
         ],
         compiler_params=pltpu.CompilerParams(vmem_limit_bytes=16 * 2**20),
-    )(meta, last, summed(mixed[:, 512:768]))
+    )(place, last, summed(mixed[:, :256]))
     return (
         result.transpose(0, 2, 1),
         grad_inputs.transpose(0, 2, 1),
         g1,
         b1,
-        grad_qkv[:, :, None, :],
+        grad_qkv[:, None].transpose(0, 3, 1, 2),
         grad_qv[:, None, :],
         grad_out,
         bo,

time: 325 us -> 306 us (0.942)
  other arithmetic: 16.7 us -> 9.08 us
  starting transfers between devices: 93.2 us -> 89.1 us
    all_to_all x6 -> x7, waiting for transfers between devices: 51.6 us -> 36.4 us  [exchange(): return lax.all_to_all(chunks, DP, 0, 0)]
    ppermute x8, waiting for transfers between devices: 17 us -> 31.7 us  [total(): got_left = lax.ppermute(left, 'z', PAIR_B)]
    ppermute x8, starting transfers between devices: 9.56 us -> 0.1 us  [total(): got_right = lax.ppermute(right, 'z', PAIR_A)]
    ppermute x8, waiting for transfers between devices: 10.6 us -> 4.33 us  [total(): got_right = lax.ppermute(right, 'z', PAIR_A)]
    all_to_all x6 -> x7, starting transfers between devices: 43.1 us -> 49.1 us  [exchange(): return lax.all_to_all(chunks, DP, 0, 0)]
    convert_element_type x17 -> x0, other arithmetic: 4.25 us -> none  [the longest x8 2.05 us: total(): right = (right.astype(F32) + got_right.astype(F32)).astype(BF)]
    ppermute x20, waiting for transfers between devices: 17.4 us -> 20.7 us  [core_swap(): return lax.ppermute(block, 'c', SWAP)]
    pallas_call x24 -> x40, Pallas kernels: 40.7 us -> 38.5 us  [run(): pl.pallas_call(body, out_shape=list(outs) + more, in_specs=specs, out_spe...]
  transfers between devices with their start and end apart: 61 -> 62, of which waited for: 45 -> 49; matrix products, arithmetic and copies ran while one was open for 5% -> 4% of each run, Pallas kernels for 11% -> 11%
where the time goes in v1:
time: 306 us; the launch traced here: 305 us
  waiting for transfers between devices  121 us (40%)
  starting transfers between devices  89.1 us (29%)
  Pallas kernels  44.6 us (15%)
  local copies, waits for them, and re-layouts  38.4 us (13%)
  other arithmetic  9.08 us (3%)
    all_to_all x7, starting transfers between devices, exchange(): return lax.all_to_all(chunks, DP, 0, 0)  49.1 us
    pallas_call x40, Pallas kernels, run(): pl.pallas_call(body, out_shape=list(outs) + more, in_specs=specs, out_spe...  38.5 us
    all_to_all x7, waiting for transfers between devices, exchange(): return lax.all_to_all(chunks, DP, 0, 0)  36.4 us
    unnamed x160, local copies, waits for them, and re-layouts  36.1 us
    ppermute x8, waiting for transfers between devices, total(): got_left = lax.ppermute(left, 'z', PAIR_B)  31.7 us
    ppermute x20, waiting for transfers between devices, core_swap(): return lax.ppermute(block, 'c', SWAP)  20.7 us
    ppermute x8, starting transfers between devices, total(): got_right = lax.ppermute(right, 'z', PAIR_B)  13.6 us
    ppermute x8, starting transfers between devices, total(): got_left = lax.ppermute(left, 'z', PAIR_B)  13.4 us
  transfers between devices with their start and end apart: 62, of which 49 were waited for; matrix products, arithmetic and copies ran while one was open for 4% of the time, Pallas kernels for 11%

profile of v1, /device:TPU:4, one launch (start us, length us, event | category | flops | bytes accessed | tf_op | source)
XLA Modules:
  0.0 304.6 jit_solution(1275233800921646297)
XLA Ops:
  0.6 3.7 %shard_map.256 = bf16[16,512,128]{2,1,0:T(8,128)(2,1)} custom-call(s32[8]{0:T(128)} %refs_0_.3, bf16[3,64,197]{2,1,0:T(8,128)(2,1)} %bitcast.34, bf16[3,64,197]{2,1,0:T(8,128)(2,1)} %bitcast.35, f32[2,64]{1,0:T(2,128)} %refs_3_.3, f32[2,64]{1,0:T(2,128)} %refs_4_.1, f32[2,64]{1,0:T(2,128)} %refs_5_.1, f32[2,64]{1,0:T(2,128)} %refs_6_.1, f32[2,64]{1,0:T(2,128)} %refs_7_.1, ...), custom_call_target="tpu_custom_call" | custom-call | bytes 2385696 | tf_op jit(solution)/shard_map/pallas_call | solution.py:135
  4.4 7.6 %all-to-all-start = ((bf16[16,512,128]{2,1,0:T(8,128)(2,1)}), bf16[16,512,128]{2,1,0:T(8,128)(2,1)}, u32[]{:S(2)}, u32[]{:S(2)}) async-start(bf16[16,512,128]{2,1,0:T(8,128)(2,1)} %shard_map.256), calls=%async_computation | async-start | bytes 4194304 | tf_op jit(solution)/shard_map/all_to_all | solution.py:539
  17.8 22.4 %all-to-all-done.refs_3_.refs_4_ = bf16[16,512,128]{2,1,0:T(8,128)(2,1)} async-done(((bf16[16,512,128]{2,1,0:T(8,128)(2,1)}), bf16[16,512,128]{2,1,0:T(8,128)(2,1)}, u32[]{:S(2)}, u32[]{:S(2)}) %all-to-all-start) | async-done | bytes 2097184 | tf_op jit(solution)/shard_map/all_to_all | solution.py:539
  40.2 5.4 %all-to-all-start.1 = ((bf16[16,768,128]{2,1,0:T(8,128)(2,1)}), bf16[16,768,128]{2,1,0:T(8,128)(2,1)S(1)}, u32[]{:S(2)}, u32[]{:S(2)}) async-start(bf16[16,768,128]{2,1,0:T(8,128)(2,1)} %copy-done), calls=%async_computation.1 | async-start | bytes 6291456 | tf_op jit(solution)/shard_map/all_to_all | solution.py:539
  50.2 4.0 %collective-permute-start.3 = (bf16[2,256,128]{2,1,0:T(8,128)(2,1)S(1)}, bf16[2,256,128]{2,1,0:T(8,128)(2,1)S(1)}, u32[]{:S(2)}, u32[]{:S(2)}) collective-permute-start(bf16[2,256,128]{2,1,0:T(8,128)(2,1)S(1)} %fusion.5.refs_1_), channel_id=1, source_target_pairs={{0,4},{2,6},{4,0},{6,2},{1,5},{3,7},{5,1},{7,3},{8,12},{10,14},{12... | collective-permute-start | bytes 393224 | tf_op jit(solution)/shard_map/ppermute | solution.py:29
  56.2 2.0 collective-permute-done.3.refs_4_
  58.2 3.4 %collective-permute-done.2.refs_3_ = bf16[2,256,128]{2,1,0:T(8,128)(2,1)S(1)} collective-permute-done((bf16[2,256,128]{2,1,0:T(8,128)(2,1)S(1)}, bf16[2,256,128]{2,1,0:T(8,128)(2,1)S(1)}, u32[]{:S(2)}, u32[]{:S(2)}) %collective-permute-start.2) | collective-permute-done | bytes 131104 | tf_op jit(solution)/shard_map/ppermute | solution.py:29
  64.5 3.2 %shard_map.258 = (bf16[224,384]{1,0:T(8,128)(2,1)S(1)}, bf16[224,128]{1,0:T(8,128)(2,1)S(1)}, f32[112,1024]{1,0:T(8,128)S(1)}, bf16[112,1024]{1,0:T(8,128)(2,1)S(1)}) custom-call(s32[6]{0:T(128)S(1)} %stack.45.refs_0_.place.meta, bf16[112,1024]{1,0:T(8,128)(2,1)S(1)} %get-tuple-element.164.refs_1_.refs_0_, ...), custom_call_target="tpu_custom_call" | custom-call | flops 234881024 | bytes 3481624 | tf_op jit(solution)/shard_map/pallas_call | solution.py:135
  70.4 2.1 collective-permute-start.8
  72.5 2.2 collective-permute-done.7.refs_1_
  74.7 1.9 collective-permute-done.8.refs_3_
  76.6 2.1 collective-permute-start.9
  78.8 3.9 %collective-permute-done.9.refs_1_ = bf16[112,512]{1,0:T(8,128)(2,1)S(1)} collective-permute-done((bf16[112,512]{1,0:T(8,128)(2,1)S(1)}, bf16[112,512]{1,0:T(8,128)(2,1)S(1)}, u32[]{:S(2)}, u32[]{:S(2)}) %collective-permute-start.9) | collective-permute-done | bytes 114720 | tf_op jit(solution)/shard_map/ppermute | solution.py:43
  92.9 7.2 %all-to-all-start.2 = ((bf16[16,512,128]{2,1,0:T(8,128)(2,1)}), bf16[16,512,128]{2,1,0:T(8,128)(2,1)}, u32[]{:S(2)}, u32[]{:S(2)}) async-start(bf16[16,512,128]{2,1,0:T(8,128)(2,1)} %copy-done.1), calls=%async_computation.2 | async-start | bytes 4194304 | tf_op jit(solution)/shard_map/all_to_all | solution.py:539
  104.5 3.7 %collective-permute-done.13.refs_1_ = bf16[112,512]{1,0:T(8,128)(2,1)S(1)} collective-permute-done((bf16[112,512]{1,0:T(8,128)(2,1)S(1)}, bf16[112,512]{1,0:T(8,128)(2,1)S(1)}, u32[]{:S(2)}, u32[]{:S(2)}) %collective-permute-start.13) | collective-permute-done | bytes 114720 | tf_op jit(solution)/shard_map/ppermute | solution.py:38
  110.9 4.8 %collective-permute-done.15.refs_1_ = bf16[112,512]{1,0:T(8,128)(2,1)S(1)} collective-permute-done((bf16[112,512]{1,0:T(8,128)(2,1)S(1)}, bf16[112,512]{1,0:T(8,128)(2,1)S(1)}, u32[]{:S(2)}, u32[]{:S(2)}) %collective-permute-start.15) | collective-permute-done | bytes 114720 | tf_op jit(solution)/shard_map/ppermute | solution.py:43
  119.3 2.0 shard_map.266
  124.5 2.1 collective-permute-start.20
  126.6 3.1 %collective-permute-done.19.refs_1_ = bf16[112,512]{1,0:T(8,128)(2,1)S(1)} collective-permute-done((bf16[112,512]{1,0:T(8,128)(2,1)S(1)}, bf16[112,512]{1,0:T(8,128)(2,1)S(1)}, u32[]{:S(2)}, u32[]{:S(2)}) %collective-permute-start.19) | collective-permute-done | bytes 114720 | tf_op jit(solution)/shard_map/ppermute | solution.py:38
  132.3 2.0 collective-permute-start.21
  134.3 4.2 %collective-permute-done.21.refs_1_ = bf16[112,512]{1,0:T(8,128)(2,1)S(1)} collective-permute-done((bf16[112,512]{1,0:T(8,128)(2,1)}, bf16[112,512]{1,0:T(8,128)(2,1)S(1)}, u32[]{:S(2)}, u32[]{:S(2)}) %collective-permute-start.21) | collective-permute-done | bytes 114720 | tf_op jit(solution)/shard_map/ppermute | solution.py:43
  144.7 2.6 shard_map.270
  148.1 2.6 shard_map.271
  153.8 2.3 shard_map.274
  159.7 7.2 %all-to-all-start.3 = ((bf16[16,512,128]{2,1,0:T(8,128)(2,1)}), bf16[16,512,128]{2,1,0:T(8,128)(2,1)}, u32[]{:S(2)}, u32[]{:S(2)}) async-start(bf16[16,512,128]{2,1,0:T(8,128)(2,1)} %copy-done.4), calls=%async_computation.3 | async-start | bytes 4194304 | tf_op jit(solution)/shard_map/all_to_all | solution.py:539
  168.2 4.7 %collective-permute-done.27.refs_1_ = bf16[112,512]{1,0:T(8,128)(2,1)S(1)} collective-permute-done((bf16[112,512]{1,0:T(8,128)(2,1)S(1)}, bf16[112,512]{1,0:T(8,128)(2,1)S(1)}, u32[]{:S(2)}, u32[]{:S(2)}) %collective-permute-start.27) | collective-permute-done | bytes 114720 | tf_op jit(solution)/shard_map/ppermute | solution.py:43
  180.3 2.5 shard_map.276
  183.3 2.0 collective-permute-start.35
  185.4 3.3 %collective-permute-done.34.refs_1_ = bf16[112,512]{1,0:T(8,128)(2,1)S(1)} collective-permute-done((bf16[112,512]{1,0:T(8,128)(2,1)S(1)}, bf16[112,512]{1,0:T(8,128)(2,1)S(1)}, u32[]{:S(2)}, u32[]{:S(2)}) %collective-permute-start.34) | collective-permute-done | bytes 114720 | tf_op jit(solution)/shard_map/ppermute | solution.py:38
  190.1 2.1 collective-permute-start.36
  192.2 2.1 collective-permute-start.31
  199.8 2.5 shard_map.282
  203.6 7.3 %all-to-all-start.4 = ((bf16[16,368,128]{2,1,0:T(8,128)(2,1)}), bf16[16,368,128]{2,1,0:T(8,128)(2,1)}, u32[]{:S(2)}, u32[]{:S(2)}) async-start(bf16[16,368,128]{2,1,0:T(8,128)(2,1)} %copy-done.16), calls=%async_computation.4 | async-start | bytes 3014656 | tf_op jit(solution)/shard_map/all_to_all | solution.py:539
  212.1 4.7 %collective-permute-done.39.refs_1_ = bf16[112,512]{1,0:T(8,128)(2,1)S(1)} collective-permute-done((bf16[112,512]{1,0:T(8,128)(2,1)S(1)}, bf16[112,512]{1,0:T(8,128)(2,1)S(1)}, u32[]{:S(2)}, u32[]{:S(2)}) %collective-permute-start.39) | collective-permute-done | bytes 114720 | tf_op jit(solution)/shard_map/ppermute | solution.py:43
  225.6 2.0 collective-permute-start.44
  227.6 2.3 shard_map.287
  232.4 7.2 %all-to-all-start.5 = ((bf16[16,512,128]{2,1,0:T(8,128)(2,1)}), bf16[16,512,128]{2,1,0:T(8,128)(2,1)}, u32[]{:S(2)}, u32[]{:S(2)}) async-start(bf16[16,512,128]{2,1,0:T(8,128)(2,1)} %copy-done.3), calls=%async_computation.5 | async-start | bytes 4194304 | tf_op jit(solution)/shard_map/all_to_all | solution.py:539
  239.6 2.0 collective-permute-start.45
  241.5 4.0 %collective-permute-done.45.refs_1_ = bf16[112,512]{1,0:T(8,128)(2,1)S(1)} collective-permute-done((bf16[112,512]{1,0:T(8,128)(2,1)S(1)}, bf16[112,512]{1,0:T(8,128)(2,1)S(1)}, u32[]{:S(2)}, u32[]{:S(2)}) %collective-permute-start.45) | collective-permute-done | bytes 114720 | tf_op jit(solution)/shard_map/ppermute | solution.py:43
  248.4 3.6 %shard_map.289 = (bf16[224,384]{1,0:T(8,128)(2,1)S(1)}, f32[1,384]{1,0:T(1,128)S(1)}, f32[112,1024]{1,0:T(8,128)S(1)}, bf16[112,1024]{1,0:T(8,128)(2,1)S(1)}) custom-call(s32[6]{0:T(128)S(1)} %copy-done.57, bf16[112,1024]{1,0:T(8,128)(2,1)S(1)} %get-tuple-element.261.refs_1_.refs_4_, bf16[112,1024]{1,0:T(8,128)(2,1)S(1)} %collective-permute-done.47.refs_2_.refs_5_, ...), custom_call_target="tpu_custom_call" | custom-call | flops 234881024 | bytes 3589656 | tf_op jit(solution)/shard_map/pallas_call | solution.py:135
  255.2 1.9 shard_map.292
  261.8 4.7 %collective-permute-done.51.refs_2_ = bf16[112,512]{1,0:T(8,128)(2,1)S(1)} collective-permute-done((bf16[112,512]{1,0:T(8,128)(2,1)S(1)}, bf16[112,512]{1,0:T(8,128)(2,1)S(1)}, u32[]{:S(2)}, u32[]{:S(2)}) %collective-permute-start.51) | collective-permute-done | bytes 114720 | tf_op jit(solution)/shard_map/ppermute | solution.py:43
  272.1 7.2 %all-to-all-start.6 = ((bf16[16,400,128]{2,1,0:T(8,128)(2,1)}), bf16[16,400,128]{2,1,0:T(8,128)(2,1)S(1)}, u32[]{:S(2)}, u32[]{:S(2)}) async-start(bf16[16,400,128]{2,1,0:T(8,128)(2,1)} %shard_map.294), calls=%async_computation.6 | async-start | bytes 3276800 | tf_op jit(solution)/shard_map/all_to_all | solution.py:539
  279.3 1.9 convert_reduce_fusion.1
  281.2 2.6 shard_map.295
  283.8 1.9 convert_reduce_fusion
  288.7 13.9 %all-to-all-done.6.received = bf16[16,400,128]{2,1,0:T(8,128)(2,1)S(1)} async-done(((bf16[16,400,128]{2,1,0:T(8,128)(2,1)}), bf16[16,400,128]{2,1,0:T(8,128)(2,1)S(1)}, u32[]{:S(2)}, u32[]{:S(2)}) %all-to-all-start.6) | async-done | bytes 1638432 | tf_op jit(solution)/shard_map/all_to_all | solution.py:539
  302.6 1.8 shard_map.296
  (300 shorter events, 106.2 us)
Async XLA Ops:
  4.4 35.8 %all-to-all-start = ((bf16[16,512,128]{2,1,0:T(8,128)(2,1)}), bf16[16,512,128]{2,1,0:T(8,128)(2,1)}, u32[]{:S(2)}, u32[]{:S(2)}) async-start(bf16[16,512,128]{2,1,0:T(8,128)(2,1)} %shard_map.256), calls=%async_computation | async-start | bytes 4194304 | tf_op jit(solution)/shard_map/all_to_all | solution.py:539
  40.2 46.7 %all-to-all-start.1 = ((bf16[16,768,128]{2,1,0:T(8,128)(2,1)}), bf16[16,768,128]{2,1,0:T(8,128)(2,1)S(1)}, u32[]{:S(2)}, u32[]{:S(2)}) async-start(bf16[16,768,128]{2,1,0:T(8,128)(2,1)} %copy-done), calls=%async_computation.1 | async-start | bytes 6291456 | tf_op jit(solution)/shard_map/all_to_all | solution.py:539
  50.2 8.0 %collective-permute-start.3 = (bf16[2,256,128]{2,1,0:T(8,128)(2,1)S(1)}, bf16[2,256,128]{2,1,0:T(8,128)(2,1)S(1)}, u32[]{:S(2)}, u32[]{:S(2)}) collective-permute-start(bf16[2,256,128]{2,1,0:T(8,128)(2,1)S(1)} %fusion.5.refs_1_), channel_id=1, source_target_pairs={{0,4},{2,6},{4,0},{6,2},{1,5},{3,7},{5,1},{7,3},{8,12},{10,14},{12... | collective-permute-start | bytes 393224 | tf_op jit(solution)/shard_map/ppermute | solution.py:29
  54.1 7.4 %collective-permute-start.2 = (bf16[2,256,128]{2,1,0:T(8,128)(2,1)S(1)}, bf16[2,256,128]{2,1,0:T(8,128)(2,1)S(1)}, u32[]{:S(2)}, u32[]{:S(2)}) collective-permute-start(bf16[2,256,128]{2,1,0:T(8,128)(2,1)S(1)} %fusion.5.refs_1_), channel_id=1, source_target_pairs={{0,6},{2,0},{4,2},{6,4},{1,7},{3,1},{5,3},{7,5},{8,14},{10,8},{12,... | collective-permute-start | bytes 393224 | tf_op jit(solution)/shard_map/ppermute | solution.py:29
  54.8 6.7 %collective-permute-start.1 = (bf16[2,256,128]{2,1,0:T(8,128)(2,1)S(1)}, bf16[2,256,128]{2,1,0:T(8,128)(2,1)S(1)}, u32[]{:S(2)}, u32[]{:S(2)}) collective-permute-start(bf16[2,256,128]{2,1,0:T(8,128)(2,1)S(1)} %fusion.5.refs_1_), channel_id=1, source_target_pairs={{0,2},{2,4},{4,6},{6,0},{1,3},{3,5},{5,7},{7,1},{8,10},{10,12},{12... | collective-permute-start | bytes 393224 | tf_op jit(solution)/shard_map/ppermute | solution.py:29
  67.8 1.6 collective-permute-start.6
  69.4 5.3 %collective-permute-start.7 = (bf16[112,512]{1,0:T(8,128)(2,1)S(1)}, bf16[112,512]{1,0:T(8,128)(2,1)S(1)}, u32[]{:S(2)}, u32[]{:S(2)}) collective-permute-start(bf16[112,512]{1,0:T(8,128)(2,1)S(1)} %get-tuple-element.168.refs_0_), channel_id=1, source_target_pairs={{0,2},{2,0},{4,6},{6,4},{1,3},{3,1},{5,7},{7,5},{8,10},{10,8},{12,... | collective-permute-start | bytes 344072 | tf_op jit(solution)/shard_map/ppermute | solution.py:38
  70.4 6.1 %collective-permute-start.8 = (bf16[112,512]{1,0:T(8,128)(2,1)S(1)}, bf16[112,512]{1,0:T(8,128)(2,1)S(1)}, u32[]{:S(2)}, u32[]{:S(2)}) collective-permute-start(bf16[112,512]{1,0:T(8,128)(2,1)S(1)} %get-tuple-element.169.refs_2_), channel_id=1, source_target_pairs={{0,6},{6,0},{2,4},{4,2},{1,7},{7,1},{3,5},{5,3},{8,14},{14,8},{10,... | collective-permute-start | bytes 344072 | tf_op jit(solution)/shard_map/ppermute | solution.py:39
  76.6 6.1 %collective-permute-start.9 = (bf16[112,512]{1,0:T(8,128)(2,1)S(1)}, bf16[112,512]{1,0:T(8,128)(2,1)S(1)}, u32[]{:S(2)}, u32[]{:S(2)}) collective-permute-start(bf16[112,512]{1,0:T(8,128)(2,1)S(1)} %get-tuple-element.170.refs_0_), channel_id=1, source_target_pairs={{0,6},{6,0},{2,4},{4,2},{1,7},{7,1},{3,5},{5,3},{8,14},{14,8},{10,... | collective-permute-start | bytes 344072 | tf_op jit(solution)/shard_map/ppermute | solution.py:43
  78.8 4.8 %collective-permute-start.10 = (bf16[112,512]{1,0:T(8,128)(2,1)S(1)}, bf16[112,512]{1,0:T(8,128)(2,1)S(1)}, u32[]{:S(2)}, u32[]{:S(2)}) collective-permute-start(bf16[112,512]{1,0:T(8,128)(2,1)S(1)} %get-tuple-element.171.refs_2_), channel_id=1, source_target_pairs={{0,2},{2,0},{4,6},{6,4},{1,3},{3,1},{5,7},{7,5},{8,10},{10,8},{12,... | collective-permute-start | bytes 344072 | tf_op jit(solution)/shard_map/ppermute | solution.py:44
  92.9 39.4 %all-to-all-start.2 = ((bf16[16,512,128]{2,1,0:T(8,128)(2,1)}), bf16[16,512,128]{2,1,0:T(8,128)(2,1)}, u32[]{:S(2)}, u32[]{:S(2)}) async-start(bf16[16,512,128]{2,1,0:T(8,128)(2,1)} %copy-done.1), calls=%async_computation.2 | async-start | bytes 4194304 | tf_op jit(solution)/shard_map/all_to_all | solution.py:539
  100.1 1.7 collective-permute-start.12
  102.9 5.3 %collective-permute-start.13 = (bf16[112,512]{1,0:T(8,128)(2,1)S(1)}, bf16[112,512]{1,0:T(8,128)(2,1)S(1)}, u32[]{:S(2)}, u32[]{:S(2)}) collective-permute-start(bf16[112,512]{1,0:T(8,128)(2,1)S(1)} %get-tuple-element.178.refs_0_), channel_id=1, source_target_pairs={{0,2},{2,0},{4,6},{6,4},{1,3},{3,1},{5,7},{7,5},{8,10},{10,8},{12,... | collective-permute-start | bytes 344072 | tf_op jit(solution)/shard_map/ppermute | solution.py:38
  103.0 6.5 %collective-permute-start.14 = (bf16[112,512]{1,0:T(8,128)(2,1)S(1)}, bf16[112,512]{1,0:T(8,128)(2,1)S(1)}, u32[]{:S(2)}, u32[]{:S(2)}) collective-permute-start(bf16[112,512]{1,0:T(8,128)(2,1)S(1)} %get-tuple-element.179.refs_2_), channel_id=1, source_target_pairs={{0,6},{6,0},{2,4},{4,2},{1,7},{7,1},{3,5},{5,3},{8,14},{14,8},{10,... | collective-permute-start | bytes 344072 | tf_op jit(solution)/shard_map/ppermute | solution.py:39
  109.6 6.1 %collective-permute-start.15 = (bf16[112,512]{1,0:T(8,128)(2,1)S(1)}, bf16[112,512]{1,0:T(8,128)(2,1)S(1)}, u32[]{:S(2)}, u32[]{:S(2)}) collective-permute-start(bf16[112,512]{1,0:T(8,128)(2,1)S(1)} %get-tuple-element.180.refs_0_), channel_id=1, source_target_pairs={{0,6},{6,0},{2,4},{4,2},{1,7},{7,1},{3,5},{5,3},{8,14},{14,8},{10,... | collective-permute-start | bytes 344072 | tf_op jit(solution)/shard_map/ppermute | solution.py:43
  110.9 4.8 %collective-permute-start.16 = (bf16[112,512]{1,0:T(8,128)(2,1)S(1)}, bf16[112,512]{1,0:T(8,128)(2,1)S(1)}, u32[]{:S(2)}, u32[]{:S(2)}) collective-permute-start(bf16[112,512]{1,0:T(8,128)(2,1)S(1)} %get-tuple-element.181.refs_2_), channel_id=1, source_target_pairs={{0,2},{2,0},{4,6},{6,4},{1,3},{3,1},{5,7},{7,5},{8,10},{10,8},{12,... | collective-permute-start | bytes 344072 | tf_op jit(solution)/shard_map/ppermute | solution.py:44
  124.2 5.4 %collective-permute-start.19 = (bf16[112,512]{1,0:T(8,128)(2,1)S(1)}, bf16[112,512]{1,0:T(8,128)(2,1)S(1)}, u32[]{:S(2)}, u32[]{:S(2)}) collective-permute-start(bf16[112,512]{1,0:T(8,128)(2,1)S(1)} %get-tuple-element.186.refs_0_), channel_id=1, source_target_pairs={{0,2},{2,0},{4,6},{6,4},{1,3},{3,1},{5,7},{7,5},{8,10},{10,8},{12,... | collective-permute-start | bytes 344072 | tf_op jit(solution)/shard_map/ppermute | solution.py:38
  124.5 6.5 %collective-permute-start.20 = (bf16[112,512]{1,0:T(8,128)(2,1)S(1)}, bf16[112,512]{1,0:T(8,128)(2,1)S(1)}, u32[]{:S(2)}, u32[]{:S(2)}) collective-permute-start(bf16[112,512]{1,0:T(8,128)(2,1)S(1)} %get-tuple-element.187.refs_2_), channel_id=1, source_target_pairs={{0,6},{6,0},{2,4},{4,2},{1,7},{7,1},{3,5},{5,3},{8,14},{14,8},{10,... | collective-permute-start | bytes 344072 | tf_op jit(solution)/shard_map/ppermute | solution.py:39
  132.3 6.2 %collective-permute-start.21 = (bf16[112,512]{1,0:T(8,128)(2,1)}, bf16[112,512]{1,0:T(8,128)(2,1)S(1)}, u32[]{:S(2)}, u32[]{:S(2)}) collective-permute-start(bf16[112,512]{1,0:T(8,128)(2,1)} %copy-done.51), channel_id=1, source_target_pairs={{0,6},{6,0},{2,4},{4,2},{1,7},{7,1},{3,5},{5,3},{8,14},{14,8},{10,... | collective-permute-start | bytes 344072 | tf_op jit(solution)/shard_map/ppermute | solution.py:43
  134.3 5.0 %collective-permute-start.22 = (bf16[112,512]{1,0:T(8,128)(2,1)}, bf16[112,512]{1,0:T(8,128)(2,1)S(1)}, u32[]{:S(2)}, u32[]{:S(2)}) collective-permute-start(bf16[112,512]{1,0:T(8,128)(2,1)} %copy-done.53), channel_id=1, source_target_pairs={{0,2},{2,0},{4,6},{6,4},{1,3},{3,1},{5,7},{7,5},{8,10},{10,8},{12,... | collective-permute-start | bytes 344072 | tf_op jit(solution)/shard_map/ppermute | solution.py:44
  143.2 4.9 %collective-permute-start.4 = (bf16[112,1024]{1,0:T(8,128)(2,1)S(1)}, bf16[112,1024]{1,0:T(8,128)(2,1)S(1)}, u32[]{:S(2)}, u32[]{:S(2)}) collective-permute-start(bf16[112,1024]{1,0:T(8,128)(2,1)S(1)} %get-tuple-element.163.refs_0_.refs_4_.refs_5_), channel_id=1, source_target_pairs={{0,1},{1,0},{2,3},{3,2},{4,5},{5,4},{6,7},{7,6},{8,9},{9,8},{10,11... | collective-permute-start | bytes 688136 | tf_op jit(solution)/shard_map/ppermute | solution.py:24
  152.4 5.3 %collective-permute-start.25 = (bf16[112,512]{1,0:T(8,128)(2,1)S(1)}, bf16[112,512]{1,0:T(8,128)(2,1)S(1)}, u32[]{:S(2)}, u32[]{:S(2)}) collective-permute-start(bf16[112,512]{1,0:T(8,128)(2,1)S(1)} %get-tuple-element.204.refs_0_), channel_id=1, source_target_pairs={{0,2},{2,0},{4,6},{6,4},{1,3},{3,1},{5,7},{7,5},{8,10},{10,8},{12,... | collective-permute-start | bytes 344072 | tf_op jit(solution)/shard_map/ppermute | solution.py:38
  152.5 6.5 %collective-permute-start.26 = (bf16[112,512]{1,0:T(8,128)(2,1)S(1)}, bf16[112,512]{1,0:T(8,128)(2,1)S(1)}, u32[]{:S(2)}, u32[]{:S(2)}) collective-permute-start(bf16[112,512]{1,0:T(8,128)(2,1)S(1)} %get-tuple-element.205.refs_2_), channel_id=1, source_target_pairs={{0,6},{6,0},{2,4},{4,2},{1,7},{7,1},{3,5},{5,3},{8,14},{14,8},{10,... | collective-permute-start | bytes 344072 | tf_op jit(solution)/shard_map/ppermute | solution.py:39
  159.7 43.9 %all-to-all-start.3 = ((bf16[16,512,128]{2,1,0:T(8,128)(2,1)}), bf16[16,512,128]{2,1,0:T(8,128)(2,1)}, u32[]{:S(2)}, u32[]{:S(2)}) async-start(bf16[16,512,128]{2,1,0:T(8,128)(2,1)} %copy-done.4), calls=%async_computation.3 | async-start | bytes 4194304 | tf_op jit(solution)/shard_map/all_to_all | solution.py:539
  166.9 6.0 %collective-permute-start.27 = (bf16[112,512]{1,0:T(8,128)(2,1)S(1)}, bf16[112,512]{1,0:T(8,128)(2,1)S(1)}, u32[]{:S(2)}, u32[]{:S(2)}) collective-permute-start(bf16[112,512]{1,0:T(8,128)(2,1)S(1)} %get-tuple-element.211.refs_0_), channel_id=1, source_target_pairs={{0,6},{6,0},{2,4},{4,2},{1,7},{7,1},{3,5},{5,3},{8,14},{14,8},{10,... | collective-permute-start | bytes 344072 | tf_op jit(solution)/shard_map/ppermute | solution.py:43
  168.1 5.0 %collective-permute-start.28 = (bf16[112,512]{1,0:T(8,128)(2,1)}, bf16[112,512]{1,0:T(8,128)(2,1)S(1)}, u32[]{:S(2)}, u32[]{:S(2)}) collective-permute-start(bf16[112,512]{1,0:T(8,128)(2,1)} %copy-done.49), channel_id=1, source_target_pairs={{0,2},{2,0},{4,6},{6,4},{1,3},{3,1},{5,7},{7,5},{8,10},{10,8},{12,... | collective-permute-start | bytes 344072 | tf_op jit(solution)/shard_map/ppermute | solution.py:44
  177.0 1.8 collective-permute-start.29
  177.0 6.1 %collective-permute-start.33 = (bf16[112,1024]{1,0:T(8,128)(2,1)}, bf16[112,1024]{1,0:T(8,128)(2,1)S(1)}, u32[]{:S(2)}, u32[]{:S(2)}) collective-permute-start(bf16[112,1024]{1,0:T(8,128)(2,1)} %copy-done.75), channel_id=1, source_target_pairs={{0,1},{1,0},{2,3},{3,2},{4,5},{5,4},{6,7},{7,6},{8,9},{9,8},{10,11... | collective-permute-start | bytes 688136 | tf_op jit(solution)/shard_map/ppermute | solution.py:24
  182.9 9.3 %collective-permute-start.30 = (bf16[112,1024]{1,0:T(8,128)(2,1)S(1)}, bf16[112,1024]{1,0:T(8,128)(2,1)S(1)}, u32[]{:S(2)}, u32[]{:S(2)}) collective-permute-start(bf16[112,1024]{1,0:T(8,128)(2,1)S(1)} %get-tuple-element.217), channel_id=1, source_target_pairs={{0,1},{1,0},{2,3},{3,2},{4,5},{5,4},{6,7},{7,6},{8,9},{9,8},{10,11... | collective-permute-start | bytes 688136 | tf_op jit(solution)/shard_map/ppermute | solution.py:24
  183.2 5.5 %collective-permute-start.34 = (bf16[112,512]{1,0:T(8,128)(2,1)S(1)}, bf16[112,512]{1,0:T(8,128)(2,1)S(1)}, u32[]{:S(2)}, u32[]{:S(2)}) collective-permute-start(bf16[112,512]{1,0:T(8,128)(2,1)S(1)} %get-tuple-element.230.refs_0_), channel_id=1, source_target_pairs={{0,2},{2,0},{4,6},{6,4},{1,3},{3,1},{5,7},{7,5},{8,10},{10,8},{12,... | collective-permute-start | bytes 344072 | tf_op jit(solution)/shard_map/ppermute | solution.py:38
  183.3 6.6 %collective-permute-start.35 = (bf16[112,512]{1,0:T(8,128)(2,1)S(1)}, bf16[112,512]{1,0:T(8,128)(2,1)S(1)}, u32[]{:S(2)}, u32[]{:S(2)}) collective-permute-start(bf16[112,512]{1,0:T(8,128)(2,1)S(1)} %get-tuple-element.231.refs_2_), channel_id=1, source_target_pairs={{0,6},{6,0},{2,4},{4,2},{1,7},{7,1},{3,5},{5,3},{8,14},{14,8},{10,... | collective-permute-start | bytes 344072 | tf_op jit(solution)/shard_map/ppermute | solution.py:39
  190.1 6.1 %collective-permute-start.36 = (bf16[112,512]{1,0:T(8,128)(2,1)S(1)}, bf16[112,512]{1,0:T(8,128)(2,1)S(1)}, u32[]{:S(2)}, u32[]{:S(2)}) collective-permute-start(bf16[112,512]{1,0:T(8,128)(2,1)S(1)} %get-tuple-element.232.refs_1_), channel_id=1, source_target_pairs={{0,6},{6,0},{2,4},{4,2},{1,7},{7,1},{3,5},{5,3},{8,14},{14,8},{10,... | collective-permute-start | bytes 344072 | tf_op jit(solution)/shard_map/ppermute | solution.py:43
  192.2 5.5 %collective-permute-start.37 = (bf16[112,512]{1,0:T(8,128)(2,1)S(1)}, bf16[112,512]{1,0:T(8,128)(2,1)S(1)}, u32[]{:S(2)}, u32[]{:S(2)}) collective-permute-start(bf16[112,512]{1,0:T(8,128)(2,1)S(1)} %get-tuple-element.233.refs_3_), channel_id=1, source_target_pairs={{0,2},{2,0},{4,6},{6,4},{1,3},{3,1},{5,7},{7,5},{8,10},{10,8},{12,... | collective-permute-start | bytes 344072 | tf_op jit(solution)/shard_map/ppermute | solution.py:44
  192.2 11.2 %collective-permute-start.31 = (bf16[112,512]{1,0:T(8,128)(2,1)S(1)}, bf16[112,512]{1,0:T(8,128)(2,1)S(1)}, u32[]{:S(2)}, u32[]{:S(2)}) collective-permute-start(bf16[112,512]{1,0:T(8,128)(2,1)S(1)} %get-tuple-element.221.refs_0_), channel_id=1, source_target_pairs={{0,2},{2,0},{4,6},{6,4},{1,3},{3,1},{5,7},{7,5},{8,10},{10,8},{12,... | collective-permute-start | bytes 344072 | tf_op jit(solution)/shard_map/ppermute | solution.py:38
  194.3 9.1 %collective-permute-start.32 = (bf16[112,512]{1,0:T(8,128)(2,1)S(1)}, bf16[112,512]{1,0:T(8,128)(2,1)S(1)}, u32[]{:S(2)}, u32[]{:S(2)}) collective-permute-start(bf16[112,512]{1,0:T(8,128)(2,1)S(1)} %get-tuple-element.222.refs_2_), channel_id=1, source_target_pairs={{0,6},{6,0},{2,4},{4,2},{1,7},{7,1},{3,5},{5,3},{8,14},{14,8},{10,... | collective-permute-start | bytes 344072 | tf_op jit(solution)/shard_map/ppermute | solution.py:39
  203.6 28.8 %all-to-all-start.4 = ((bf16[16,368,128]{2,1,0:T(8,128)(2,1)}), bf16[16,368,128]{2,1,0:T(8,128)(2,1)}, u32[]{:S(2)}, u32[]{:S(2)}) async-start(bf16[16,368,128]{2,1,0:T(8,128)(2,1)} %copy-done.16), calls=%async_computation.4 | async-start | bytes 3014656 | tf_op jit(solution)/shard_map/all_to_all | solution.py:539
  210.8 6.0 %collective-permute-start.39 = (bf16[112,512]{1,0:T(8,128)(2,1)S(1)}, bf16[112,512]{1,0:T(8,128)(2,1)S(1)}, u32[]{:S(2)}, u32[]{:S(2)}) collective-permute-start(bf16[112,512]{1,0:T(8,128)(2,1)S(1)} %get-tuple-element.237.refs_0_), channel_id=1, source_target_pairs={{0,6},{6,0},{2,4},{4,2},{1,7},{7,1},{3,5},{5,3},{8,14},{14,8},{10,... | collective-permute-start | bytes 344072 | tf_op jit(solution)/shard_map/ppermute | solution.py:43
  212.1 4.8 %collective-permute-start.40 = (bf16[112,512]{1,0:T(8,128)(2,1)S(1)}, bf16[112,512]{1,0:T(8,128)(2,1)S(1)}, u32[]{:S(2)}, u32[]{:S(2)}) collective-permute-start(bf16[112,512]{1,0:T(8,128)(2,1)S(1)} %get-tuple-element.238.refs_2_), channel_id=1, source_target_pairs={{0,2},{2,0},{4,6},{6,4},{1,3},{3,1},{5,7},{7,5},{8,10},{10,8},{12,... | collective-permute-start | bytes 344072 | tf_op jit(solution)/shard_map/ppermute | solution.py:44
  225.5 5.7 %collective-permute-start.43 = (bf16[112,512]{1,0:T(8,128)(2,1)S(1)}, bf16[112,512]{1,0:T(8,128)(2,1)S(1)}, u32[]{:S(2)}, u32[]{:S(2)}) collective-permute-start(bf16[112,512]{1,0:T(8,128)(2,1)S(1)} %get-tuple-element.247.refs_0_), channel_id=1, source_target_pairs={{0,2},{2,0},{4,6},{6,4},{1,3},{3,1},{5,7},{7,5},{8,10},{10,8},{12,... | collective-permute-start | bytes 344072 | tf_op jit(solution)/shard_map/ppermute | solution.py:38
  225.6 6.5 %collective-permute-start.44 = (bf16[112,512]{1,0:T(8,128)(2,1)S(1)}, bf16[112,512]{1,0:T(8,128)(2,1)S(1)}, u32[]{:S(2)}, u32[]{:S(2)}) collective-permute-start(bf16[112,512]{1,0:T(8,128)(2,1)S(1)} %get-tuple-element.248.refs_2_), channel_id=1, source_target_pairs={{0,6},{6,0},{2,4},{4,2},{1,7},{7,1},{3,5},{5,3},{8,14},{14,8},{10,... | collective-permute-start | bytes 344072 | tf_op jit(solution)/shard_map/ppermute | solution.py:39
  232.4 39.7 %all-to-all-start.5 = ((bf16[16,512,128]{2,1,0:T(8,128)(2,1)}), bf16[16,512,128]{2,1,0:T(8,128)(2,1)}, u32[]{:S(2)}, u32[]{:S(2)}) async-start(bf16[16,512,128]{2,1,0:T(8,128)(2,1)} %copy-done.3), calls=%async_computation.5 | async-start | bytes 4194304 | tf_op jit(solution)/shard_map/all_to_all | solution.py:539
  239.6 6.0 %collective-permute-start.45 = (bf16[112,512]{1,0:T(8,128)(2,1)S(1)}, bf16[112,512]{1,0:T(8,128)(2,1)S(1)}, u32[]{:S(2)}, u32[]{:S(2)}) collective-permute-start(bf16[112,512]{1,0:T(8,128)(2,1)S(1)} %get-tuple-element.258.refs_0_), channel_id=1, source_target_pairs={{0,6},{6,0},{2,4},{4,2},{1,7},{7,1},{3,5},{5,3},{8,14},{14,8},{10,... | collective-permute-start | bytes 344072 | tf_op jit(solution)/shard_map/ppermute | solution.py:43
  241.5 4.8 %collective-permute-start.46 = (bf16[112,512]{1,0:T(8,128)(2,1)S(1)}, bf16[112,512]{1,0:T(8,128)(2,1)S(1)}, u32[]{:S(2)}, u32[]{:S(2)}) collective-permute-start(bf16[112,512]{1,0:T(8,128)(2,1)S(1)} %get-tuple-element.259.refs_2_), channel_id=1, source_target_pairs={{0,2},{2,0},{4,6},{6,4},{1,3},{3,1},{5,7},{7,5},{8,10},{10,8},{12,... | collective-permute-start | bytes 344072 | tf_op jit(solution)/shard_map/ppermute | solution.py:44
  253.7 5.3 %collective-permute-start.49 = (bf16[112,512]{1,0:T(8,128)(2,1)S(1)}, bf16[112,512]{1,0:T(8,128)(2,1)S(1)}, u32[]{:S(2)}, u32[]{:S(2)}) collective-permute-start(bf16[112,512]{1,0:T(8,128)(2,1)S(1)} %get-tuple-element.268.refs_0_), channel_id=1, source_target_pairs={{0,2},{2,0},{4,6},{6,4},{1,3},{3,1},{5,7},{7,5},{8,10},{10,8},{12,... | collective-permute-start | bytes 344072 | tf_op jit(solution)/shard_map/ppermute | solution.py:38
  253.8 6.5 %collective-permute-start.50 = (bf16[112,512]{1,0:T(8,128)(2,1)S(1)}, bf16[112,512]{1,0:T(8,128)(2,1)S(1)}, u32[]{:S(2)}, u32[]{:S(2)}) collective-permute-start(bf16[112,512]{1,0:T(8,128)(2,1)S(1)} %get-tuple-element.269.refs_2_), channel_id=1, source_target_pairs={{0,6},{6,0},{2,4},{4,2},{1,7},{7,1},{3,5},{5,3},{8,14},{14,8},{10,... | collective-permute-start | bytes 344072 | tf_op jit(solution)/shard_map/ppermute | solution.py:39
  260.4 6.1 %collective-permute-start.51 = (bf16[112,512]{1,0:T(8,128)(2,1)S(1)}, bf16[112,512]{1,0:T(8,128)(2,1)S(1)}, u32[]{:S(2)}, u32[]{:S(2)}) collective-permute-start(bf16[112,512]{1,0:T(8,128)(2,1)S(1)} %get-tuple-element.276.refs_1_), channel_id=1, source_target_pairs={{0,6},{6,0},{2,4},{4,2},{1,7},{7,1},{3,5},{5,3},{8,14},{14,8},{10,... | collective-permute-start | bytes 344072 | tf_op jit(solution)/shard_map/ppermute | solution.py:43
  261.8 4.8 %collective-permute-start.52 = (bf16[112,512]{1,0:T(8,128)(2,1)S(1)}, bf16[112,512]{1,0:T(8,128)(2,1)S(1)}, u32[]{:S(2)}, u32[]{:S(2)}) collective-permute-start(bf16[112,512]{1,0:T(8,128)(2,1)S(1)} %get-tuple-element.277.refs_3_), channel_id=1, source_target_pairs={{0,2},{2,0},{4,6},{6,4},{1,3},{3,1},{5,7},{7,5},{8,10},{10,8},{12,... | collective-permute-start | bytes 344072 | tf_op jit(solution)/shard_map/ppermute | solution.py:44
  272.1 30.5 %all-to-all-start.6 = ((bf16[16,400,128]{2,1,0:T(8,128)(2,1)}), bf16[16,400,128]{2,1,0:T(8,128)(2,1)S(1)}, u32[]{:S(2)}, u32[]{:S(2)}) async-start(bf16[16,400,128]{2,1,0:T(8,128)(2,1)} %shard_map.294), calls=%async_computation.6 | async-start | bytes 3276800 | tf_op jit(solution)/shard_map/all_to_all | solution.py:539
  (94 other events, 587.4 us)

commit v2 on v1

--- a/solution.py
+++ b/solution.py
@@ -31,7 +31,7 @@
 
 
 def total(mine, theirs, work=None, late=None):
-    parts = (shape(BF, HALF, WIDTH // 2),) * 2
+    parts = (shape(BF, HALF, mine.shape[1] // 2),) * 2
     left, right = run(add_cores, parts, (mine, core_swap(theirs)), 0)
     if work is not None:
         left, right, given = lax.optimization_barrier((left, right, work[1]))
@@ -47,8 +47,9 @@
 
 def add_cores(mine, got, left, right):
     both = (mine[...] + got[...].astype(F32)).astype(BF)
-    left[...] = both[:, : WIDTH // 2]
-    right[...] = both[:, WIDTH // 2 :]
+    cut = mine.shape[1] // 2
+    left[...] = both[:, :cut]
+    right[...] = both[:, cut:]
 
 
 def add_pairs(left, got_left, right, got_right, left_out, right_out):
@@ -268,6 +269,16 @@
     away[...] = result[HALF:].astype(BF)
 
 
+def mlp_backward_and_out(
+    mine, other, w, slope, f_mine, f_theirs, grad_out, sums, out, away, w_up, w_down
+):
+    mlp_backward(
+        mine, other, w, slope, grad_out, sums, out.at[:, :WIDTH], away.at[:, :WIDTH], w_up, w_down
+    )
+    out[:, WIDTH:] = f_mine[...]
+    away[:, WIDTH:] = f_theirs[...]
+
+
 def attention_weights_and_out(place, h_mine, h_other, grad, heads, mine, other, keep, got, rows_out, send):
     attention_weights(h_mine, h_other, grad, heads, mine, other, rows_out, send)
     tokens = owner_rows(place[1] == 0, keep, got)
@@ -364,8 +375,8 @@
     return jnp.where(live, tokens.T[:, :197], 0.0)
 
 
-def norm_last(place, left, got_left, right, got_right, stream, wide, keep, give, new):
-    new[...] = stream[...] + (pair_sum(left, got_left, right, got_right) + wide[1, 5:6])
+def norm_last(place, part, got, stream, wide, keep, give, new):
+    new[...] = stream[...] + (part[...].astype(F32) + got[...].astype(F32) + wide[1, 5:6])
     owner_lanes(new, place[0], place[1] == 0, keep, give)
 
 
@@ -430,6 +441,15 @@
 
 def norm_backward(at, left, got_left, right, got_right, stream, upstream, wide, grad_out, low_out, sums):
     grad = pair_sum(left, got_left, right, got_right)
+    norm_backward_of(grad, at, stream, upstream, wide, grad_out, low_out, sums)
+
+
+def norm_backward_single(at, part, got, stream, upstream, wide, grad_out, low_out, sums):
+    grad = part[...].astype(F32) + got[...].astype(F32)
+    norm_backward_of(grad, at, stream, upstream, wide, grad_out, low_out, sums)
+
+
+def norm_backward_of(grad, at, stream, upstream, wide, grad_out, low_out, sums):
     normed, factor = norm_parts(stream[...])
     scaled = grad * wide[at[0], at[1] : at[1] + 1]
     first = jnp.mean(scaled, axis=-1, keepdims=True)
@@ -647,6 +667,9 @@
             pairs + (stream, wide),
             0,
         )
+        if d == 0:
+            mlp_rows_1, _, h2 = lax.optimization_barrier((mlp_rows_1, following, h2))
+            mlp_w[1] = exchange(mlp_rows_1)
         h2_other = core_swap(h2)
         act, slope, mine, theirs = run(
             functools.partial(mlp_forward, d),
@@ -660,8 +683,6 @@
         kept.append((stream, h1, h1_other, packed, heads, middle, h2, h2_other, act, slope))
         if d == 0:
             pairs, _, _ = total(mine, theirs)
-            mlp_rows_1, _ = lax.optimization_barrier((mlp_rows_1, act))
-            mlp_w[1] = exchange(mlp_rows_1)
             stream, h1 = run(
                 functools.partial(norm_forward, ((0, 5), (1, 0), (1, 1))),
                 NORM_SHAPES,
@@ -670,17 +691,6 @@
             )
     grad_low = cotangent_low
     low_other = core_swap(grad_low)
-    pairs, _, _ = total(mine, theirs)
-    keep, give = run(
-        norm_last,
-        (shape(BF, half, 128), shape(BF, half, 128)),
-        (place,) + pairs + (middle, wide),
-        0,
-        (pltpu.VMEM((half, WIDTH), F32),),
-        1,
-    )
-    out_keep, out_got = keep, core_swap(give)
-
     grad_stream = cotangent_low
     previous = mlp_got = None
     sums, narrow_sums = {}, {}
@@ -690,10 +700,13 @@
             low_other = core_swap(grad_low)
             attention_grad, _ = lax.optimization_barrier((attention_grad, mlp_got))
             mixed = exchange(attention_grad)
+        extra = (mine, theirs) if d == 1 else ()
+        both = WIDTH * 2 if d == 1 else WIDTH
         upper_grad, up_sum, mine, theirs = run(
-            mlp_backward,
-            (shape(BF, ROWS, 512), shape(F32, 1, 512)) + SUM_SHAPES,
-            (grad_low, low_other, mlp_w[d], slope),
+            mlp_backward_and_out if d == 1 else mlp_backward,
+            (shape(BF, ROWS, 512), shape(F32, 1, 512))
+            + (shape(F32, HALF, both), shape(BF, HALF, both)),
+            (grad_low, low_other, mlp_w[d], slope) + extra,
             MLP_FLOPS,
             MLP_SCRATCH,
             0,
@@ -714,8 +727,22 @@
         if d == 0:
             mlp_grad, mixed = lax.optimization_barrier((mlp_grad, mixed))
         previous = exchange(mlp_grad)
+        step = norm_backward
+        if d == 1:
+            pairs = lax.optimization_barrier(pairs)
+            keep, give = run(
+                norm_last,
+                (shape(BF, half, 128), shape(BF, half, 128)),
+                (place,) + pairs[2:] + (middle, wide),
+                0,
+                (pltpu.VMEM((half, WIDTH), F32),),
+                1,
+            )
+            keep, give, pairs = lax.optimization_barrier((keep, give, pairs))
+            out_keep, out_got = keep, core_swap(give)
+            step, pairs = norm_backward_single, pairs[:2]
         grad_stream, grad_low, sums[2, d] = run(
-            functools.partial(norm_backward, (d, 3)),
+            functools.partial(step, (d, 3)),
             NORM_SHAPES + (shape(F32, 8, WIDTH),),
             pairs + (middle, grad_stream, wide),
             0,

time: 306 us -> 296 us (0.967)
  local copies, waits for them, and re-layouts: 38.4 us -> 32.4 us
  starting transfers between devices: 89.1 us -> 85.4 us
    unnamed x160 -> x136, local copies, waits for them, and re-layouts: 36.1 us -> 30.2 us
    ppermute x8 -> x7, waiting for transfers between devices: 13.1 us -> 9.96 us  [total(): got_left = lax.ppermute(left, 'z', PAIR_A)]
    ppermute x20 -> x19, waiting for transfers between devices: 20.7 us -> 23.2 us  [core_swap(): return lax.ppermute(block, 'c', SWAP)]
    ppermute x8 -> x7, waiting for transfers between devices: 31.7 us -> 30.4 us  [total(): got_left = lax.ppermute(left, 'z', PAIR_B)]
    ppermute x8 -> x7, starting transfers between devices: 13.6 us -> 12.6 us  [total(): got_right = lax.ppermute(right, 'z', PAIR_B)]
    ppermute x8 -> x7, waiting for transfers between devices: 9.24 us -> 8.83 us  [total(): got_right = lax.ppermute(right, 'z', PAIR_B)]
    pallas_call x40 -> x38, Pallas kernels: 38.5 us -> 38.3 us  [run(): pl.pallas_call(body, out_shape=list(outs) + more, in_specs=specs, out_spe...]
    ppermute x8 -> x7, starting transfers between devices: 13.4 us -> 13.3 us  [total(): got_left = lax.ppermute(left, 'z', PAIR_B)]
  transfers between devices with their start and end apart: 62 -> 57, of which waited for: 49 -> 47; matrix products, arithmetic and copies ran while one was open for 4% -> 4% of each run, Pallas kernels for 11% -> 12%
where the time goes in v2:
time: 296 us; the launch traced here: 294 us
  waiting for transfers between devices  120 us (41%)
  starting transfers between devices  85.4 us (29%)
  Pallas kernels  44.5 us (15%)
  local copies, waits for them, and re-layouts  32.4 us (11%)
  other arithmetic  9.08 us (3%)
    all_to_all x7, starting transfers between devices, exchange(): return lax.all_to_all(chunks, DP, 0, 0)  47.3 us
    pallas_call x38, Pallas kernels, run(): pl.pallas_call(body, out_shape=list(outs) + more, in_specs=specs, out_spe...  38.3 us
    all_to_all x7, waiting for transfers between devices, exchange(): return lax.all_to_all(chunks, DP, 0, 0)  38.3 us
    ppermute x7, waiting for transfers between devices, total(): got_left = lax.ppermute(left, 'z', PAIR_B)  30.4 us
    unnamed x136, local copies, waits for them, and re-layouts  30.2 us
    ppermute x19, waiting for transfers between devices, core_swap(): return lax.ppermute(block, 'c', SWAP)  23.2 us
    ppermute x7, starting transfers between devices, total(): got_left = lax.ppermute(left, 'z', PAIR_B)  13.3 us
    ppermute x7, starting transfers between devices, total(): got_right = lax.ppermute(right, 'z', PAIR_B)  12.6 us
  transfers between devices with their start and end apart: 57, of which 47 were waited for; matrix products, arithmetic and copies ran while one was open for 4% of the time, Pallas kernels for 12%

profile of v2, /device:TPU:4, one launch (start us, length us, event | category | flops | bytes accessed | tf_op | source)
XLA Modules:
  0.0 294.2 jit_solution(4243965440557112596)
XLA Ops:
  0.6 3.6 %shard_map.256 = bf16[16,512,128]{2,1,0:T(8,128)(2,1)} custom-call(s32[8]{0:T(128)} %refs_0_.3, bf16[3,64,197]{2,1,0:T(8,128)(2,1)} %bitcast.34, bf16[3,64,197]{2,1,0:T(8,128)(2,1)} %bitcast.35, f32[2,64]{1,0:T(2,128)} %refs_3_.3, f32[2,64]{1,0:T(2,128)} %refs_4_.1, f32[2,64]{1,0:T(2,128)} %refs_5_.1, f32[2,64]{1,0:T(2,128)} %refs_6_.1, f32[2,64]{1,0:T(2,128)} %refs_7_.1, ...), custom_call_target="tpu_custom_call" | custom-call | bytes 2385696 | tf_op jit(solution)/shard_map/pallas_call | solution.py:136
  4.3 7.6 %all-to-all-start = ((bf16[16,512,128]{2,1,0:T(8,128)(2,1)}), bf16[16,512,128]{2,1,0:T(8,128)(2,1)}, u32[]{:S(2)}, u32[]{:S(2)}) async-start(bf16[16,512,128]{2,1,0:T(8,128)(2,1)} %shard_map.256), calls=%async_computation | async-start | bytes 4194304 | tf_op jit(solution)/shard_map/all_to_all | solution.py:559
  17.8 22.4 %all-to-all-done.refs_3_.refs_4_ = bf16[16,512,128]{2,1,0:T(8,128)(2,1)} async-done(((bf16[16,512,128]{2,1,0:T(8,128)(2,1)}), bf16[16,512,128]{2,1,0:T(8,128)(2,1)}, u32[]{:S(2)}, u32[]{:S(2)}) %all-to-all-start) | async-done | bytes 2097184 | tf_op jit(solution)/shard_map/all_to_all | solution.py:559
  40.1 5.4 %all-to-all-start.1 = ((bf16[16,768,128]{2,1,0:T(8,128)(2,1)}), bf16[16,768,128]{2,1,0:T(8,128)(2,1)S(1)}, u32[]{:S(2)}, u32[]{:S(2)}) async-start(bf16[16,768,128]{2,1,0:T(8,128)(2,1)} %copy-done), calls=%async_computation.1 | async-start | bytes 6291456 | tf_op jit(solution)/shard_map/all_to_all | solution.py:559
  50.1 4.0 %collective-permute-start.3 = (bf16[2,256,128]{2,1,0:T(8,128)(2,1)S(1)}, bf16[2,256,128]{2,1,0:T(8,128)(2,1)S(1)}, u32[]{:S(2)}, u32[]{:S(2)}) collective-permute-start(bf16[2,256,128]{2,1,0:T(8,128)(2,1)S(1)} %fusion.5.refs_1_), channel_id=1, source_target_pairs={{0,4},{2,6},{4,0},{6,2},{1,5},{3,7},{5,1},{7,3},{8,12},{10,14},{12... | collective-permute-start | bytes 393224 | tf_op jit(solution)/shard_map/ppermute | solution.py:29
  56.1 2.0 collective-permute-done.3.refs_4_
  58.1 3.4 %collective-permute-done.2.refs_3_ = bf16[2,256,128]{2,1,0:T(8,128)(2,1)S(1)} collective-permute-done((bf16[2,256,128]{2,1,0:T(8,128)(2,1)S(1)}, bf16[2,256,128]{2,1,0:T(8,128)(2,1)S(1)}, u32[]{:S(2)}, u32[]{:S(2)}) %collective-permute-start.2) | collective-permute-done | bytes 131104 | tf_op jit(solution)/shard_map/ppermute | solution.py:29
  64.0 3.2 %shard_map.258 = (bf16[224,384]{1,0:T(8,128)(2,1)S(1)}, bf16[224,128]{1,0:T(8,128)(2,1)S(1)}, f32[112,1024]{1,0:T(8,128)S(1)}, bf16[112,1024]{1,0:T(8,128)(2,1)S(1)}) custom-call(s32[6]{0:T(128)S(1)} %stack.45.refs_0_.place.meta, bf16[112,1024]{1,0:T(8,128)(2,1)S(1)} %get-tuple-element.171.refs_1_.refs_0_, ...), custom_call_target="tpu_custom_call" | custom-call | flops 234881024 | bytes 3481624 | tf_op jit(solution)/shard_map/pallas_call | solution.py:136
  69.9 2.1 collective-permute-start.8
  72.0 2.2 collective-permute-done.7.refs_1_
  74.1 1.9 collective-permute-done.8.refs_3_
  76.1 2.2 collective-permute-start.9
  78.2 3.9 %collective-permute-done.9.refs_1_ = bf16[112,512]{1,0:T(8,128)(2,1)S(1)} collective-permute-done((bf16[112,512]{1,0:T(8,128)(2,1)S(1)}, bf16[112,512]{1,0:T(8,128)(2,1)S(1)}, u32[]{:S(2)}, u32[]{:S(2)}) %collective-permute-start.9) | collective-permute-done | bytes 114720 | tf_op jit(solution)/shard_map/ppermute | solution.py:43
  84.9 7.2 %all-to-all-start.2 = ((bf16[16,512,128]{2,1,0:T(8,128)(2,1)}), bf16[16,512,128]{2,1,0:T(8,128)(2,1)}, u32[]{:S(2)}, u32[]{:S(2)}) async-start(bf16[16,512,128]{2,1,0:T(8,128)(2,1)} %copy-done.1), calls=%async_computation.2 | async-start | bytes 4194304 | tf_op jit(solution)/shard_map/all_to_all | solution.py:559
  99.3 2.5 collective-permute-start.14
  103.6 1.9 collective-permute-done.14.refs_3_
  105.5 2.6 collective-permute-start.15
  108.1 3.5 %collective-permute-done.15.refs_1_ = bf16[112,512]{1,0:T(8,128)(2,1)S(1)} collective-permute-done((bf16[112,512]{1,0:T(8,128)(2,1)S(1)}, bf16[112,512]{1,0:T(8,128)(2,1)S(1)}, u32[]{:S(2)}, u32[]{:S(2)}) %collective-permute-start.15) | collective-permute-done | bytes 114720 | tf_op jit(solution)/shard_map/ppermute | solution.py:43
  115.5 2.0 shard_map.266
  122.0 3.9 %collective-permute-done.19.refs_1_ = bf16[112,512]{1,0:T(8,128)(2,1)S(1)} collective-permute-done((bf16[112,512]{1,0:T(8,128)(2,1)S(1)}, bf16[112,512]{1,0:T(8,128)(2,1)S(1)}, u32[]{:S(2)}, u32[]{:S(2)}) %collective-permute-start.19) | collective-permute-done | bytes 114720 | tf_op jit(solution)/shard_map/ppermute | solution.py:38
  129.8 5.0 %collective-permute-done.21.refs_1_ = bf16[112,512]{1,0:T(8,128)(2,1)S(1)} collective-permute-done((bf16[112,512]{1,0:T(8,128)(2,1)}, bf16[112,512]{1,0:T(8,128)(2,1)S(1)}, u32[]{:S(2)}, u32[]{:S(2)}) %collective-permute-start.21) | collective-permute-done | bytes 114720 | tf_op jit(solution)/shard_map/ppermute | solution.py:43
  140.2 2.6 shard_map.270
  142.9 2.6 shard_map.271
  148.1 2.1 collective-permute-start.26
  150.2 2.3 shard_map.274
  153.8 1.9 collective-permute-done.25.refs_1_
  158.5 7.2 %all-to-all-start.3 = ((bf16[16,512,128]{2,1,0:T(8,128)(2,1)}), bf16[16,512,128]{2,1,0:T(8,128)(2,1)}, u32[]{:S(2)}, u32[]{:S(2)}) async-start(bf16[16,512,128]{2,1,0:T(8,128)(2,1)} %copy-done.4), calls=%async_computation.3 | async-start | bytes 4194304 | tf_op jit(solution)/shard_map/all_to_all | solution.py:559
  165.7 2.0 collective-permute-start.27
  167.8 5.7 %collective-permute-done.27.refs_1_ = bf16[112,1024]{1,0:T(8,128)(2,1)S(1)} collective-permute-done((bf16[112,1024]{1,0:T(8,128)(2,1)}, bf16[112,1024]{1,0:T(8,128)(2,1)S(1)}, u32[]{:S(2)}, u32[]{:S(2)}) %collective-permute-start.27) | collective-permute-done | bytes 229408 | tf_op jit(solution)/shard_map/ppermute | solution.py:43
  180.5 2.5 shard_map.277
  187.5 2.5 shard_map.280
  191.3 2.0 all-to-all-done.3
  193.4 5.3 %all-to-all-start.4 = ((bf16[16,368,128]{2,1,0:T(8,128)(2,1)}), bf16[16,368,128]{2,1,0:T(8,128)(2,1)}, u32[]{:S(2)}, u32[]{:S(2)}) async-start(bf16[16,368,128]{2,1,0:T(8,128)(2,1)} %copy-done.15), calls=%async_computation.4 | async-start | bytes 3014656 | tf_op jit(solution)/shard_map/all_to_all | solution.py:559
  198.6 2.0 collective-permute-start.34
  201.0 3.6 %collective-permute-done.34.refs_1_ = bf16[112,512]{1,0:T(8,128)(2,1)S(1)} collective-permute-done((bf16[112,512]{1,0:T(8,128)(2,1)S(1)}, bf16[112,512]{1,0:T(8,128)(2,1)S(1)}, u32[]{:S(2)}, u32[]{:S(2)}) %collective-permute-start.34) | collective-permute-done | bytes 114720 | tf_op jit(solution)/shard_map/ppermute | solution.py:43
  216.6 2.2 shard_map.285
  221.4 7.4 %all-to-all-start.5 = ((bf16[16,512,128]{2,1,0:T(8,128)(2,1)}), bf16[16,512,128]{2,1,0:T(8,128)(2,1)}, u32[]{:S(2)}, u32[]{:S(2)}) async-start(bf16[16,512,128]{2,1,0:T(8,128)(2,1)} %copy-done.3), calls=%async_computation.5 | async-start | bytes 4194304 | tf_op jit(solution)/shard_map/all_to_all | solution.py:559
  230.2 4.6 %collective-permute-done.40.refs_1_ = bf16[112,512]{1,0:T(8,128)(2,1)S(1)} collective-permute-done((bf16[112,512]{1,0:T(8,128)(2,1)S(1)}, bf16[112,512]{1,0:T(8,128)(2,1)S(1)}, u32[]{:S(2)}, u32[]{:S(2)}) %collective-permute-start.40) | collective-permute-done | bytes 114720 | tf_op jit(solution)/shard_map/ppermute | solution.py:43
  237.1 3.6 %shard_map.287 = (bf16[224,384]{1,0:T(8,128)(2,1)S(1)}, f32[1,384]{1,0:T(1,128)S(1)}, f32[112,1024]{1,0:T(8,128)S(1)}, bf16[112,1024]{1,0:T(8,128)(2,1)S(1)}) custom-call(s32[6]{0:T(128)S(1)} %stack.45.refs_0_.place.meta, bf16[112,1024]{1,0:T(8,128)(2,1)S(1)} %get-tuple-element.271.refs_1_.refs_4_, ...), custom_call_target="tpu_custom_call" | custom-call | flops 234881024 | bytes 3589656 | tf_op jit(solution)/shard_map/pallas_call | solution.py:136
  243.0 1.9 collective-permute-start.45
  244.8 1.9 shard_map.290
  249.5 1.9 collective-permute-start.46
  251.4 4.2 %collective-permute-done.46.refs_2_ = bf16[112,512]{1,0:T(8,128)(2,1)S(1)} collective-permute-done((bf16[112,512]{1,0:T(8,128)(2,1)S(1)}, bf16[112,512]{1,0:T(8,128)(2,1)S(1)}, u32[]{:S(2)}, u32[]{:S(2)}) %collective-permute-start.46) | collective-permute-done | bytes 114720 | tf_op jit(solution)/shard_map/ppermute | solution.py:43
  261.7 7.2 %all-to-all-start.6 = ((bf16[16,400,128]{2,1,0:T(8,128)(2,1)}), bf16[16,400,128]{2,1,0:T(8,128)(2,1)S(1)}, u32[]{:S(2)}, u32[]{:S(2)}) async-start(bf16[16,400,128]{2,1,0:T(8,128)(2,1)} %shard_map.292), calls=%async_computation.6 | async-start | bytes 3276800 | tf_op jit(solution)/shard_map/all_to_all | solution.py:559
  268.9 1.9 convert_reduce_fusion.1
  270.8 2.6 shard_map.293
  273.5 1.9 convert_reduce_fusion
  278.3 13.9 %all-to-all-done.6.received = bf16[16,400,128]{2,1,0:T(8,128)(2,1)S(1)} async-done(((bf16[16,400,128]{2,1,0:T(8,128)(2,1)}), bf16[16,400,128]{2,1,0:T(8,128)(2,1)S(1)}, u32[]{:S(2)}, u32[]{:S(2)}) %all-to-all-start.6) | async-done | bytes 1638432 | tf_op jit(solution)/shard_map/all_to_all | solution.py:559
  (264 shorter events, 100.0 us)
Async XLA Ops:
  4.3 35.8 %all-to-all-start = ((bf16[16,512,128]{2,1,0:T(8,128)(2,1)}), bf16[16,512,128]{2,1,0:T(8,128)(2,1)}, u32[]{:S(2)}, u32[]{:S(2)}) async-start(bf16[16,512,128]{2,1,0:T(8,128)(2,1)} %shard_map.256), calls=%async_computation | async-start | bytes 4194304 | tf_op jit(solution)/shard_map/all_to_all | solution.py:559
  40.1 44.7 %all-to-all-start.1 = ((bf16[16,768,128]{2,1,0:T(8,128)(2,1)}), bf16[16,768,128]{2,1,0:T(8,128)(2,1)S(1)}, u32[]{:S(2)}, u32[]{:S(2)}) async-start(bf16[16,768,128]{2,1,0:T(8,128)(2,1)} %copy-done), calls=%async_computation.1 | async-start | bytes 6291456 | tf_op jit(solution)/shard_map/all_to_all | solution.py:559
  50.1 8.0 %collective-permute-start.3 = (bf16[2,256,128]{2,1,0:T(8,128)(2,1)S(1)}, bf16[2,256,128]{2,1,0:T(8,128)(2,1)S(1)}, u32[]{:S(2)}, u32[]{:S(2)}) collective-permute-start(bf16[2,256,128]{2,1,0:T(8,128)(2,1)S(1)} %fusion.5.refs_1_), channel_id=1, source_target_pairs={{0,4},{2,6},{4,0},{6,2},{1,5},{3,7},{5,1},{7,3},{8,12},{10,14},{12... | collective-permute-start | bytes 393224 | tf_op jit(solution)/shard_map/ppermute | solution.py:29
  54.1 7.4 %collective-permute-start.2 = (bf16[2,256,128]{2,1,0:T(8,128)(2,1)S(1)}, bf16[2,256,128]{2,1,0:T(8,128)(2,1)S(1)}, u32[]{:S(2)}, u32[]{:S(2)}) collective-permute-start(bf16[2,256,128]{2,1,0:T(8,128)(2,1)S(1)} %fusion.5.refs_1_), channel_id=1, source_target_pairs={{0,6},{2,0},{4,2},{6,4},{1,7},{3,1},{5,3},{7,5},{8,14},{10,8},{12,... | collective-permute-start | bytes 393224 | tf_op jit(solution)/shard_map/ppermute | solution.py:29
  54.8 6.7 %collective-permute-start.1 = (bf16[2,256,128]{2,1,0:T(8,128)(2,1)S(1)}, bf16[2,256,128]{2,1,0:T(8,128)(2,1)S(1)}, u32[]{:S(2)}, u32[]{:S(2)}) collective-permute-start(bf16[2,256,128]{2,1,0:T(8,128)(2,1)S(1)} %fusion.5.refs_1_), channel_id=1, source_target_pairs={{0,2},{2,4},{4,6},{6,0},{1,3},{3,5},{5,7},{7,1},{8,10},{10,12},{12... | collective-permute-start | bytes 393224 | tf_op jit(solution)/shard_map/ppermute | solution.py:29
  62.4 1.6 collective-permute-start.5
  67.2 1.6 collective-permute-start.6
  68.8 5.3 %collective-permute-start.7 = (bf16[112,512]{1,0:T(8,128)(2,1)S(1)}, bf16[112,512]{1,0:T(8,128)(2,1)S(1)}, u32[]{:S(2)}, u32[]{:S(2)}) collective-permute-start(bf16[112,512]{1,0:T(8,128)(2,1)S(1)} %get-tuple-element.175.refs_0_), channel_id=1, source_target_pairs={{0,2},{2,0},{4,6},{6,4},{1,3},{3,1},{5,7},{7,5},{8,10},{10,8},{12,... | collective-permute-start | bytes 344072 | tf_op jit(solution)/shard_map/ppermute | solution.py:38
  69.9 6.1 %collective-permute-start.8 = (bf16[112,512]{1,0:T(8,128)(2,1)S(1)}, bf16[112,512]{1,0:T(8,128)(2,1)S(1)}, u32[]{:S(2)}, u32[]{:S(2)}) collective-permute-start(bf16[112,512]{1,0:T(8,128)(2,1)S(1)} %get-tuple-element.176.refs_2_), channel_id=1, source_target_pairs={{0,6},{6,0},{2,4},{4,2},{1,7},{7,1},{3,5},{5,3},{8,14},{14,8},{10,... | collective-permute-start | bytes 344072 | tf_op jit(solution)/shard_map/ppermute | solution.py:39
  76.1 6.1 %collective-permute-start.9 = (bf16[112,512]{1,0:T(8,128)(2,1)S(1)}, bf16[112,512]{1,0:T(8,128)(2,1)S(1)}, u32[]{:S(2)}, u32[]{:S(2)}) collective-permute-start(bf16[112,512]{1,0:T(8,128)(2,1)S(1)} %get-tuple-element.177.refs_0_), channel_id=1, source_target_pairs={{0,6},{6,0},{2,4},{4,2},{1,7},{7,1},{3,5},{5,3},{8,14},{14,8},{10,... | collective-permute-start | bytes 344072 | tf_op jit(solution)/shard_map/ppermute | solution.py:43
  78.2 4.8 %collective-permute-start.10 = (bf16[112,512]{1,0:T(8,128)(2,1)S(1)}, bf16[112,512]{1,0:T(8,128)(2,1)S(1)}, u32[]{:S(2)}, u32[]{:S(2)}) collective-permute-start(bf16[112,512]{1,0:T(8,128)(2,1)S(1)} %get-tuple-element.178.refs_2_), channel_id=1, source_target_pairs={{0,2},{2,0},{4,6},{6,4},{1,3},{3,1},{5,7},{7,5},{8,10},{10,8},{12,... | collective-permute-start | bytes 344072 | tf_op jit(solution)/shard_map/ppermute | solution.py:44
  84.9 43.7 %all-to-all-start.2 = ((bf16[16,512,128]{2,1,0:T(8,128)(2,1)}), bf16[16,512,128]{2,1,0:T(8,128)(2,1)}, u32[]{:S(2)}, u32[]{:S(2)}) async-start(bf16[16,512,128]{2,1,0:T(8,128)(2,1)} %copy-done.1), calls=%async_computation.2 | async-start | bytes 4194304 | tf_op jit(solution)/shard_map/all_to_all | solution.py:559
  92.1 1.8 collective-permute-start.11
  96.7 1.5 collective-permute-start.12
  98.3 5.3 %collective-permute-start.13 = (bf16[112,512]{1,0:T(8,128)(2,1)S(1)}, bf16[112,512]{1,0:T(8,128)(2,1)S(1)}, u32[]{:S(2)}, u32[]{:S(2)}) collective-permute-start(bf16[112,512]{1,0:T(8,128)(2,1)S(1)} %get-tuple-element.185.refs_0_), channel_id=1, source_target_pairs={{0,2},{2,0},{4,6},{6,4},{1,3},{3,1},{5,7},{7,5},{8,10},{10,8},{12,... | collective-permute-start | bytes 344072 | tf_op jit(solution)/shard_map/ppermute | solution.py:38
  99.3 6.1 %collective-permute-start.14 = (bf16[112,512]{1,0:T(8,128)(2,1)S(1)}, bf16[112,512]{1,0:T(8,128)(2,1)S(1)}, u32[]{:S(2)}, u32[]{:S(2)}) collective-permute-start(bf16[112,512]{1,0:T(8,128)(2,1)S(1)} %get-tuple-element.186.refs_2_), channel_id=1, source_target_pairs={{0,6},{6,0},{2,4},{4,2},{1,7},{7,1},{3,5},{5,3},{8,14},{14,8},{10,... | collective-permute-start | bytes 344072 | tf_op jit(solution)/shard_map/ppermute | solution.py:39
  105.5 6.1 %collective-permute-start.15 = (bf16[112,512]{1,0:T(8,128)(2,1)S(1)}, bf16[112,512]{1,0:T(8,128)(2,1)S(1)}, u32[]{:S(2)}, u32[]{:S(2)}) collective-permute-start(bf16[112,512]{1,0:T(8,128)(2,1)S(1)} %get-tuple-element.187.refs_0_), channel_id=1, source_target_pairs={{0,6},{6,0},{2,4},{4,2},{1,7},{7,1},{3,5},{5,3},{8,14},{14,8},{10,... | collective-permute-start | bytes 344072 | tf_op jit(solution)/shard_map/ppermute | solution.py:43
  108.1 4.8 %collective-permute-start.16 = (bf16[112,512]{1,0:T(8,128)(2,1)S(1)}, bf16[112,512]{1,0:T(8,128)(2,1)S(1)}, u32[]{:S(2)}, u32[]{:S(2)}) collective-permute-start(bf16[112,512]{1,0:T(8,128)(2,1)S(1)} %get-tuple-element.188.refs_2_), channel_id=1, source_target_pairs={{0,2},{2,0},{4,6},{6,4},{1,3},{3,1},{5,7},{7,5},{8,10},{10,8},{12,... | collective-permute-start | bytes 344072 | tf_op jit(solution)/shard_map/ppermute | solution.py:44
  120.5 5.4 %collective-permute-start.19 = (bf16[112,512]{1,0:T(8,128)(2,1)S(1)}, bf16[112,512]{1,0:T(8,128)(2,1)S(1)}, u32[]{:S(2)}, u32[]{:S(2)}) collective-permute-start(bf16[112,512]{1,0:T(8,128)(2,1)S(1)} %get-tuple-element.193.refs_0_), channel_id=1, source_target_pairs={{0,2},{2,0},{4,6},{6,4},{1,3},{3,1},{5,7},{7,5},{8,10},{10,8},{12,... | collective-permute-start | bytes 344072 | tf_op jit(solution)/shard_map/ppermute | solution.py:38
  120.7 6.5 %collective-permute-start.20 = (bf16[112,512]{1,0:T(8,128)(2,1)S(1)}, bf16[112,512]{1,0:T(8,128)(2,1)S(1)}, u32[]{:S(2)}, u32[]{:S(2)}) collective-permute-start(bf16[112,512]{1,0:T(8,128)(2,1)S(1)} %get-tuple-element.194.refs_2_), channel_id=1, source_target_pairs={{0,6},{6,0},{2,4},{4,2},{1,7},{7,1},{3,5},{5,3},{8,14},{14,8},{10,... | collective-permute-start | bytes 344072 | tf_op jit(solution)/shard_map/ppermute | solution.py:39
  128.6 6.2 %collective-permute-start.21 = (bf16[112,512]{1,0:T(8,128)(2,1)}, bf16[112,512]{1,0:T(8,128)(2,1)S(1)}, u32[]{:S(2)}, u32[]{:S(2)}) collective-permute-start(bf16[112,512]{1,0:T(8,128)(2,1)} %copy-done.47), channel_id=1, source_target_pairs={{0,6},{6,0},{2,4},{4,2},{1,7},{7,1},{3,5},{5,3},{8,14},{14,8},{10,... | collective-permute-start | bytes 344072 | tf_op jit(solution)/shard_map/ppermute | solution.py:43
  129.8 5.0 %collective-permute-start.22 = (bf16[112,512]{1,0:T(8,128)(2,1)}, bf16[112,512]{1,0:T(8,128)(2,1)S(1)}, u32[]{:S(2)}, u32[]{:S(2)}) collective-permute-start(bf16[112,512]{1,0:T(8,128)(2,1)} %copy-done.49), channel_id=1, source_target_pairs={{0,2},{2,0},{4,6},{6,4},{1,3},{3,1},{5,7},{7,5},{8,10},{10,8},{12,... | collective-permute-start | bytes 344072 | tf_op jit(solution)/shard_map/ppermute | solution.py:44
  138.7 4.1 %collective-permute-start.4 = (bf16[112,1024]{1,0:T(8,128)(2,1)S(1)}, bf16[112,1024]{1,0:T(8,128)(2,1)S(1)}, u32[]{:S(2)}, u32[]{:S(2)}) collective-permute-start(bf16[112,1024]{1,0:T(8,128)(2,1)S(1)} %get-tuple-element.168.refs_0_.refs_4_.refs_3_), channel_id=1, source_target_pairs={{0,1},{1,0},{2,3},{3,2},{4,5},{5,4},{6,7},{7,6},{8,9},{9,8},{10,11... | collective-permute-start | bytes 688136 | tf_op jit(solution)/shard_map/ppermute | solution.py:24
  146.0 1.8 collective-permute-start.24
  148.0 7.7 %collective-permute-start.25 = (bf16[112,1024]{1,0:T(8,128)(2,1)S(1)}, bf16[112,1024]{1,0:T(8,128)(2,1)S(1)}, u32[]{:S(2)}, u32[]{:S(2)}) collective-permute-start(bf16[112,1024]{1,0:T(8,128)(2,1)S(1)} %get-tuple-element.211.refs_0_), channel_id=1, source_target_pairs={{0,2},{2,0},{4,6},{6,4},{1,3},{3,1},{5,7},{7,5},{8,10},{10,8},{12,... | collective-permute-start | bytes 688136 | tf_op jit(solution)/shard_map/ppermute | solution.py:38
  148.1 8.9 %collective-permute-start.26 = (bf16[112,1024]{1,0:T(8,128)(2,1)S(1)}, bf16[112,1024]{1,0:T(8,128)(2,1)S(1)}, u32[]{:S(2)}, u32[]{:S(2)}) collective-permute-start(bf16[112,1024]{1,0:T(8,128)(2,1)S(1)} %get-tuple-element.212.refs_2_), channel_id=1, source_target_pairs={{0,6},{6,0},{2,4},{4,2},{1,7},{7,1},{3,5},{5,3},{8,14},{14,8},{10,... | collective-permute-start | bytes 688136 | tf_op jit(solution)/shard_map/ppermute | solution.py:39
  158.5 34.9 %all-to-all-start.3 = ((bf16[16,512,128]{2,1,0:T(8,128)(2,1)}), bf16[16,512,128]{2,1,0:T(8,128)(2,1)}, u32[]{:S(2)}, u32[]{:S(2)}) async-start(bf16[16,512,128]{2,1,0:T(8,128)(2,1)} %copy-done.4), calls=%async_computation.3 | async-start | bytes 4194304 | tf_op jit(solution)/shard_map/all_to_all | solution.py:559
  165.7 7.7 %collective-permute-start.27 = (bf16[112,1024]{1,0:T(8,128)(2,1)}, bf16[112,1024]{1,0:T(8,128)(2,1)S(1)}, u32[]{:S(2)}, u32[]{:S(2)}) collective-permute-start(bf16[112,1024]{1,0:T(8,128)(2,1)} %copy-done.38), channel_id=1, source_target_pairs={{0,6},{6,0},{2,4},{4,2},{1,7},{7,1},{3,5},{5,3},{8,14},{14,8},{10,... | collective-permute-start | bytes 688136 | tf_op jit(solution)/shard_map/ppermute | solution.py:43
  167.8 6.2 %collective-permute-start.28 = (bf16[112,1024]{1,0:T(8,128)(2,1)}, bf16[112,1024]{1,0:T(8,128)(2,1)S(1)}, u32[]{:S(2)}, u32[]{:S(2)}) collective-permute-start(bf16[112,1024]{1,0:T(8,128)(2,1)} %copy-done.40), channel_id=1, source_target_pairs={{0,2},{2,0},{4,6},{6,4},{1,3},{3,1},{5,7},{7,5},{8,10},{10,8},{12,... | collective-permute-start | bytes 688136 | tf_op jit(solution)/shard_map/ppermute | solution.py:44
  183.0 1.6 collective-permute-start.30
  184.7 6.5 %collective-permute-start.31 = (bf16[112,512]{1,0:T(8,128)(2,1)S(1)}, bf16[112,512]{1,0:T(8,128)(2,1)S(1)}, u32[]{:S(2)}, u32[]{:S(2)}) collective-permute-start(bf16[112,512]{1,0:T(8,128)(2,1)S(1)} %get-tuple-element.236.refs_0_), channel_id=1, source_target_pairs={{0,2},{2,0},{4,6},{6,4},{1,3},{3,1},{5,7},{7,5},{8,10},{10,8},{12,... | collective-permute-start | bytes 344072 | tf_op jit(solution)/shard_map/ppermute | solution.py:38
  185.0 6.3 %collective-permute-start.32 = (bf16[112,512]{1,0:T(8,128)(2,1)S(1)}, bf16[112,512]{1,0:T(8,128)(2,1)S(1)}, u32[]{:S(2)}, u32[]{:S(2)}) collective-permute-start(bf16[112,512]{1,0:T(8,128)(2,1)S(1)} %get-tuple-element.237.refs_2_), channel_id=1, source_target_pairs={{0,6},{6,0},{2,4},{4,2},{1,7},{7,1},{3,5},{5,3},{8,14},{14,8},{10,... | collective-permute-start | bytes 344072 | tf_op jit(solution)/shard_map/ppermute | solution.py:39
  193.4 28.0 %all-to-all-start.4 = ((bf16[16,368,128]{2,1,0:T(8,128)(2,1)}), bf16[16,368,128]{2,1,0:T(8,128)(2,1)}, u32[]{:S(2)}, u32[]{:S(2)}) async-start(bf16[16,368,128]{2,1,0:T(8,128)(2,1)} %copy-done.15), calls=%async_computation.4 | async-start | bytes 3014656 | tf_op jit(solution)/shard_map/all_to_all | solution.py:559
  198.6 6.0 %collective-permute-start.34 = (bf16[112,512]{1,0:T(8,128)(2,1)S(1)}, bf16[112,512]{1,0:T(8,128)(2,1)S(1)}, u32[]{:S(2)}, u32[]{:S(2)}) collective-permute-start(bf16[112,512]{1,0:T(8,128)(2,1)S(1)} %get-tuple-element.246.refs_0_), channel_id=1, source_target_pairs={{0,6},{6,0},{2,4},{4,2},{1,7},{7,1},{3,5},{5,3},{8,14},{14,8},{10,... | collective-permute-start | bytes 344072 | tf_op jit(solution)/shard_map/ppermute | solution.py:43
  200.7 4.8 %collective-permute-start.35 = (bf16[112,512]{1,0:T(8,128)(2,1)S(1)}, bf16[112,512]{1,0:T(8,128)(2,1)S(1)}, u32[]{:S(2)}, u32[]{:S(2)}) collective-permute-start(bf16[112,512]{1,0:T(8,128)(2,1)S(1)} %get-tuple-element.247.refs_2_), channel_id=1, source_target_pairs={{0,2},{2,0},{4,6},{6,4},{1,3},{3,1},{5,7},{7,5},{8,10},{10,8},{12,... | collective-permute-start | bytes 344072 | tf_op jit(solution)/shard_map/ppermute | solution.py:44
  209.4 1.5 collective-permute-start.36
  213.0 1.6 collective-permute-start.37
  214.7 5.5 %collective-permute-start.38 = (bf16[112,512]{1,0:T(8,128)(2,1)S(1)}, bf16[112,512]{1,0:T(8,128)(2,1)S(1)}, u32[]{:S(2)}, u32[]{:S(2)}) collective-permute-start(bf16[112,512]{1,0:T(8,128)(2,1)S(1)} %get-tuple-element.256.refs_0_), channel_id=1, source_target_pairs={{0,2},{2,0},{4,6},{6,4},{1,3},{3,1},{5,7},{7,5},{8,10},{10,8},{12,... | collective-permute-start | bytes 344072 | tf_op jit(solution)/shard_map/ppermute | solution.py:38
  215.1 6.1 %collective-permute-start.39 = (bf16[112,512]{1,0:T(8,128)(2,1)S(1)}, bf16[112,512]{1,0:T(8,128)(2,1)S(1)}, u32[]{:S(2)}, u32[]{:S(2)}) collective-permute-start(bf16[112,512]{1,0:T(8,128)(2,1)S(1)} %get-tuple-element.257.refs_2_), channel_id=1, source_target_pairs={{0,6},{6,0},{2,4},{4,2},{1,7},{7,1},{3,5},{5,3},{8,14},{14,8},{10,... | collective-permute-start | bytes 344072 | tf_op jit(solution)/shard_map/ppermute | solution.py:39
  221.4 40.3 %all-to-all-start.5 = ((bf16[16,512,128]{2,1,0:T(8,128)(2,1)}), bf16[16,512,128]{2,1,0:T(8,128)(2,1)}, u32[]{:S(2)}, u32[]{:S(2)}) async-start(bf16[16,512,128]{2,1,0:T(8,128)(2,1)} %copy-done.3), calls=%async_computation.5 | async-start | bytes 4194304 | tf_op jit(solution)/shard_map/all_to_all | solution.py:559
  228.8 6.0 %collective-permute-start.40 = (bf16[112,512]{1,0:T(8,128)(2,1)S(1)}, bf16[112,512]{1,0:T(8,128)(2,1)S(1)}, u32[]{:S(2)}, u32[]{:S(2)}) collective-permute-start(bf16[112,512]{1,0:T(8,128)(2,1)S(1)} %get-tuple-element.268.refs_0_), channel_id=1, source_target_pairs={{0,6},{6,0},{2,4},{4,2},{1,7},{7,1},{3,5},{5,3},{8,14},{14,8},{10,... | collective-permute-start | bytes 344072 | tf_op jit(solution)/shard_map/ppermute | solution.py:43
  230.2 4.8 %collective-permute-start.41 = (bf16[112,512]{1,0:T(8,128)(2,1)S(1)}, bf16[112,512]{1,0:T(8,128)(2,1)S(1)}, u32[]{:S(2)}, u32[]{:S(2)}) collective-permute-start(bf16[112,512]{1,0:T(8,128)(2,1)S(1)} %get-tuple-element.269.refs_2_), channel_id=1, source_target_pairs={{0,2},{2,0},{4,6},{6,4},{1,3},{3,1},{5,7},{7,5},{8,10},{10,8},{12,... | collective-permute-start | bytes 344072 | tf_op jit(solution)/shard_map/ppermute | solution.py:44
  235.5 1.6 collective-permute-start.42
  242.9 5.3 %collective-permute-start.44 = (bf16[112,512]{1,0:T(8,128)(2,1)S(1)}, bf16[112,512]{1,0:T(8,128)(2,1)S(1)}, u32[]{:S(2)}, u32[]{:S(2)}) collective-permute-start(bf16[112,512]{1,0:T(8,128)(2,1)S(1)} %get-tuple-element.278.refs_0_), channel_id=1, source_target_pairs={{0,2},{2,0},{4,6},{6,4},{1,3},{3,1},{5,7},{7,5},{8,10},{10,8},{12,... | collective-permute-start | bytes 344072 | tf_op jit(solution)/shard_map/ppermute | solution.py:38
  243.0 6.5 %collective-permute-start.45 = (bf16[112,512]{1,0:T(8,128)(2,1)S(1)}, bf16[112,512]{1,0:T(8,128)(2,1)S(1)}, u32[]{:S(2)}, u32[]{:S(2)}) collective-permute-start(bf16[112,512]{1,0:T(8,128)(2,1)S(1)} %get-tuple-element.279.refs_2_), channel_id=1, source_target_pairs={{0,6},{6,0},{2,4},{4,2},{1,7},{7,1},{3,5},{5,3},{8,14},{14,8},{10,... | collective-permute-start | bytes 344072 | tf_op jit(solution)/shard_map/ppermute | solution.py:39
  249.5 6.1 %collective-permute-start.46 = (bf16[112,512]{1,0:T(8,128)(2,1)S(1)}, bf16[112,512]{1,0:T(8,128)(2,1)S(1)}, u32[]{:S(2)}, u32[]{:S(2)}) collective-permute-start(bf16[112,512]{1,0:T(8,128)(2,1)S(1)} %get-tuple-element.286.refs_1_), channel_id=1, source_target_pairs={{0,6},{6,0},{2,4},{4,2},{1,7},{7,1},{3,5},{5,3},{8,14},{14,8},{10,... | collective-permute-start | bytes 344072 | tf_op jit(solution)/shard_map/ppermute | solution.py:43
  251.4 4.8 %collective-permute-start.47 = (bf16[112,512]{1,0:T(8,128)(2,1)S(1)}, bf16[112,512]{1,0:T(8,128)(2,1)S(1)}, u32[]{:S(2)}, u32[]{:S(2)}) collective-permute-start(bf16[112,512]{1,0:T(8,128)(2,1)S(1)} %get-tuple-element.287.refs_3_), channel_id=1, source_target_pairs={{0,2},{2,0},{4,6},{6,4},{1,3},{3,1},{5,7},{7,5},{8,10},{10,8},{12,... | collective-permute-start | bytes 344072 | tf_op jit(solution)/shard_map/ppermute | solution.py:44
  261.7 30.5 %all-to-all-start.6 = ((bf16[16,400,128]{2,1,0:T(8,128)(2,1)}), bf16[16,400,128]{2,1,0:T(8,128)(2,1)S(1)}, u32[]{:S(2)}, u32[]{:S(2)}) async-start(bf16[16,400,128]{2,1,0:T(8,128)(2,1)} %shard_map.292), calls=%async_computation.6 | async-start | bytes 3276800 | tf_op jit(solution)/shard_map/all_to_all | solution.py:559
  (77 other events, 585.4 us)

commit v3 on v2

--- a/solution.py
+++ b/solution.py
@@ -659,8 +659,7 @@
             1,
             ((3, attention_at[d], 256),),
         )
-        pairs, _, done = total(mine, theirs, None, mlp_w[1])
-        mlp_w[1] = done
+        pairs, _, _ = total(mine, theirs)
         middle, h2 = run(
             functools.partial(norm_forward, ((d, 2), (d, 3), (d, 4))),
             NORM_SHAPES,

time: 296 us -> 294 us (level)
    unnamed x136 -> x138, local copies, waits for them, and re-layouts: 30.2 us -> 27.8 us
  transfers between devices with their start and end apart: 57 -> 57, of which waited for: 47 -> 47; matrix products, arithmetic and copies ran while one was open for 4% -> 4% of each run, Pallas kernels for 12% -> 13%
where the time goes in v3:
time: 294 us; the launch traced here: 292 us
  waiting for transfers between devices  119 us (40%)
  starting transfers between devices  85.6 us (29%)
  Pallas kernels  46.5 us (16%)
  local copies, waits for them, and re-layouts  30.1 us (10%)
  other arithmetic  9.08 us (3%)
    all_to_all x7, starting transfers between devices, exchange(): return lax.all_to_all(chunks, DP, 0, 0)  47.3 us
    pallas_call x38, Pallas kernels, run(): pl.pallas_call(body, out_shape=list(outs) + more, in_specs=specs, out_spe...  40.3 us
    all_to_all x7, waiting for transfers between devices, exchange(): return lax.all_to_all(chunks, DP, 0, 0)  38.4 us
    ppermute x7, waiting for transfers between devices, total(): got_left = lax.ppermute(left, 'z', PAIR_B)  30.2 us
    unnamed x138, local copies, waits for them, and re-layouts  27.8 us
    ppermute x19, waiting for transfers between devices, core_swap(): return lax.ppermute(block, 'c', SWAP)  22.4 us
    ppermute x7, starting transfers between devices, total(): got_left = lax.ppermute(left, 'z', PAIR_B)  13.4 us
    ppermute x7, starting transfers between devices, total(): got_right = lax.ppermute(right, 'z', PAIR_B)  12.6 us
  transfers between devices with their start and end apart: 57, of which 47 were waited for; matrix products, arithmetic and copies ran while one was open for 4% of the time, Pallas kernels for 13%

profile of v3, /device:TPU:4, one launch (start us, length us, event | category | flops | bytes accessed | tf_op | source)
XLA Modules:
  0.0 292.3 jit_solution(2397623115502750038)
XLA Ops:
  0.6 3.6 %shard_map.256 = bf16[16,512,128]{2,1,0:T(8,128)(2,1)} custom-call(s32[8]{0:T(128)} %refs_0_.3, bf16[3,64,197]{2,1,0:T(8,128)(2,1)} %bitcast.34, bf16[3,64,197]{2,1,0:T(8,128)(2,1)} %bitcast.35, f32[2,64]{1,0:T(2,128)} %refs_3_.3, f32[2,64]{1,0:T(2,128)} %refs_4_.1, f32[2,64]{1,0:T(2,128)} %refs_5_.1, f32[2,64]{1,0:T(2,128)} %refs_6_.1, f32[2,64]{1,0:T(2,128)} %refs_7_.1, ...), custom_call_target="tpu_custom_call" | custom-call | bytes 2385696 | tf_op jit(solution)/shard_map/pallas_call | solution.py:136
  4.3 7.6 %all-to-all-start = ((bf16[16,512,128]{2,1,0:T(8,128)(2,1)}), bf16[16,512,128]{2,1,0:T(8,128)(2,1)}, u32[]{:S(2)}, u32[]{:S(2)}) async-start(bf16[16,512,128]{2,1,0:T(8,128)(2,1)} %shard_map.256), calls=%async_computation | async-start | bytes 4194304 | tf_op jit(solution)/shard_map/all_to_all | solution.py:559
  17.8 22.4 %all-to-all-done.refs_3_.refs_4_ = bf16[16,512,128]{2,1,0:T(8,128)(2,1)} async-done(((bf16[16,512,128]{2,1,0:T(8,128)(2,1)}), bf16[16,512,128]{2,1,0:T(8,128)(2,1)}, u32[]{:S(2)}, u32[]{:S(2)}) %all-to-all-start) | async-done | bytes 2097184 | tf_op jit(solution)/shard_map/all_to_all | solution.py:559
  40.1 5.4 %all-to-all-start.1 = ((bf16[16,768,128]{2,1,0:T(8,128)(2,1)}), bf16[16,768,128]{2,1,0:T(8,128)(2,1)S(1)}, u32[]{:S(2)}, u32[]{:S(2)}) async-start(bf16[16,768,128]{2,1,0:T(8,128)(2,1)} %copy-done), calls=%async_computation.1 | async-start | bytes 6291456 | tf_op jit(solution)/shard_map/all_to_all | solution.py:559
  50.1 4.0 %collective-permute-start.3 = (bf16[2,256,128]{2,1,0:T(8,128)(2,1)S(1)}, bf16[2,256,128]{2,1,0:T(8,128)(2,1)S(1)}, u32[]{:S(2)}, u32[]{:S(2)}) collective-permute-start(bf16[2,256,128]{2,1,0:T(8,128)(2,1)S(1)} %fusion.5.refs_1_), channel_id=1, source_target_pairs={{0,4},{2,6},{4,0},{6,2},{1,5},{3,7},{5,1},{7,3},{8,12},{10,14},{12... | collective-permute-start | bytes 393224 | tf_op jit(solution)/shard_map/ppermute | solution.py:29
  56.1 2.0 collective-permute-done.3.refs_4_
  58.1 3.4 %collective-permute-done.2.refs_3_ = bf16[2,256,128]{2,1,0:T(8,128)(2,1)S(1)} collective-permute-done((bf16[2,256,128]{2,1,0:T(8,128)(2,1)S(1)}, bf16[2,256,128]{2,1,0:T(8,128)(2,1)S(1)}, u32[]{:S(2)}, u32[]{:S(2)}) %collective-permute-start.2) | collective-permute-done | bytes 131104 | tf_op jit(solution)/shard_map/ppermute | solution.py:29
  64.0 3.2 %shard_map.258 = (bf16[224,384]{1,0:T(8,128)(2,1)S(1)}, bf16[224,128]{1,0:T(8,128)(2,1)S(1)}, f32[112,1024]{1,0:T(8,128)S(1)}, bf16[112,1024]{1,0:T(8,128)(2,1)S(1)}) custom-call(s32[6]{0:T(128)S(1)} %stack.45.refs_0_.place.meta, bf16[112,1024]{1,0:T(8,128)(2,1)S(1)} %get-tuple-element.168.refs_1_.refs_0_, ...), custom_call_target="tpu_custom_call" | custom-call | flops 234881024 | bytes 3481624 | tf_op jit(solution)/shard_map/pallas_call | solution.py:136
  69.9 2.1 collective-permute-start.8
  72.0 2.2 collective-permute-done.7.refs_1_
  74.1 1.9 collective-permute-done.8.refs_3_
  76.1 2.1 collective-permute-start.9
  78.2 3.9 %collective-permute-done.9.refs_1_ = bf16[112,512]{1,0:T(8,128)(2,1)S(1)} collective-permute-done((bf16[112,512]{1,0:T(8,128)(2,1)S(1)}, bf16[112,512]{1,0:T(8,128)(2,1)S(1)}, u32[]{:S(2)}, u32[]{:S(2)}) %collective-permute-start.9) | collective-permute-done | bytes 114720 | tf_op jit(solution)/shard_map/ppermute | solution.py:43
  84.8 7.2 %all-to-all-start.2 = ((bf16[16,512,128]{2,1,0:T(8,128)(2,1)}), bf16[16,512,128]{2,1,0:T(8,128)(2,1)}, u32[]{:S(2)}, u32[]{:S(2)}) async-start(bf16[16,512,128]{2,1,0:T(8,128)(2,1)} %copy-done.1), calls=%async_computation.2 | async-start | bytes 4194304 | tf_op jit(solution)/shard_map/all_to_all | solution.py:559
  99.3 2.5 collective-permute-start.14
  103.6 1.9 collective-permute-done.14.refs_3_
  105.5 2.6 collective-permute-start.15
  108.1 3.5 %collective-permute-done.15.refs_1_ = bf16[112,512]{1,0:T(8,128)(2,1)S(1)} collective-permute-done((bf16[112,512]{1,0:T(8,128)(2,1)S(1)}, bf16[112,512]{1,0:T(8,128)(2,1)S(1)}, u32[]{:S(2)}, u32[]{:S(2)}) %collective-permute-start.15) | collective-permute-done | bytes 114720 | tf_op jit(solution)/shard_map/ppermute | solution.py:43
  114.8 2.0 shard_map.266
  121.3 3.9 %collective-permute-done.19.refs_1_ = bf16[112,512]{1,0:T(8,128)(2,1)S(1)} collective-permute-done((bf16[112,512]{1,0:T(8,128)(2,1)S(1)}, bf16[112,512]{1,0:T(8,128)(2,1)S(1)}, u32[]{:S(2)}, u32[]{:S(2)}) %collective-permute-start.19) | collective-permute-done | bytes 114720 | tf_op jit(solution)/shard_map/ppermute | solution.py:38
  127.8 4.8 %collective-permute-done.21.refs_1_ = bf16[112,512]{1,0:T(8,128)(2,1)S(1)} collective-permute-done((bf16[112,512]{1,0:T(8,128)(2,1)S(1)}, bf16[112,512]{1,0:T(8,128)(2,1)S(1)}, u32[]{:S(2)}, u32[]{:S(2)}) %collective-permute-start.21) | collective-permute-done | bytes 114720 | tf_op jit(solution)/shard_map/ppermute | solution.py:43
  137.8 2.6 shard_map.270
  140.4 3.6 %shard_map.271 = (bf16[224,512]{1,0:T(8,128)(2,1)S(1)}, f32[1,512]{1,0:T(1,128)S(1)}, f32[112,2048]{1,0:T(8,128)S(1)}, bf16[112,2048]{1,0:T(8,128)(2,1)S(1)}) custom-call(bf16[112,1024]{1,0:T(8,128)(2,1)S(1)} %get-tuple-element.165.refs_0_.refs_4_.refs_3_, bf16[112,1024]{1,0:T(8,128)(2,1)} %collective-permute-done.4.refs_1_.refs_5_, ...), custom_call_target="tpu_custom_call" | custom-call | flops 469762048 | bytes 5310464 | tf_op jit(solution)/shard_map/pallas_call | solution.py:136
  146.1 2.1 collective-permute-start.26
  148.2 3.2 %shard_map.274 = (bf16[16,512,128]{2,1,0:T(8,128)(2,1)}, bf16[16,512,128]{2,1,0:T(8,128)(2,1)S(1)}) custom-call(bf16[112,1024]{1,0:T(8,128)(2,1)S(1)} %copy-done.39, bf16[112,1024]{1,0:T(8,128)(2,1)S(1)} %copy-done.42, bf16[224,512]{1,0:T(8,128)(2,1)S(1)} %get-tuple-element.209.refs_2_, bf16[224,512]{1,0:T(8,128)(2,1)S(1)} %get-tuple-element.210.refs_3_, ...), custom_call_target="tpu_custom_call" | custom-call | flops 469762048 | bytes 3473408 | tf_op jit(solution)/shard_map/pallas_call | solution.py:136
  156.6 7.2 %all-to-all-start.3 = ((bf16[16,512,128]{2,1,0:T(8,128)(2,1)}), bf16[16,512,128]{2,1,0:T(8,128)(2,1)}, u32[]{:S(2)}, u32[]{:S(2)}) async-start(bf16[16,512,128]{2,1,0:T(8,128)(2,1)} %copy-done.4), calls=%async_computation.3 | async-start | bytes 4194304 | tf_op jit(solution)/shard_map/all_to_all | solution.py:559
  163.8 2.0 collective-permute-start.27
  165.8 5.7 %collective-permute-done.27.refs_1_ = bf16[112,1024]{1,0:T(8,128)(2,1)S(1)} collective-permute-done((bf16[112,1024]{1,0:T(8,128)(2,1)}, bf16[112,1024]{1,0:T(8,128)(2,1)S(1)}, u32[]{:S(2)}, u32[]{:S(2)}) %collective-permute-start.27) | collective-permute-done | bytes 229408 | tf_op jit(solution)/shard_map/ppermute | solution.py:43
  178.6 2.5 shard_map.277
  185.6 2.5 shard_map.280
  189.4 2.0 all-to-all-done.3
  191.4 5.3 %all-to-all-start.4 = ((bf16[16,368,128]{2,1,0:T(8,128)(2,1)}), bf16[16,368,128]{2,1,0:T(8,128)(2,1)}, u32[]{:S(2)}, u32[]{:S(2)}) async-start(bf16[16,368,128]{2,1,0:T(8,128)(2,1)} %copy-done.14), calls=%async_computation.4 | async-start | bytes 3014656 | tf_op jit(solution)/shard_map/all_to_all | solution.py:559
  196.7 2.0 collective-permute-start.34
  199.1 3.6 %collective-permute-done.34.refs_1_ = bf16[112,512]{1,0:T(8,128)(2,1)S(1)} collective-permute-done((bf16[112,512]{1,0:T(8,128)(2,1)S(1)}, bf16[112,512]{1,0:T(8,128)(2,1)S(1)}, u32[]{:S(2)}, u32[]{:S(2)}) %collective-permute-start.34) | collective-permute-done | bytes 114720 | tf_op jit(solution)/shard_map/ppermute | solution.py:43
  214.7 2.3 shard_map.285
  219.5 7.4 %all-to-all-start.5 = ((bf16[16,512,128]{2,1,0:T(8,128)(2,1)}), bf16[16,512,128]{2,1,0:T(8,128)(2,1)}, u32[]{:S(2)}, u32[]{:S(2)}) async-start(bf16[16,512,128]{2,1,0:T(8,128)(2,1)} %copy-done.3), calls=%async_computation.5 | async-start | bytes 4194304 | tf_op jit(solution)/shard_map/all_to_all | solution.py:559
  228.3 4.6 %collective-permute-done.40.refs_1_ = bf16[112,512]{1,0:T(8,128)(2,1)S(1)} collective-permute-done((bf16[112,512]{1,0:T(8,128)(2,1)S(1)}, bf16[112,512]{1,0:T(8,128)(2,1)S(1)}, u32[]{:S(2)}, u32[]{:S(2)}) %collective-permute-start.40) | collective-permute-done | bytes 114720 | tf_op jit(solution)/shard_map/ppermute | solution.py:43
  235.2 3.6 %shard_map.287 = (bf16[224,384]{1,0:T(8,128)(2,1)S(1)}, f32[1,384]{1,0:T(1,128)S(1)}, f32[112,1024]{1,0:T(8,128)S(1)}, bf16[112,1024]{1,0:T(8,128)(2,1)S(1)}) custom-call(s32[6]{0:T(128)S(1)} %stack.45.refs_0_.place.meta, bf16[112,1024]{1,0:T(8,128)(2,1)S(1)} %get-tuple-element.265.refs_1_.refs_4_, ...), custom_call_target="tpu_custom_call" | custom-call | flops 234881024 | bytes 3589656 | tf_op jit(solution)/shard_map/pallas_call | solution.py:136
  241.0 1.9 collective-permute-start.45
  242.9 1.9 shard_map.290
  247.6 1.9 collective-permute-start.46
  249.5 4.2 %collective-permute-done.46.refs_2_ = bf16[112,512]{1,0:T(8,128)(2,1)S(1)} collective-permute-done((bf16[112,512]{1,0:T(8,128)(2,1)S(1)}, bf16[112,512]{1,0:T(8,128)(2,1)S(1)}, u32[]{:S(2)}, u32[]{:S(2)}) %collective-permute-start.46) | collective-permute-done | bytes 114720 | tf_op jit(solution)/shard_map/ppermute | solution.py:43
  259.8 7.2 %all-to-all-start.6 = ((bf16[16,400,128]{2,1,0:T(8,128)(2,1)}), bf16[16,400,128]{2,1,0:T(8,128)(2,1)S(1)}, u32[]{:S(2)}, u32[]{:S(2)}) async-start(bf16[16,400,128]{2,1,0:T(8,128)(2,1)} %shard_map.292), calls=%async_computation.6 | async-start | bytes 3276800 | tf_op jit(solution)/shard_map/all_to_all | solution.py:559
  267.1 1.9 convert_reduce_fusion.1
  269.0 2.6 shard_map.293
  271.6 1.9 convert_reduce_fusion
  276.4 13.9 %all-to-all-done.6.received = bf16[16,400,128]{2,1,0:T(8,128)(2,1)S(1)} async-done(((bf16[16,400,128]{2,1,0:T(8,128)(2,1)}), bf16[16,400,128]{2,1,0:T(8,128)(2,1)S(1)}, u32[]{:S(2)}, u32[]{:S(2)}) %all-to-all-start.6) | async-done | bytes 1638432 | tf_op jit(solution)/shard_map/all_to_all | solution.py:559
  290.3 1.8 shard_map.294
  (266 shorter events, 96.4 us)
Async XLA Ops:
  4.3 35.8 %all-to-all-start = ((bf16[16,512,128]{2,1,0:T(8,128)(2,1)}), bf16[16,512,128]{2,1,0:T(8,128)(2,1)}, u32[]{:S(2)}, u32[]{:S(2)}) async-start(bf16[16,512,128]{2,1,0:T(8,128)(2,1)} %shard_map.256), calls=%async_computation | async-start | bytes 4194304 | tf_op jit(solution)/shard_map/all_to_all | solution.py:559
  40.1 44.7 %all-to-all-start.1 = ((bf16[16,768,128]{2,1,0:T(8,128)(2,1)}), bf16[16,768,128]{2,1,0:T(8,128)(2,1)S(1)}, u32[]{:S(2)}, u32[]{:S(2)}) async-start(bf16[16,768,128]{2,1,0:T(8,128)(2,1)} %copy-done), calls=%async_computation.1 | async-start | bytes 6291456 | tf_op jit(solution)/shard_map/all_to_all | solution.py:559
  50.1 8.0 %collective-permute-start.3 = (bf16[2,256,128]{2,1,0:T(8,128)(2,1)S(1)}, bf16[2,256,128]{2,1,0:T(8,128)(2,1)S(1)}, u32[]{:S(2)}, u32[]{:S(2)}) collective-permute-start(bf16[2,256,128]{2,1,0:T(8,128)(2,1)S(1)} %fusion.5.refs_1_), channel_id=1, source_target_pairs={{0,4},{2,6},{4,0},{6,2},{1,5},{3,7},{5,1},{7,3},{8,12},{10,14},{12... | collective-permute-start | bytes 393224 | tf_op jit(solution)/shard_map/ppermute | solution.py:29
  54.1 7.4 %collective-permute-start.2 = (bf16[2,256,128]{2,1,0:T(8,128)(2,1)S(1)}, bf16[2,256,128]{2,1,0:T(8,128)(2,1)S(1)}, u32[]{:S(2)}, u32[]{:S(2)}) collective-permute-start(bf16[2,256,128]{2,1,0:T(8,128)(2,1)S(1)} %fusion.5.refs_1_), channel_id=1, source_target_pairs={{0,6},{2,0},{4,2},{6,4},{1,7},{3,1},{5,3},{7,5},{8,14},{10,8},{12,... | collective-permute-start | bytes 393224 | tf_op jit(solution)/shard_map/ppermute | solution.py:29
  54.8 6.7 %collective-permute-start.1 = (bf16[2,256,128]{2,1,0:T(8,128)(2,1)S(1)}, bf16[2,256,128]{2,1,0:T(8,128)(2,1)S(1)}, u32[]{:S(2)}, u32[]{:S(2)}) collective-permute-start(bf16[2,256,128]{2,1,0:T(8,128)(2,1)S(1)} %fusion.5.refs_1_), channel_id=1, source_target_pairs={{0,2},{2,4},{4,6},{6,0},{1,3},{3,5},{5,7},{7,1},{8,10},{10,12},{12... | collective-permute-start | bytes 393224 | tf_op jit(solution)/shard_map/ppermute | solution.py:29
  62.4 1.6 collective-permute-start.5
  67.2 1.6 collective-permute-start.6
  68.8 5.3 %collective-permute-start.7 = (bf16[112,512]{1,0:T(8,128)(2,1)S(1)}, bf16[112,512]{1,0:T(8,128)(2,1)S(1)}, u32[]{:S(2)}, u32[]{:S(2)}) collective-permute-start(bf16[112,512]{1,0:T(8,128)(2,1)S(1)} %get-tuple-element.172.refs_0_), channel_id=1, source_target_pairs={{0,2},{2,0},{4,6},{6,4},{1,3},{3,1},{5,7},{7,5},{8,10},{10,8},{12,... | collective-permute-start | bytes 344072 | tf_op jit(solution)/shard_map/ppermute | solution.py:38
  69.9 6.1 %collective-permute-start.8 = (bf16[112,512]{1,0:T(8,128)(2,1)S(1)}, bf16[112,512]{1,0:T(8,128)(2,1)S(1)}, u32[]{:S(2)}, u32[]{:S(2)}) collective-permute-start(bf16[112,512]{1,0:T(8,128)(2,1)S(1)} %get-tuple-element.173.refs_2_), channel_id=1, source_target_pairs={{0,6},{6,0},{2,4},{4,2},{1,7},{7,1},{3,5},{5,3},{8,14},{14,8},{10,... | collective-permute-start | bytes 344072 | tf_op jit(solution)/shard_map/ppermute | solution.py:39
  76.1 6.1 %collective-permute-start.9 = (bf16[112,512]{1,0:T(8,128)(2,1)S(1)}, bf16[112,512]{1,0:T(8,128)(2,1)S(1)}, u32[]{:S(2)}, u32[]{:S(2)}) collective-permute-start(bf16[112,512]{1,0:T(8,128)(2,1)S(1)} %get-tuple-element.174.refs_0_), channel_id=1, source_target_pairs={{0,6},{6,0},{2,4},{4,2},{1,7},{7,1},{3,5},{5,3},{8,14},{14,8},{10,... | collective-permute-start | bytes 344072 | tf_op jit(solution)/shard_map/ppermute | solution.py:43
  78.2 4.8 %collective-permute-start.10 = (bf16[112,512]{1,0:T(8,128)(2,1)S(1)}, bf16[112,512]{1,0:T(8,128)(2,1)S(1)}, u32[]{:S(2)}, u32[]{:S(2)}) collective-permute-start(bf16[112,512]{1,0:T(8,128)(2,1)S(1)} %get-tuple-element.175.refs_2_), channel_id=1, source_target_pairs={{0,2},{2,0},{4,6},{6,4},{1,3},{3,1},{5,7},{7,5},{8,10},{10,8},{12,... | collective-permute-start | bytes 344072 | tf_op jit(solution)/shard_map/ppermute | solution.py:44
  84.8 51.1 %all-to-all-start.2 = ((bf16[16,512,128]{2,1,0:T(8,128)(2,1)}), bf16[16,512,128]{2,1,0:T(8,128)(2,1)}, u32[]{:S(2)}, u32[]{:S(2)}) async-start(bf16[16,512,128]{2,1,0:T(8,128)(2,1)} %copy-done.1), calls=%async_computation.2 | async-start | bytes 4194304 | tf_op jit(solution)/shard_map/all_to_all | solution.py:559
  92.1 1.8 collective-permute-start.11
  98.3 5.3 %collective-permute-start.13 = (bf16[112,512]{1,0:T(8,128)(2,1)S(1)}, bf16[112,512]{1,0:T(8,128)(2,1)S(1)}, u32[]{:S(2)}, u32[]{:S(2)}) collective-permute-start(bf16[112,512]{1,0:T(8,128)(2,1)S(1)} %get-tuple-element.183.refs_0_), channel_id=1, source_target_pairs={{0,2},{2,0},{4,6},{6,4},{1,3},{3,1},{5,7},{7,5},{8,10},{10,8},{12,... | collective-permute-start | bytes 344072 | tf_op jit(solution)/shard_map/ppermute | solution.py:38
  99.3 6.1 %collective-permute-start.14 = (bf16[112,512]{1,0:T(8,128)(2,1)S(1)}, bf16[112,512]{1,0:T(8,128)(2,1)S(1)}, u32[]{:S(2)}, u32[]{:S(2)}) collective-permute-start(bf16[112,512]{1,0:T(8,128)(2,1)S(1)} %get-tuple-element.184.refs_2_), channel_id=1, source_target_pairs={{0,6},{6,0},{2,4},{4,2},{1,7},{7,1},{3,5},{5,3},{8,14},{14,8},{10,... | collective-permute-start | bytes 344072 | tf_op jit(solution)/shard_map/ppermute | solution.py:39
  105.5 6.1 %collective-permute-start.15 = (bf16[112,512]{1,0:T(8,128)(2,1)S(1)}, bf16[112,512]{1,0:T(8,128)(2,1)S(1)}, u32[]{:S(2)}, u32[]{:S(2)}) collective-permute-start(bf16[112,512]{1,0:T(8,128)(2,1)S(1)} %get-tuple-element.185.refs_0_), channel_id=1, source_target_pairs={{0,6},{6,0},{2,4},{4,2},{1,7},{7,1},{3,5},{5,3},{8,14},{14,8},{10,... | collective-permute-start | bytes 344072 | tf_op jit(solution)/shard_map/ppermute | solution.py:43
  108.1 4.8 %collective-permute-start.16 = (bf16[112,512]{1,0:T(8,128)(2,1)S(1)}, bf16[112,512]{1,0:T(8,128)(2,1)S(1)}, u32[]{:S(2)}, u32[]{:S(2)}) collective-permute-start(bf16[112,512]{1,0:T(8,128)(2,1)S(1)} %get-tuple-element.186.refs_2_), channel_id=1, source_target_pairs={{0,2},{2,0},{4,6},{6,4},{1,3},{3,1},{5,7},{7,5},{8,10},{10,8},{12,... | collective-permute-start | bytes 344072 | tf_op jit(solution)/shard_map/ppermute | solution.py:44
  113.2 1.6 collective-permute-start.17
  119.7 5.5 %collective-permute-start.19 = (bf16[112,512]{1,0:T(8,128)(2,1)S(1)}, bf16[112,512]{1,0:T(8,128)(2,1)S(1)}, u32[]{:S(2)}, u32[]{:S(2)}) collective-permute-start(bf16[112,512]{1,0:T(8,128)(2,1)S(1)} %get-tuple-element.191.refs_0_), channel_id=1, source_target_pairs={{0,2},{2,0},{4,6},{6,4},{1,3},{3,1},{5,7},{7,5},{8,10},{10,8},{12,... | collective-permute-start | bytes 344072 | tf_op jit(solution)/shard_map/ppermute | solution.py:38
  120.0 6.5 %collective-permute-start.20 = (bf16[112,512]{1,0:T(8,128)(2,1)S(1)}, bf16[112,512]{1,0:T(8,128)(2,1)S(1)}, u32[]{:S(2)}, u32[]{:S(2)}) collective-permute-start(bf16[112,512]{1,0:T(8,128)(2,1)S(1)} %get-tuple-element.192.refs_2_), channel_id=1, source_target_pairs={{0,6},{6,0},{2,4},{4,2},{1,7},{7,1},{3,5},{5,3},{8,14},{14,8},{10,... | collective-permute-start | bytes 344072 | tf_op jit(solution)/shard_map/ppermute | solution.py:39
  126.5 6.1 %collective-permute-start.21 = (bf16[112,512]{1,0:T(8,128)(2,1)S(1)}, bf16[112,512]{1,0:T(8,128)(2,1)S(1)}, u32[]{:S(2)}, u32[]{:S(2)}) collective-permute-start(bf16[112,512]{1,0:T(8,128)(2,1)S(1)} %get-tuple-element.193.refs_0_), channel_id=1, source_target_pairs={{0,6},{6,0},{2,4},{4,2},{1,7},{7,1},{3,5},{5,3},{8,14},{14,8},{10,... | collective-permute-start | bytes 344072 | tf_op jit(solution)/shard_map/ppermute | solution.py:43
  127.8 4.8 %collective-permute-start.22 = (bf16[112,512]{1,0:T(8,128)(2,1)S(1)}, bf16[112,512]{1,0:T(8,128)(2,1)S(1)}, u32[]{:S(2)}, u32[]{:S(2)}) collective-permute-start(bf16[112,512]{1,0:T(8,128)(2,1)S(1)} %get-tuple-element.194.refs_2_), channel_id=1, source_target_pairs={{0,2},{2,0},{4,6},{6,4},{1,3},{3,1},{5,7},{7,5},{8,10},{10,8},{12,... | collective-permute-start | bytes 344072 | tf_op jit(solution)/shard_map/ppermute | solution.py:44
  134.4 6.0 %collective-permute-start.4 = (bf16[112,1024]{1,0:T(8,128)(2,1)S(1)}, bf16[112,1024]{1,0:T(8,128)(2,1)}, u32[]{:S(2)}, u32[]{:S(2)}) collective-permute-start(bf16[112,1024]{1,0:T(8,128)(2,1)S(1)} %get-tuple-element.165.refs_0_.refs_4_.refs_3_), channel_id=1, source_target_pairs={{0,1},{1,0},{2,3},{3,2},{4,5},{5,4},{6,7},{7,6},{8,9},{9,8},{10,11... | collective-permute-start | bytes 688136 | tf_op jit(solution)/shard_map/ppermute | solution.py:24
  144.0 1.9 collective-permute-start.24
  146.0 7.7 %collective-permute-start.25 = (bf16[112,1024]{1,0:T(8,128)(2,1)S(1)}, bf16[112,1024]{1,0:T(8,128)(2,1)S(1)}, u32[]{:S(2)}, u32[]{:S(2)}) collective-permute-start(bf16[112,1024]{1,0:T(8,128)(2,1)S(1)} %get-tuple-element.205.refs_0_), channel_id=1, source_target_pairs={{0,2},{2,0},{4,6},{6,4},{1,3},{3,1},{5,7},{7,5},{8,10},{10,8},{12,... | collective-permute-start | bytes 688136 | tf_op jit(solution)/shard_map/ppermute | solution.py:38
  146.1 8.9 %collective-permute-start.26 = (bf16[112,1024]{1,0:T(8,128)(2,1)S(1)}, bf16[112,1024]{1,0:T(8,128)(2,1)S(1)}, u32[]{:S(2)}, u32[]{:S(2)}) collective-permute-start(bf16[112,1024]{1,0:T(8,128)(2,1)S(1)} %get-tuple-element.206.refs_2_), channel_id=1, source_target_pairs={{0,6},{6,0},{2,4},{4,2},{1,7},{7,1},{3,5},{5,3},{8,14},{14,8},{10,... | collective-permute-start | bytes 688136 | tf_op jit(solution)/shard_map/ppermute | solution.py:39
  156.6 34.9 %all-to-all-start.3 = ((bf16[16,512,128]{2,1,0:T(8,128)(2,1)}), bf16[16,512,128]{2,1,0:T(8,128)(2,1)}, u32[]{:S(2)}, u32[]{:S(2)}) async-start(bf16[16,512,128]{2,1,0:T(8,128)(2,1)} %copy-done.4), calls=%async_computation.3 | async-start | bytes 4194304 | tf_op jit(solution)/shard_map/all_to_all | solution.py:559
  163.8 7.7 %collective-permute-start.27 = (bf16[112,1024]{1,0:T(8,128)(2,1)}, bf16[112,1024]{1,0:T(8,128)(2,1)S(1)}, u32[]{:S(2)}, u32[]{:S(2)}) collective-permute-start(bf16[112,1024]{1,0:T(8,128)(2,1)} %copy-done.43), channel_id=1, source_target_pairs={{0,6},{6,0},{2,4},{4,2},{1,7},{7,1},{3,5},{5,3},{8,14},{14,8},{10,... | collective-permute-start | bytes 688136 | tf_op jit(solution)/shard_map/ppermute | solution.py:43
  165.8 6.2 %collective-permute-start.28 = (bf16[112,1024]{1,0:T(8,128)(2,1)}, bf16[112,1024]{1,0:T(8,128)(2,1)S(1)}, u32[]{:S(2)}, u32[]{:S(2)}) collective-permute-start(bf16[112,1024]{1,0:T(8,128)(2,1)} %copy-done.45), channel_id=1, source_target_pairs={{0,2},{2,0},{4,6},{6,4},{1,3},{3,1},{5,7},{7,5},{8,10},{10,8},{12,... | collective-permute-start | bytes 688136 | tf_op jit(solution)/shard_map/ppermute | solution.py:44
  181.1 1.6 collective-permute-start.30
  182.7 6.5 %collective-permute-start.31 = (bf16[112,512]{1,0:T(8,128)(2,1)S(1)}, bf16[112,512]{1,0:T(8,128)(2,1)S(1)}, u32[]{:S(2)}, u32[]{:S(2)}) collective-permute-start(bf16[112,512]{1,0:T(8,128)(2,1)S(1)} %get-tuple-element.230.refs_0_), channel_id=1, source_target_pairs={{0,2},{2,0},{4,6},{6,4},{1,3},{3,1},{5,7},{7,5},{8,10},{10,8},{12,... | collective-permute-start | bytes 344072 | tf_op jit(solution)/shard_map/ppermute | solution.py:38
  183.1 6.3 %collective-permute-start.32 = (bf16[112,512]{1,0:T(8,128)(2,1)S(1)}, bf16[112,512]{1,0:T(8,128)(2,1)S(1)}, u32[]{:S(2)}, u32[]{:S(2)}) collective-permute-start(bf16[112,512]{1,0:T(8,128)(2,1)S(1)} %get-tuple-element.231.refs_2_), channel_id=1, source_target_pairs={{0,6},{6,0},{2,4},{4,2},{1,7},{7,1},{3,5},{5,3},{8,14},{14,8},{10,... | collective-permute-start | bytes 344072 | tf_op jit(solution)/shard_map/ppermute | solution.py:39
  191.4 28.0 %all-to-all-start.4 = ((bf16[16,368,128]{2,1,0:T(8,128)(2,1)}), bf16[16,368,128]{2,1,0:T(8,128)(2,1)}, u32[]{:S(2)}, u32[]{:S(2)}) async-start(bf16[16,368,128]{2,1,0:T(8,128)(2,1)} %copy-done.14), calls=%async_computation.4 | async-start | bytes 3014656 | tf_op jit(solution)/shard_map/all_to_all | solution.py:559
  196.7 6.0 %collective-permute-start.34 = (bf16[112,512]{1,0:T(8,128)(2,1)S(1)}, bf16[112,512]{1,0:T(8,128)(2,1)S(1)}, u32[]{:S(2)}, u32[]{:S(2)}) collective-permute-start(bf16[112,512]{1,0:T(8,128)(2,1)S(1)} %get-tuple-element.240.refs_0_), channel_id=1, source_target_pairs={{0,6},{6,0},{2,4},{4,2},{1,7},{7,1},{3,5},{5,3},{8,14},{14,8},{10,... | collective-permute-start | bytes 344072 | tf_op jit(solution)/shard_map/ppermute | solution.py:43
  198.7 4.8 %collective-permute-start.35 = (bf16[112,512]{1,0:T(8,128)(2,1)S(1)}, bf16[112,512]{1,0:T(8,128)(2,1)S(1)}, u32[]{:S(2)}, u32[]{:S(2)}) collective-permute-start(bf16[112,512]{1,0:T(8,128)(2,1)S(1)} %get-tuple-element.241.refs_2_), channel_id=1, source_target_pairs={{0,2},{2,0},{4,6},{6,4},{1,3},{3,1},{5,7},{7,5},{8,10},{10,8},{12,... | collective-permute-start | bytes 344072 | tf_op jit(solution)/shard_map/ppermute | solution.py:44
  207.5 1.5 collective-permute-start.36
  211.1 1.6 collective-permute-start.37
  212.8 5.6 %collective-permute-start.38 = (bf16[112,512]{1,0:T(8,128)(2,1)S(1)}, bf16[112,512]{1,0:T(8,128)(2,1)S(1)}, u32[]{:S(2)}, u32[]{:S(2)}) collective-permute-start(bf16[112,512]{1,0:T(8,128)(2,1)S(1)} %get-tuple-element.250.refs_0_), channel_id=1, source_target_pairs={{0,2},{2,0},{4,6},{6,4},{1,3},{3,1},{5,7},{7,5},{8,10},{10,8},{12,... | collective-permute-start | bytes 344072 | tf_op jit(solution)/shard_map/ppermute | solution.py:38
  213.2 6.1 %collective-permute-start.39 = (bf16[112,512]{1,0:T(8,128)(2,1)S(1)}, bf16[112,512]{1,0:T(8,128)(2,1)S(1)}, u32[]{:S(2)}, u32[]{:S(2)}) collective-permute-start(bf16[112,512]{1,0:T(8,128)(2,1)S(1)} %get-tuple-element.251.refs_2_), channel_id=1, source_target_pairs={{0,6},{6,0},{2,4},{4,2},{1,7},{7,1},{3,5},{5,3},{8,14},{14,8},{10,... | collective-permute-start | bytes 344072 | tf_op jit(solution)/shard_map/ppermute | solution.py:39
  219.5 40.3 %all-to-all-start.5 = ((bf16[16,512,128]{2,1,0:T(8,128)(2,1)}), bf16[16,512,128]{2,1,0:T(8,128)(2,1)}, u32[]{:S(2)}, u32[]{:S(2)}) async-start(bf16[16,512,128]{2,1,0:T(8,128)(2,1)} %copy-done.3), calls=%async_computation.5 | async-start | bytes 4194304 | tf_op jit(solution)/shard_map/all_to_all | solution.py:559
  226.8 6.0 %collective-permute-start.40 = (bf16[112,512]{1,0:T(8,128)(2,1)S(1)}, bf16[112,512]{1,0:T(8,128)(2,1)S(1)}, u32[]{:S(2)}, u32[]{:S(2)}) collective-permute-start(bf16[112,512]{1,0:T(8,128)(2,1)S(1)} %get-tuple-element.262.refs_0_), channel_id=1, source_target_pairs={{0,6},{6,0},{2,4},{4,2},{1,7},{7,1},{3,5},{5,3},{8,14},{14,8},{10,... | collective-permute-start | bytes 344072 | tf_op jit(solution)/shard_map/ppermute | solution.py:43
  228.3 4.8 %collective-permute-start.41 = (bf16[112,512]{1,0:T(8,128)(2,1)S(1)}, bf16[112,512]{1,0:T(8,128)(2,1)S(1)}, u32[]{:S(2)}, u32[]{:S(2)}) collective-permute-start(bf16[112,512]{1,0:T(8,128)(2,1)S(1)} %get-tuple-element.263.refs_2_), channel_id=1, source_target_pairs={{0,2},{2,0},{4,6},{6,4},{1,3},{3,1},{5,7},{7,5},{8,10},{10,8},{12,... | collective-permute-start | bytes 344072 | tf_op jit(solution)/shard_map/ppermute | solution.py:44
  233.6 1.6 collective-permute-start.42
  240.9 5.3 %collective-permute-start.44 = (bf16[112,512]{1,0:T(8,128)(2,1)S(1)}, bf16[112,512]{1,0:T(8,128)(2,1)S(1)}, u32[]{:S(2)}, u32[]{:S(2)}) collective-permute-start(bf16[112,512]{1,0:T(8,128)(2,1)S(1)} %get-tuple-element.272.refs_0_), channel_id=1, source_target_pairs={{0,2},{2,0},{4,6},{6,4},{1,3},{3,1},{5,7},{7,5},{8,10},{10,8},{12,... | collective-permute-start | bytes 344072 | tf_op jit(solution)/shard_map/ppermute | solution.py:38
  241.0 6.5 %collective-permute-start.45 = (bf16[112,512]{1,0:T(8,128)(2,1)S(1)}, bf16[112,512]{1,0:T(8,128)(2,1)S(1)}, u32[]{:S(2)}, u32[]{:S(2)}) collective-permute-start(bf16[112,512]{1,0:T(8,128)(2,1)S(1)} %get-tuple-element.273.refs_2_), channel_id=1, source_target_pairs={{0,6},{6,0},{2,4},{4,2},{1,7},{7,1},{3,5},{5,3},{8,14},{14,8},{10,... | collective-permute-start | bytes 344072 | tf_op jit(solution)/shard_map/ppermute | solution.py:39
  247.6 6.1 %collective-permute-start.46 = (bf16[112,512]{1,0:T(8,128)(2,1)S(1)}, bf16[112,512]{1,0:T(8,128)(2,1)S(1)}, u32[]{:S(2)}, u32[]{:S(2)}) collective-permute-start(bf16[112,512]{1,0:T(8,128)(2,1)S(1)} %get-tuple-element.280.refs_1_), channel_id=1, source_target_pairs={{0,6},{6,0},{2,4},{4,2},{1,7},{7,1},{3,5},{5,3},{8,14},{14,8},{10,... | collective-permute-start | bytes 344072 | tf_op jit(solution)/shard_map/ppermute | solution.py:43
  249.5 4.8 %collective-permute-start.47 = (bf16[112,512]{1,0:T(8,128)(2,1)S(1)}, bf16[112,512]{1,0:T(8,128)(2,1)S(1)}, u32[]{:S(2)}, u32[]{:S(2)}) collective-permute-start(bf16[112,512]{1,0:T(8,128)(2,1)S(1)} %get-tuple-element.281.refs_3_), channel_id=1, source_target_pairs={{0,2},{2,0},{4,6},{6,4},{1,3},{3,1},{5,7},{7,5},{8,10},{10,8},{12,... | collective-permute-start | bytes 344072 | tf_op jit(solution)/shard_map/ppermute | solution.py:44
  259.8 30.5 %all-to-all-start.6 = ((bf16[16,400,128]{2,1,0:T(8,128)(2,1)}), bf16[16,400,128]{2,1,0:T(8,128)(2,1)S(1)}, u32[]{:S(2)}, u32[]{:S(2)}) async-start(bf16[16,400,128]{2,1,0:T(8,128)(2,1)} %shard_map.292), calls=%async_computation.6 | async-start | bytes 3276800 | tf_op jit(solution)/shard_map/all_to_all | solution.py:559
  (78 other events, 633.3 us)

commit v4 on v3

--- a/solution.py
+++ b/solution.py
@@ -805,7 +805,7 @@
         out_specs=[pl.BlockSpec(memory_space=pltpu.HBM)],
         scratch_shapes=[pltpu.VMEM((16, 144, 128), BF), pltpu.SemaphoreType.DMA(())],
         input_output_aliases={1: 0},
-        compiler_params=pltpu.CompilerParams(vmem_limit_bytes=56 * 2**20),
+        compiler_params=pltpu.CompilerParams(vmem_limit_bytes=16 * 2**20),
     )(
         place,
         attention_grad,

time: 294 us -> 292 us (level)
    unnamed x138 -> x122, local copies, waits for them, and re-layouts: 27.8 us -> 26.1 us
  transfers between devices with their start and end apart: 57 -> 57, of which waited for: 47 -> 46; matrix products, arithmetic and copies ran while one was open for 4% -> 4% of each run, Pallas kernels for 13% -> 12%
where the time goes in v4:
time: 292 us; the launch traced here: 291 us
  waiting for transfers between devices  120 us (41%)
  starting transfers between devices  85.8 us (29%)
  Pallas kernels  45.5 us (16%)
  local copies, waits for them, and re-layouts  28.3 us (10%)
  other arithmetic  9.08 us (3%)
    all_to_all x7, starting transfers between devices, exchange(): return lax.all_to_all(chunks, DP, 0, 0)  47.3 us
    pallas_call x38, Pallas kernels, run(): pl.pallas_call(body, out_shape=list(outs) + more, in_specs=specs, out_spe...  40.4 us
    all_to_all x7, waiting for transfers between devices, exchange(): return lax.all_to_all(chunks, DP, 0, 0)  38.3 us
    ppermute x7, waiting for transfers between devices, total(): got_left = lax.ppermute(left, 'z', PAIR_B)  30.2 us
    unnamed x122, local copies, waits for them, and re-layouts  26.1 us
    ppermute x19, waiting for transfers between devices, core_swap(): return lax.ppermute(block, 'c', SWAP)  22.5 us
    ppermute x7, starting transfers between devices, total(): got_left = lax.ppermute(left, 'z', PAIR_B)  13.4 us
    ppermute x7, starting transfers between devices, total(): got_right = lax.ppermute(right, 'z', PAIR_B)  12.6 us
  transfers between devices with their start and end apart: 57, of which 46 were waited for; matrix products, arithmetic and copies ran while one was open for 4% of the time, Pallas kernels for 12%

profile of v4, /device:TPU:4, one launch (start us, length us, event | category | flops | bytes accessed | tf_op | source)
XLA Modules:
  0.0 290.7 jit_solution(9115765303843880180)
XLA Ops:
  0.6 3.7 %shard_map.256 = bf16[16,512,128]{2,1,0:T(8,128)(2,1)} custom-call(s32[8]{0:T(128)} %refs_0_.3, bf16[3,64,197]{2,1,0:T(8,128)(2,1)} %bitcast.34, bf16[3,64,197]{2,1,0:T(8,128)(2,1)} %bitcast.35, f32[2,64]{1,0:T(2,128)} %refs_3_.3, f32[2,64]{1,0:T(2,128)} %refs_4_.1, f32[2,64]{1,0:T(2,128)} %refs_5_.1, f32[2,64]{1,0:T(2,128)} %refs_6_.1, f32[2,64]{1,0:T(2,128)} %refs_7_.1, ...), custom_call_target="tpu_custom_call" | custom-call | bytes 2385696 | tf_op jit(solution)/shard_map/pallas_call | solution.py:136
  4.3 7.6 %all-to-all-start = ((bf16[16,512,128]{2,1,0:T(8,128)(2,1)}), bf16[16,512,128]{2,1,0:T(8,128)(2,1)}, u32[]{:S(2)}, u32[]{:S(2)}) async-start(bf16[16,512,128]{2,1,0:T(8,128)(2,1)} %shard_map.256), calls=%async_computation | async-start | bytes 4194304 | tf_op jit(solution)/shard_map/all_to_all | solution.py:559
  17.8 22.4 %all-to-all-done.refs_3_.refs_4_ = bf16[16,512,128]{2,1,0:T(8,128)(2,1)} async-done(((bf16[16,512,128]{2,1,0:T(8,128)(2,1)}), bf16[16,512,128]{2,1,0:T(8,128)(2,1)}, u32[]{:S(2)}, u32[]{:S(2)}) %all-to-all-start) | async-done | bytes 2097184 | tf_op jit(solution)/shard_map/all_to_all | solution.py:559
  40.2 5.4 %all-to-all-start.1 = ((bf16[16,768,128]{2,1,0:T(8,128)(2,1)}), bf16[16,768,128]{2,1,0:T(8,128)(2,1)S(1)}, u32[]{:S(2)}, u32[]{:S(2)}) async-start(bf16[16,768,128]{2,1,0:T(8,128)(2,1)} %copy-done), calls=%async_computation.1 | async-start | bytes 6291456 | tf_op jit(solution)/shard_map/all_to_all | solution.py:559
  50.2 4.0 %collective-permute-start.3 = (bf16[2,256,128]{2,1,0:T(8,128)(2,1)S(1)}, bf16[2,256,128]{2,1,0:T(8,128)(2,1)S(1)}, u32[]{:S(2)}, u32[]{:S(2)}) collective-permute-start(bf16[2,256,128]{2,1,0:T(8,128)(2,1)S(1)} %fusion.5.refs_1_), channel_id=1, source_target_pairs={{0,4},{2,6},{4,0},{6,2},{1,5},{3,7},{5,1},{7,3},{8,12},{10,14},{12... | collective-permute-start | bytes 393224 | tf_op jit(solution)/shard_map/ppermute | solution.py:29
  56.1 2.0 collective-permute-done.3.refs_4_
  58.2 3.4 %collective-permute-done.2.refs_3_ = bf16[2,256,128]{2,1,0:T(8,128)(2,1)S(1)} collective-permute-done((bf16[2,256,128]{2,1,0:T(8,128)(2,1)S(1)}, bf16[2,256,128]{2,1,0:T(8,128)(2,1)S(1)}, u32[]{:S(2)}, u32[]{:S(2)}) %collective-permute-start.2) | collective-permute-done | bytes 131104 | tf_op jit(solution)/shard_map/ppermute | solution.py:29
  64.0 3.2 %shard_map.258 = (bf16[224,384]{1,0:T(8,128)(2,1)S(1)}, bf16[224,128]{1,0:T(8,128)(2,1)S(1)}, f32[112,1024]{1,0:T(8,128)S(1)}, bf16[112,1024]{1,0:T(8,128)(2,1)S(1)}) custom-call(s32[6]{0:T(128)S(1)} %stack.45.refs_0_.place.meta, bf16[112,1024]{1,0:T(8,128)(2,1)S(1)} %get-tuple-element.168.refs_1_.refs_0_, ...), custom_call_target="tpu_custom_call" | custom-call | flops 234881024 | bytes 3481624 | tf_op jit(solution)/shard_map/pallas_call | solution.py:136
  69.9 2.1 collective-permute-start.8
  72.0 2.2 collective-permute-done.7.refs_1_
  74.1 1.9 collective-permute-done.8.refs_3_
  76.1 2.1 collective-permute-start.9
  78.3 3.9 %collective-permute-done.9.refs_1_ = bf16[112,512]{1,0:T(8,128)(2,1)S(1)} collective-permute-done((bf16[112,512]{1,0:T(8,128)(2,1)S(1)}, bf16[112,512]{1,0:T(8,128)(2,1)S(1)}, u32[]{:S(2)}, u32[]{:S(2)}) %collective-permute-start.9) | collective-permute-done | bytes 114720 | tf_op jit(solution)/shard_map/ppermute | solution.py:43
  84.9 7.2 %all-to-all-start.2 = ((bf16[16,512,128]{2,1,0:T(8,128)(2,1)}), bf16[16,512,128]{2,1,0:T(8,128)(2,1)}, u32[]{:S(2)}, u32[]{:S(2)}) async-start(bf16[16,512,128]{2,1,0:T(8,128)(2,1)} %copy-done.1), calls=%async_computation.2 | async-start | bytes 4194304 | tf_op jit(solution)/shard_map/all_to_all | solution.py:559
  99.3 2.5 collective-permute-start.14
  103.6 1.9 collective-permute-done.14.refs_3_
  105.5 2.6 collective-permute-start.15
  108.1 3.5 %collective-permute-done.15.refs_1_ = bf16[112,512]{1,0:T(8,128)(2,1)S(1)} collective-permute-done((bf16[112,512]{1,0:T(8,128)(2,1)S(1)}, bf16[112,512]{1,0:T(8,128)(2,1)S(1)}, u32[]{:S(2)}, u32[]{:S(2)}) %collective-permute-start.15) | collective-permute-done | bytes 114720 | tf_op jit(solution)/shard_map/ppermute | solution.py:43
  114.8 2.0 shard_map.266
  121.3 3.9 %collective-permute-done.19.refs_1_ = bf16[112,512]{1,0:T(8,128)(2,1)S(1)} collective-permute-done((bf16[112,512]{1,0:T(8,128)(2,1)S(1)}, bf16[112,512]{1,0:T(8,128)(2,1)S(1)}, u32[]{:S(2)}, u32[]{:S(2)}) %collective-permute-start.19) | collective-permute-done | bytes 114720 | tf_op jit(solution)/shard_map/ppermute | solution.py:38
  127.9 4.8 %collective-permute-done.21.refs_1_ = bf16[112,512]{1,0:T(8,128)(2,1)S(1)} collective-permute-done((bf16[112,512]{1,0:T(8,128)(2,1)S(1)}, bf16[112,512]{1,0:T(8,128)(2,1)S(1)}, u32[]{:S(2)}, u32[]{:S(2)}) %collective-permute-start.21) | collective-permute-done | bytes 114720 | tf_op jit(solution)/shard_map/ppermute | solution.py:43
  137.8 2.6 shard_map.270
  140.4 3.6 %shard_map.271 = (bf16[224,512]{1,0:T(8,128)(2,1)S(1)}, f32[1,512]{1,0:T(1,128)S(1)}, f32[112,2048]{1,0:T(8,128)S(1)}, bf16[112,2048]{1,0:T(8,128)(2,1)S(1)}) custom-call(bf16[112,1024]{1,0:T(8,128)(2,1)S(1)} %get-tuple-element.165.refs_0_.refs_4_.refs_3_, bf16[112,1024]{1,0:T(8,128)(2,1)} %collective-permute-done.4.refs_1_.refs_5_, ...), custom_call_target="tpu_custom_call" | custom-call | flops 469762048 | bytes 5310464 | tf_op jit(solution)/shard_map/pallas_call | solution.py:136
  146.1 2.1 collective-permute-start.26
  148.2 3.2 %shard_map.274 = (bf16[16,512,128]{2,1,0:T(8,128)(2,1)}, bf16[16,512,128]{2,1,0:T(8,128)(2,1)S(1)}) custom-call(bf16[112,1024]{1,0:T(8,128)(2,1)S(1)} %copy-done.39, bf16[112,1024]{1,0:T(8,128)(2,1)S(1)} %copy-done.42, bf16[224,512]{1,0:T(8,128)(2,1)S(1)} %get-tuple-element.209.refs_2_, bf16[224,512]{1,0:T(8,128)(2,1)S(1)} %get-tuple-element.210.refs_3_, ...), custom_call_target="tpu_custom_call" | custom-call | flops 469762048 | bytes 3473408 | tf_op jit(solution)/shard_map/pallas_call | solution.py:136
  156.6 7.2 %all-to-all-start.3 = ((bf16[16,512,128]{2,1,0:T(8,128)(2,1)}), bf16[16,512,128]{2,1,0:T(8,128)(2,1)}, u32[]{:S(2)}, u32[]{:S(2)}) async-start(bf16[16,512,128]{2,1,0:T(8,128)(2,1)} %copy-done.4), calls=%async_computation.3 | async-start | bytes 4194304 | tf_op jit(solution)/shard_map/all_to_all | solution.py:559
  163.8 2.0 collective-permute-start.27
  165.8 5.7 %collective-permute-done.27.refs_1_ = bf16[112,1024]{1,0:T(8,128)(2,1)S(1)} collective-permute-done((bf16[112,1024]{1,0:T(8,128)(2,1)}, bf16[112,1024]{1,0:T(8,128)(2,1)S(1)}, u32[]{:S(2)}, u32[]{:S(2)}) %collective-permute-start.27) | collective-permute-done | bytes 229408 | tf_op jit(solution)/shard_map/ppermute | solution.py:43
  178.6 2.5 shard_map.277
  185.5 2.6 shard_map.280
  189.4 2.1 all-to-all-done.3
  191.4 5.3 %all-to-all-start.4 = ((bf16[16,368,128]{2,1,0:T(8,128)(2,1)}), bf16[16,368,128]{2,1,0:T(8,128)(2,1)}, u32[]{:S(2)}, u32[]{:S(2)}) async-start(bf16[16,368,128]{2,1,0:T(8,128)(2,1)} %copy-done.14), calls=%async_computation.4 | async-start | bytes 3014656 | tf_op jit(solution)/shard_map/all_to_all | solution.py:559
  196.7 2.0 collective-permute-start.34
  199.1 3.6 %collective-permute-done.34.refs_1_ = bf16[112,512]{1,0:T(8,128)(2,1)S(1)} collective-permute-done((bf16[112,512]{1,0:T(8,128)(2,1)S(1)}, bf16[112,512]{1,0:T(8,128)(2,1)S(1)}, u32[]{:S(2)}, u32[]{:S(2)}) %collective-permute-start.34) | collective-permute-done | bytes 114720 | tf_op jit(solution)/shard_map/ppermute | solution.py:43
  214.7 2.3 shard_map.285
  219.5 7.4 %all-to-all-start.5 = ((bf16[16,512,128]{2,1,0:T(8,128)(2,1)}), bf16[16,512,128]{2,1,0:T(8,128)(2,1)}, u32[]{:S(2)}, u32[]{:S(2)}) async-start(bf16[16,512,128]{2,1,0:T(8,128)(2,1)} %copy-done.3), calls=%async_computation.5 | async-start | bytes 4194304 | tf_op jit(solution)/shard_map/all_to_all | solution.py:559
  228.3 4.6 %collective-permute-done.40.refs_1_ = bf16[112,512]{1,0:T(8,128)(2,1)S(1)} collective-permute-done((bf16[112,512]{1,0:T(8,128)(2,1)S(1)}, bf16[112,512]{1,0:T(8,128)(2,1)S(1)}, u32[]{:S(2)}, u32[]{:S(2)}) %collective-permute-start.40) | collective-permute-done | bytes 114720 | tf_op jit(solution)/shard_map/ppermute | solution.py:43
  235.2 3.6 %shard_map.287 = (bf16[224,384]{1,0:T(8,128)(2,1)S(1)}, f32[1,384]{1,0:T(1,128)S(1)}, f32[112,1024]{1,0:T(8,128)S(1)}, bf16[112,1024]{1,0:T(8,128)(2,1)S(1)}) custom-call(s32[6]{0:T(128)S(1)} %stack.45.refs_0_.place.meta, bf16[112,1024]{1,0:T(8,128)(2,1)S(1)} %get-tuple-element.265.refs_1_.refs_4_, ...), custom_call_target="tpu_custom_call" | custom-call | flops 234881024 | bytes 3589656 | tf_op jit(solution)/shard_map/pallas_call | solution.py:136
  240.6 1.9 collective-permute-start.45
  242.4 1.9 shard_map.290
  247.1 1.9 collective-permute-start.46
  249.0 4.2 %collective-permute-done.46.refs_2_ = bf16[112,512]{1,0:T(8,128)(2,1)S(1)} collective-permute-done((bf16[112,512]{1,0:T(8,128)(2,1)S(1)}, bf16[112,512]{1,0:T(8,128)(2,1)S(1)}, u32[]{:S(2)}, u32[]{:S(2)}) %collective-permute-start.46) | collective-permute-done | bytes 114720 | tf_op jit(solution)/shard_map/ppermute | solution.py:43
  258.2 7.2 %all-to-all-start.6 = ((bf16[16,400,128]{2,1,0:T(8,128)(2,1)}), bf16[16,400,128]{2,1,0:T(8,128)(2,1)S(1)}, u32[]{:S(2)}, u32[]{:S(2)}) async-start(bf16[16,400,128]{2,1,0:T(8,128)(2,1)} %copy-done.2), calls=%async_computation.6 | async-start | bytes 3276800 | tf_op jit(solution)/shard_map/all_to_all | solution.py:559
  265.5 1.9 convert_reduce_fusion.1
  267.4 2.6 shard_map.293
  270.0 1.9 convert_reduce_fusion
  274.8 13.9 %all-to-all-done.6.received = bf16[16,400,128]{2,1,0:T(8,128)(2,1)S(1)} async-done(((bf16[16,400,128]{2,1,0:T(8,128)(2,1)}), bf16[16,400,128]{2,1,0:T(8,128)(2,1)S(1)}, u32[]{:S(2)}, u32[]{:S(2)}) %all-to-all-start.6) | async-done | bytes 1638432 | tf_op jit(solution)/shard_map/all_to_all | solution.py:559
  288.7 1.8 shard_map.294
  (250 shorter events, 94.9 us)
Async XLA Ops:
  4.3 35.8 %all-to-all-start = ((bf16[16,512,128]{2,1,0:T(8,128)(2,1)}), bf16[16,512,128]{2,1,0:T(8,128)(2,1)}, u32[]{:S(2)}, u32[]{:S(2)}) async-start(bf16[16,512,128]{2,1,0:T(8,128)(2,1)} %shard_map.256), calls=%async_computation | async-start | bytes 4194304 | tf_op jit(solution)/shard_map/all_to_all | solution.py:559
  40.2 44.7 %all-to-all-start.1 = ((bf16[16,768,128]{2,1,0:T(8,128)(2,1)}), bf16[16,768,128]{2,1,0:T(8,128)(2,1)S(1)}, u32[]{:S(2)}, u32[]{:S(2)}) async-start(bf16[16,768,128]{2,1,0:T(8,128)(2,1)} %copy-done), calls=%async_computation.1 | async-start | bytes 6291456 | tf_op jit(solution)/shard_map/all_to_all | solution.py:559
  50.2 8.0 %collective-permute-start.3 = (bf16[2,256,128]{2,1,0:T(8,128)(2,1)S(1)}, bf16[2,256,128]{2,1,0:T(8,128)(2,1)S(1)}, u32[]{:S(2)}, u32[]{:S(2)}) collective-permute-start(bf16[2,256,128]{2,1,0:T(8,128)(2,1)S(1)} %fusion.5.refs_1_), channel_id=1, source_target_pairs={{0,4},{2,6},{4,0},{6,2},{1,5},{3,7},{5,1},{7,3},{8,12},{10,14},{12... | collective-permute-start | bytes 393224 | tf_op jit(solution)/shard_map/ppermute | solution.py:29
  54.1 7.4 %collective-permute-start.2 = (bf16[2,256,128]{2,1,0:T(8,128)(2,1)S(1)}, bf16[2,256,128]{2,1,0:T(8,128)(2,1)S(1)}, u32[]{:S(2)}, u32[]{:S(2)}) collective-permute-start(bf16[2,256,128]{2,1,0:T(8,128)(2,1)S(1)} %fusion.5.refs_1_), channel_id=1, source_target_pairs={{0,6},{2,0},{4,2},{6,4},{1,7},{3,1},{5,3},{7,5},{8,14},{10,8},{12,... | collective-permute-start | bytes 393224 | tf_op jit(solution)/shard_map/ppermute | solution.py:29
  54.8 6.7 %collective-permute-start.1 = (bf16[2,256,128]{2,1,0:T(8,128)(2,1)S(1)}, bf16[2,256,128]{2,1,0:T(8,128)(2,1)S(1)}, u32[]{:S(2)}, u32[]{:S(2)}) collective-permute-start(bf16[2,256,128]{2,1,0:T(8,128)(2,1)S(1)} %fusion.5.refs_1_), channel_id=1, source_target_pairs={{0,2},{2,4},{4,6},{6,0},{1,3},{3,5},{5,7},{7,1},{8,10},{10,12},{12... | collective-permute-start | bytes 393224 | tf_op jit(solution)/shard_map/ppermute | solution.py:29
  62.5 1.6 collective-permute-start.5
  67.2 1.6 collective-permute-start.6
  68.9 5.3 %collective-permute-start.7 = (bf16[112,512]{1,0:T(8,128)(2,1)S(1)}, bf16[112,512]{1,0:T(8,128)(2,1)S(1)}, u32[]{:S(2)}, u32[]{:S(2)}) collective-permute-start(bf16[112,512]{1,0:T(8,128)(2,1)S(1)} %get-tuple-element.172.refs_0_), channel_id=1, source_target_pairs={{0,2},{2,0},{4,6},{6,4},{1,3},{3,1},{5,7},{7,5},{8,10},{10,8},{12,... | collective-permute-start | bytes 344072 | tf_op jit(solution)/shard_map/ppermute | solution.py:38
  69.9 6.1 %collective-permute-start.8 = (bf16[112,512]{1,0:T(8,128)(2,1)S(1)}, bf16[112,512]{1,0:T(8,128)(2,1)S(1)}, u32[]{:S(2)}, u32[]{:S(2)}) collective-permute-start(bf16[112,512]{1,0:T(8,128)(2,1)S(1)} %get-tuple-element.173.refs_2_), channel_id=1, source_target_pairs={{0,6},{6,0},{2,4},{4,2},{1,7},{7,1},{3,5},{5,3},{8,14},{14,8},{10,... | collective-permute-start | bytes 344072 | tf_op jit(solution)/shard_map/ppermute | solution.py:39
  76.1 6.1 %collective-permute-start.9 = (bf16[112,512]{1,0:T(8,128)(2,1)S(1)}, bf16[112,512]{1,0:T(8,128)(2,1)S(1)}, u32[]{:S(2)}, u32[]{:S(2)}) collective-permute-start(bf16[112,512]{1,0:T(8,128)(2,1)S(1)} %get-tuple-element.174.refs_0_), channel_id=1, source_target_pairs={{0,6},{6,0},{2,4},{4,2},{1,7},{7,1},{3,5},{5,3},{8,14},{14,8},{10,... | collective-permute-start | bytes 344072 | tf_op jit(solution)/shard_map/ppermute | solution.py:43
  78.3 4.8 %collective-permute-start.10 = (bf16[112,512]{1,0:T(8,128)(2,1)S(1)}, bf16[112,512]{1,0:T(8,128)(2,1)S(1)}, u32[]{:S(2)}, u32[]{:S(2)}) collective-permute-start(bf16[112,512]{1,0:T(8,128)(2,1)S(1)} %get-tuple-element.175.refs_2_), channel_id=1, source_target_pairs={{0,2},{2,0},{4,6},{6,4},{1,3},{3,1},{5,7},{7,5},{8,10},{10,8},{12,... | collective-permute-start | bytes 344072 | tf_op jit(solution)/shard_map/ppermute | solution.py:44
  84.9 51.0 %all-to-all-start.2 = ((bf16[16,512,128]{2,1,0:T(8,128)(2,1)}), bf16[16,512,128]{2,1,0:T(8,128)(2,1)}, u32[]{:S(2)}, u32[]{:S(2)}) async-start(bf16[16,512,128]{2,1,0:T(8,128)(2,1)} %copy-done.1), calls=%async_computation.2 | async-start | bytes 4194304 | tf_op jit(solution)/shard_map/all_to_all | solution.py:559
  92.1 1.8 collective-permute-start.11
  98.3 5.3 %collective-permute-start.13 = (bf16[112,512]{1,0:T(8,128)(2,1)S(1)}, bf16[112,512]{1,0:T(8,128)(2,1)S(1)}, u32[]{:S(2)}, u32[]{:S(2)}) collective-permute-start(bf16[112,512]{1,0:T(8,128)(2,1)S(1)} %get-tuple-element.183.refs_0_), channel_id=1, source_target_pairs={{0,2},{2,0},{4,6},{6,4},{1,3},{3,1},{5,7},{7,5},{8,10},{10,8},{12,... | collective-permute-start | bytes 344072 | tf_op jit(solution)/shard_map/ppermute | solution.py:38
  99.3 6.1 %collective-permute-start.14 = (bf16[112,512]{1,0:T(8,128)(2,1)S(1)}, bf16[112,512]{1,0:T(8,128)(2,1)S(1)}, u32[]{:S(2)}, u32[]{:S(2)}) collective-permute-start(bf16[112,512]{1,0:T(8,128)(2,1)S(1)} %get-tuple-element.184.refs_2_), channel_id=1, source_target_pairs={{0,6},{6,0},{2,4},{4,2},{1,7},{7,1},{3,5},{5,3},{8,14},{14,8},{10,... | collective-permute-start | bytes 344072 | tf_op jit(solution)/shard_map/ppermute | solution.py:39
  105.5 6.1 %collective-permute-start.15 = (bf16[112,512]{1,0:T(8,128)(2,1)S(1)}, bf16[112,512]{1,0:T(8,128)(2,1)S(1)}, u32[]{:S(2)}, u32[]{:S(2)}) collective-permute-start(bf16[112,512]{1,0:T(8,128)(2,1)S(1)} %get-tuple-element.185.refs_0_), channel_id=1, source_target_pairs={{0,6},{6,0},{2,4},{4,2},{1,7},{7,1},{3,5},{5,3},{8,14},{14,8},{10,... | collective-permute-start | bytes 344072 | tf_op jit(solution)/shard_map/ppermute | solution.py:43
  108.1 4.8 %collective-permute-start.16 = (bf16[112,512]{1,0:T(8,128)(2,1)S(1)}, bf16[112,512]{1,0:T(8,128)(2,1)S(1)}, u32[]{:S(2)}, u32[]{:S(2)}) collective-permute-start(bf16[112,512]{1,0:T(8,128)(2,1)S(1)} %get-tuple-element.186.refs_2_), channel_id=1, source_target_pairs={{0,2},{2,0},{4,6},{6,4},{1,3},{3,1},{5,7},{7,5},{8,10},{10,8},{12,... | collective-permute-start | bytes 344072 | tf_op jit(solution)/shard_map/ppermute | solution.py:44
  113.2 1.6 collective-permute-start.17
  119.7 5.4 %collective-permute-start.19 = (bf16[112,512]{1,0:T(8,128)(2,1)S(1)}, bf16[112,512]{1,0:T(8,128)(2,1)S(1)}, u32[]{:S(2)}, u32[]{:S(2)}) collective-permute-start(bf16[112,512]{1,0:T(8,128)(2,1)S(1)} %get-tuple-element.191.refs_0_), channel_id=1, source_target_pairs={{0,2},{2,0},{4,6},{6,4},{1,3},{3,1},{5,7},{7,5},{8,10},{10,8},{12,... | collective-permute-start | bytes 344072 | tf_op jit(solution)/shard_map/ppermute | solution.py:38
  120.0 6.5 %collective-permute-start.20 = (bf16[112,512]{1,0:T(8,128)(2,1)S(1)}, bf16[112,512]{1,0:T(8,128)(2,1)S(1)}, u32[]{:S(2)}, u32[]{:S(2)}) collective-permute-start(bf16[112,512]{1,0:T(8,128)(2,1)S(1)} %get-tuple-element.192.refs_2_), channel_id=1, source_target_pairs={{0,6},{6,0},{2,4},{4,2},{1,7},{7,1},{3,5},{5,3},{8,14},{14,8},{10,... | collective-permute-start | bytes 344072 | tf_op jit(solution)/shard_map/ppermute | solution.py:39
  126.6 6.1 %collective-permute-start.21 = (bf16[112,512]{1,0:T(8,128)(2,1)S(1)}, bf16[112,512]{1,0:T(8,128)(2,1)S(1)}, u32[]{:S(2)}, u32[]{:S(2)}) collective-permute-start(bf16[112,512]{1,0:T(8,128)(2,1)S(1)} %get-tuple-element.193.refs_0_), channel_id=1, source_target_pairs={{0,6},{6,0},{2,4},{4,2},{1,7},{7,1},{3,5},{5,3},{8,14},{14,8},{10,... | collective-permute-start | bytes 344072 | tf_op jit(solution)/shard_map/ppermute | solution.py:43
  127.8 4.8 %collective-permute-start.22 = (bf16[112,512]{1,0:T(8,128)(2,1)S(1)}, bf16[112,512]{1,0:T(8,128)(2,1)S(1)}, u32[]{:S(2)}, u32[]{:S(2)}) collective-permute-start(bf16[112,512]{1,0:T(8,128)(2,1)S(1)} %get-tuple-element.194.refs_2_), channel_id=1, source_target_pairs={{0,2},{2,0},{4,6},{6,4},{1,3},{3,1},{5,7},{7,5},{8,10},{10,8},{12,... | collective-permute-start | bytes 344072 | tf_op jit(solution)/shard_map/ppermute | solution.py:44
  134.4 6.0 %collective-permute-start.4 = (bf16[112,1024]{1,0:T(8,128)(2,1)S(1)}, bf16[112,1024]{1,0:T(8,128)(2,1)}, u32[]{:S(2)}, u32[]{:S(2)}) collective-permute-start(bf16[112,1024]{1,0:T(8,128)(2,1)S(1)} %get-tuple-element.165.refs_0_.refs_4_.refs_3_), channel_id=1, source_target_pairs={{0,1},{1,0},{2,3},{3,2},{4,5},{5,4},{6,7},{7,6},{8,9},{9,8},{10,11... | collective-permute-start | bytes 688136 | tf_op jit(solution)/shard_map/ppermute | solution.py:24
  144.0 1.9 collective-permute-start.24
  146.0 7.7 %collective-permute-start.25 = (bf16[112,1024]{1,0:T(8,128)(2,1)S(1)}, bf16[112,1024]{1,0:T(8,128)(2,1)S(1)}, u32[]{:S(2)}, u32[]{:S(2)}) collective-permute-start(bf16[112,1024]{1,0:T(8,128)(2,1)S(1)} %get-tuple-element.205.refs_0_), channel_id=1, source_target_pairs={{0,2},{2,0},{4,6},{6,4},{1,3},{3,1},{5,7},{7,5},{8,10},{10,8},{12,... | collective-permute-start | bytes 688136 | tf_op jit(solution)/shard_map/ppermute | solution.py:38
  146.1 8.9 %collective-permute-start.26 = (bf16[112,1024]{1,0:T(8,128)(2,1)S(1)}, bf16[112,1024]{1,0:T(8,128)(2,1)S(1)}, u32[]{:S(2)}, u32[]{:S(2)}) collective-permute-start(bf16[112,1024]{1,0:T(8,128)(2,1)S(1)} %get-tuple-element.206.refs_2_), channel_id=1, source_target_pairs={{0,6},{6,0},{2,4},{4,2},{1,7},{7,1},{3,5},{5,3},{8,14},{14,8},{10,... | collective-permute-start | bytes 688136 | tf_op jit(solution)/shard_map/ppermute | solution.py:39
  156.6 34.8 %all-to-all-start.3 = ((bf16[16,512,128]{2,1,0:T(8,128)(2,1)}), bf16[16,512,128]{2,1,0:T(8,128)(2,1)}, u32[]{:S(2)}, u32[]{:S(2)}) async-start(bf16[16,512,128]{2,1,0:T(8,128)(2,1)} %copy-done.4), calls=%async_computation.3 | async-start | bytes 4194304 | tf_op jit(solution)/shard_map/all_to_all | solution.py:559
  163.8 7.7 %collective-permute-start.27 = (bf16[112,1024]{1,0:T(8,128)(2,1)}, bf16[112,1024]{1,0:T(8,128)(2,1)S(1)}, u32[]{:S(2)}, u32[]{:S(2)}) collective-permute-start(bf16[112,1024]{1,0:T(8,128)(2,1)} %copy-done.43), channel_id=1, source_target_pairs={{0,6},{6,0},{2,4},{4,2},{1,7},{7,1},{3,5},{5,3},{8,14},{14,8},{10,... | collective-permute-start | bytes 688136 | tf_op jit(solution)/shard_map/ppermute | solution.py:43
  165.8 6.2 %collective-permute-start.28 = (bf16[112,1024]{1,0:T(8,128)(2,1)}, bf16[112,1024]{1,0:T(8,128)(2,1)S(1)}, u32[]{:S(2)}, u32[]{:S(2)}) collective-permute-start(bf16[112,1024]{1,0:T(8,128)(2,1)} %copy-done.45), channel_id=1, source_target_pairs={{0,2},{2,0},{4,6},{6,4},{1,3},{3,1},{5,7},{7,5},{8,10},{10,8},{12,... | collective-permute-start | bytes 688136 | tf_op jit(solution)/shard_map/ppermute | solution.py:44
  181.1 1.6 collective-permute-start.30
  182.7 6.6 %collective-permute-start.31 = (bf16[112,512]{1,0:T(8,128)(2,1)S(1)}, bf16[112,512]{1,0:T(8,128)(2,1)S(1)}, u32[]{:S(2)}, u32[]{:S(2)}) collective-permute-start(bf16[112,512]{1,0:T(8,128)(2,1)S(1)} %get-tuple-element.230.refs_0_), channel_id=1, source_target_pairs={{0,2},{2,0},{4,6},{6,4},{1,3},{3,1},{5,7},{7,5},{8,10},{10,8},{12,... | collective-permute-start | bytes 344072 | tf_op jit(solution)/shard_map/ppermute | solution.py:38
  183.0 6.3 %collective-permute-start.32 = (bf16[112,512]{1,0:T(8,128)(2,1)S(1)}, bf16[112,512]{1,0:T(8,128)(2,1)S(1)}, u32[]{:S(2)}, u32[]{:S(2)}) collective-permute-start(bf16[112,512]{1,0:T(8,128)(2,1)S(1)} %get-tuple-element.231.refs_2_), channel_id=1, source_target_pairs={{0,6},{6,0},{2,4},{4,2},{1,7},{7,1},{3,5},{5,3},{8,14},{14,8},{10,... | collective-permute-start | bytes 344072 | tf_op jit(solution)/shard_map/ppermute | solution.py:39
  191.4 28.0 %all-to-all-start.4 = ((bf16[16,368,128]{2,1,0:T(8,128)(2,1)}), bf16[16,368,128]{2,1,0:T(8,128)(2,1)}, u32[]{:S(2)}, u32[]{:S(2)}) async-start(bf16[16,368,128]{2,1,0:T(8,128)(2,1)} %copy-done.14), calls=%async_computation.4 | async-start | bytes 3014656 | tf_op jit(solution)/shard_map/all_to_all | solution.py:559
  196.7 6.0 %collective-permute-start.34 = (bf16[112,512]{1,0:T(8,128)(2,1)S(1)}, bf16[112,512]{1,0:T(8,128)(2,1)S(1)}, u32[]{:S(2)}, u32[]{:S(2)}) collective-permute-start(bf16[112,512]{1,0:T(8,128)(2,1)S(1)} %get-tuple-element.240.refs_0_), channel_id=1, source_target_pairs={{0,6},{6,0},{2,4},{4,2},{1,7},{7,1},{3,5},{5,3},{8,14},{14,8},{10,... | collective-permute-start | bytes 344072 | tf_op jit(solution)/shard_map/ppermute | solution.py:43
  198.7 4.8 %collective-permute-start.35 = (bf16[112,512]{1,0:T(8,128)(2,1)S(1)}, bf16[112,512]{1,0:T(8,128)(2,1)S(1)}, u32[]{:S(2)}, u32[]{:S(2)}) collective-permute-start(bf16[112,512]{1,0:T(8,128)(2,1)S(1)} %get-tuple-element.241.refs_2_), channel_id=1, source_target_pairs={{0,2},{2,0},{4,6},{6,4},{1,3},{3,1},{5,7},{7,5},{8,10},{10,8},{12,... | collective-permute-start | bytes 344072 | tf_op jit(solution)/shard_map/ppermute | solution.py:44
  211.1 1.6 collective-permute-start.37
  212.7 5.6 %collective-permute-start.38 = (bf16[112,512]{1,0:T(8,128)(2,1)S(1)}, bf16[112,512]{1,0:T(8,128)(2,1)S(1)}, u32[]{:S(2)}, u32[]{:S(2)}) collective-permute-start(bf16[112,512]{1,0:T(8,128)(2,1)S(1)} %get-tuple-element.250.refs_0_), channel_id=1, source_target_pairs={{0,2},{2,0},{4,6},{6,4},{1,3},{3,1},{5,7},{7,5},{8,10},{10,8},{12,... | collective-permute-start | bytes 344072 | tf_op jit(solution)/shard_map/ppermute | solution.py:38
  213.2 6.1 %collective-permute-start.39 = (bf16[112,512]{1,0:T(8,128)(2,1)S(1)}, bf16[112,512]{1,0:T(8,128)(2,1)S(1)}, u32[]{:S(2)}, u32[]{:S(2)}) collective-permute-start(bf16[112,512]{1,0:T(8,128)(2,1)S(1)} %get-tuple-element.251.refs_2_), channel_id=1, source_target_pairs={{0,6},{6,0},{2,4},{4,2},{1,7},{7,1},{3,5},{5,3},{8,14},{14,8},{10,... | collective-permute-start | bytes 344072 | tf_op jit(solution)/shard_map/ppermute | solution.py:39
  219.5 38.8 %all-to-all-start.5 = ((bf16[16,512,128]{2,1,0:T(8,128)(2,1)}), bf16[16,512,128]{2,1,0:T(8,128)(2,1)}, u32[]{:S(2)}, u32[]{:S(2)}) async-start(bf16[16,512,128]{2,1,0:T(8,128)(2,1)} %copy-done.3), calls=%async_computation.5 | async-start | bytes 4194304 | tf_op jit(solution)/shard_map/all_to_all | solution.py:559
  226.8 6.0 %collective-permute-start.40 = (bf16[112,512]{1,0:T(8,128)(2,1)S(1)}, bf16[112,512]{1,0:T(8,128)(2,1)S(1)}, u32[]{:S(2)}, u32[]{:S(2)}) collective-permute-start(bf16[112,512]{1,0:T(8,128)(2,1)S(1)} %get-tuple-element.262.refs_0_), channel_id=1, source_target_pairs={{0,6},{6,0},{2,4},{4,2},{1,7},{7,1},{3,5},{5,3},{8,14},{14,8},{10,... | collective-permute-start | bytes 344072 | tf_op jit(solution)/shard_map/ppermute | solution.py:43
  228.3 4.8 %collective-permute-start.41 = (bf16[112,512]{1,0:T(8,128)(2,1)S(1)}, bf16[112,512]{1,0:T(8,128)(2,1)S(1)}, u32[]{:S(2)}, u32[]{:S(2)}) collective-permute-start(bf16[112,512]{1,0:T(8,128)(2,1)S(1)} %get-tuple-element.263.refs_2_), channel_id=1, source_target_pairs={{0,2},{2,0},{4,6},{6,4},{1,3},{3,1},{5,7},{7,5},{8,10},{10,8},{12,... | collective-permute-start | bytes 344072 | tf_op jit(solution)/shard_map/ppermute | solution.py:44
  233.6 1.6 collective-permute-start.42
  238.8 1.6 collective-permute-start.43
  240.5 5.3 %collective-permute-start.44 = (bf16[112,512]{1,0:T(8,128)(2,1)S(1)}, bf16[112,512]{1,0:T(8,128)(2,1)S(1)}, u32[]{:S(2)}, u32[]{:S(2)}) collective-permute-start(bf16[112,512]{1,0:T(8,128)(2,1)S(1)} %get-tuple-element.272.refs_0_), channel_id=1, source_target_pairs={{0,2},{2,0},{4,6},{6,4},{1,3},{3,1},{5,7},{7,5},{8,10},{10,8},{12,... | collective-permute-start | bytes 344072 | tf_op jit(solution)/shard_map/ppermute | solution.py:38
  240.6 6.5 %collective-permute-start.45 = (bf16[112,512]{1,0:T(8,128)(2,1)S(1)}, bf16[112,512]{1,0:T(8,128)(2,1)S(1)}, u32[]{:S(2)}, u32[]{:S(2)}) collective-permute-start(bf16[112,512]{1,0:T(8,128)(2,1)S(1)} %get-tuple-element.273.refs_2_), channel_id=1, source_target_pairs={{0,6},{6,0},{2,4},{4,2},{1,7},{7,1},{3,5},{5,3},{8,14},{14,8},{10,... | collective-permute-start | bytes 344072 | tf_op jit(solution)/shard_map/ppermute | solution.py:39
  247.1 6.1 %collective-permute-start.46 = (bf16[112,512]{1,0:T(8,128)(2,1)S(1)}, bf16[112,512]{1,0:T(8,128)(2,1)S(1)}, u32[]{:S(2)}, u32[]{:S(2)}) collective-permute-start(bf16[112,512]{1,0:T(8,128)(2,1)S(1)} %get-tuple-element.280.refs_1_), channel_id=1, source_target_pairs={{0,6},{6,0},{2,4},{4,2},{1,7},{7,1},{3,5},{5,3},{8,14},{14,8},{10,... | collective-permute-start | bytes 344072 | tf_op jit(solution)/shard_map/ppermute | solution.py:43
  249.0 4.8 %collective-permute-start.47 = (bf16[112,512]{1,0:T(8,128)(2,1)S(1)}, bf16[112,512]{1,0:T(8,128)(2,1)S(1)}, u32[]{:S(2)}, u32[]{:S(2)}) collective-permute-start(bf16[112,512]{1,0:T(8,128)(2,1)S(1)} %get-tuple-element.281.refs_3_), channel_id=1, source_target_pairs={{0,2},{2,0},{4,6},{6,4},{1,3},{3,1},{5,7},{7,5},{8,10},{10,8},{12,... | collective-permute-start | bytes 344072 | tf_op jit(solution)/shard_map/ppermute | solution.py:44
  258.2 30.5 %all-to-all-start.6 = ((bf16[16,400,128]{2,1,0:T(8,128)(2,1)}), bf16[16,400,128]{2,1,0:T(8,128)(2,1)S(1)}, u32[]{:S(2)}, u32[]{:S(2)}) async-start(bf16[16,400,128]{2,1,0:T(8,128)(2,1)} %copy-done.2), calls=%async_computation.6 | async-start | bytes 3276800 | tf_op jit(solution)/shard_map/all_to_all | solution.py:559
  (70 other events, 609.1 us)
